TPU v7x, 32 devices: a whole 2x2x4 slice. The times are simulated.
32 devices in a mesh: groups: 2 (over x), mp: 8 (over z, y), sub: 2 (over core).
Axes of the slice: x: 2, y: 2, z: 4, core: 2. Of those that a mesh axis runs over, the one named last changes fastest.
Arguments:
- tokens: bfloat16 [1024, 8192], P(('groups', 'mp'), 'sub'), parts along dimension 0, may hold values from -6 to 6
- gate_matrix: bfloat16 [8192, 28672], P('sub', 'mp'), may hold values from -0.0625 to 0.0625
- adapter_down_panels: bfloat16 [8, 8192, 64], P('mp', 'sub'), may hold values from -0.0625 to 0.0625
- adapter_up_panels: bfloat16 [8, 64, 28672], P('mp'), may hold values from -0.75 to 0.75
- request_adapter_index: int32 [512, 1], P('groups'), parts along dimension 0, may hold values from 0 to 7; in each aligned block of 256 rows (0 to 255, 256 to 511, ...) at most 64 rows name the same one
- adapter_store_row: int32 [8], replicated, may hold values from 0 to 7, each once
Outputs:
- gated: bfloat16 [1024, 28672], P(('groups', 'sub'), 'mp'), parts along dimension 0
There are 2 independent parts, one for each index of `groups`. A program takes and returns all parts, laid end to end along the dimension named above; an argument that names none is the same for every part. Nothing has to cross between parts.
Inputs may be any that keep to these rules, and one draw needn't show every extreme that they name: `request_adapter_index`: in each part no adapter serves more than 64 requests, and some adapter serves exactly 64. `adapter_store_row`: each store row once.
All inputs are finite; a program needn't handle non-finite values.
Results may differ from a plain program's by a relative error of at most 0.0039.
Values may be sent and summed in bfloat16 or wider, within the bound.
No kernel may reach another device: no remote copies, remote signals or barrier semaphores. Data moves between devices by JAX's collectives and lax.ppermute only.
A program may use at most 192 MiB of HBM per device.

v0:
```python
import jax
import jax.numpy as jnp
from jax import lax
from jax.sharding import PartitionSpec as P


def per_device(
    tokens,
    gate_matrix,
    adapter_down_panels,
    adapter_up_panels,
    request_adapter_index,
    adapter_store_row,
):
    rows_all = lax.all_gather(tokens, "mp", axis=0, tiled=True)
    total = rows_all.shape[0]
    count = adapter_store_row.shape[0]
    rank = adapter_down_panels.shape[2]
    per_token = jnp.repeat(request_adapter_index[:, 0], 2, total_repeat_length=total)
    adapter_hot = per_token[:, None] == jnp.arange(count, dtype=jnp.int32)[None, :]
    store_row = jnp.sum(jnp.where(adapter_hot, adapter_store_row[None, :], 0), axis=1)
    row_mask = (store_row[:, None] == jnp.arange(count, dtype=jnp.int32)[None, :]).astype(
        jnp.float32
    )
    term = jnp.einsum(
        "td,adr->tar",
        rows_all,
        lax.all_gather(adapter_down_panels, "mp", axis=0, tiled=True),
        preferred_element_type=jnp.float32,
    )
    low_all = lax.psum(term, "sub")
    low_masked = row_mask[:, :, None] * low_all
    low_rank_batch = low_masked.astype(jnp.bfloat16)
    base = jnp.dot(rows_all, gate_matrix, preferred_element_type=jnp.float32)
    width = rank // lax.axis_size("sub")
    begin = lax.axis_index("sub") * width
    own_rank = lax.dynamic_slice_in_dim(adapter_up_panels, begin, width, 1)
    block_list = lax.all_to_all(own_rank, "mp", split_axis=2, concat_axis=0, tiled=True)
    low_part = lax.dynamic_slice_in_dim(low_rank_batch, begin, width, 2).reshape(
        total, count * width
    )
    delta = jnp.dot(
        low_part,
        block_list.reshape(count * width, block_list.shape[2]),
        preferred_element_type=jnp.float32,
    )
    result = lax.psum_scatter(base + delta, "sub", scatter_dimension=0, tiled=True)
    return result.astype(jnp.bfloat16)


def solution(mesh):
    return jax.shard_map(
        per_device,
        mesh=mesh,
        in_specs=(
            P(("groups", "mp"), "sub"),
            P("sub", "mp"),
            P("mp", "sub", None),
            P("mp", None, None),
            P("groups", None),
            P(),
        ),
        out_specs=P(("groups", "sub"), "mp"),
        check_vma=False,
    )
```

profile of v0, /device:TPU:0, one launch (start us, length us, event | category | flops | bytes accessed | tf_op | source)
XLA Modules:
  0.0 350.2 jit_solution(5402326355900073290)
XLA Ops:
  6.5 0.7 all-gather.3.cloned.1.call-update
  7.3 0.7 all-gather.5.cloned.1.call-update
  8.0 1.6 constant_dynamic-slice_fusion
  9.6 22.0 %copy.14 = bf16[1,32,28672]{1,0,2:T(2,128)(2,1)} copy(bf16[1,32,28672]{2,1,0:T(8,128)(2,1)S(1)} %constant_dynamic-slice_fusion) | data formatting | bytes 3670016
  31.7 0.5 broadcast.136
  32.2 157.1 %reduce.4 = bf16[28672,32]{1,0:T(8,128)(2,1)} reduce(bf16[28672,1,32]{2,1,0:T(2,128)(2,1)} %bitcast.38, bf16[]{:T(256)} %broadcast.136), dimensions={1}, to_apply=%bitcast.28.reduce_sub_computation | reduce | bytes 3670018
  189.3 10.4 %reshape.182 = bf16[8,2,57344]{2,1,0:T(2,128)(2,1)} reshape(bf16[28672,32]{1,0:T(8,128)(2,1)} %reduce.4) | data formatting | bytes 3670016
  199.7 7.4 %all-to-all-start = ((bf16[8,2,57344]{2,1,0:T(2,128)(2,1)}), bf16[8,2,57344]{2,1,0:T(2,128)(2,1)S(1)}, u32[]{:S(2)}, u32[]{:S(2)}) async-start(bf16[8,2,57344]{2,1,0:T(2,128)(2,1)} %reshape.182), calls=%async_computation | async-start | bytes 3670016 | tf_op jit(solution)/shard_map/all_to_all | solution.py:38
  207.2 2.5 scatter_custom_fusion
  209.7 0.3 reduce-window.14
  210.1 0.1 slice_reduce_fusion
  210.3 3.5 %gather_fusion = s32[512]{0:T(512)S(1)} fusion(s32[256]{0:T(256)S(1)} %bitcast.37, s32[1024]{0:T(1024)S(1)} %pad_clamp_fusion), kind=kCustom, calls=%fused_computation | custom fusion | bytes 6144 | tf_op jit(solution)/shard_map/jit(_take)/gather | solution.py:19
  214.0 35.7 %all-to-all-done = bf16[8,2,57344]{2,1,0:T(2,128)(2,1)S(1)} async-done(((bf16[8,2,57344]{2,1,0:T(2,128)(2,1)}), bf16[8,2,57344]{2,1,0:T(2,128)(2,1)S(1)}, u32[]{:S(2)}, u32[]{:S(2)}) %all-to-all-start) | async-done | bytes 1835040 | tf_op jit(solution)/shard_map/all_to_all | solution.py:38
  249.7 8.9 %reshape.183 = bf16[28672,1,32]{2,1,0:T(2,128)(2,1)} reshape(bf16[8,2,57344]{2,1,0:T(2,128)(2,1)S(1)} %all-to-all-done) | data formatting | bytes 3670016
  258.6 26.4 %copy.12 = bf16[1,32,28672]{2,1,0:T(8,128)(2,1)S(1)} copy(bf16[1,32,28672]{1,0,2:T(2,128)(2,1)} %bitcast.39) | data formatting | bytes 3670016 | tf_op jit(solution)/shard_map/all_to_all | solution.py:38
  285.1 0.5 copy.15
  285.6 0.1 bitcast_bitcast_fusion
  285.7 0.5 copy.13
  286.3 6.8 %fusion.5 = f32[512,512]{0,1} fusion(bf16[512,4096]{1,0:T(8,128)(2,1)} %all-gather.3.cloned.1.call-done, bf16[4096,512]{0,1:T(8,128)(2,1)} %bitcast.51), kind=kOutput, calls=%fused_computation.24 | convolution fusion | flops 2147483648 | bytes 9437184
  293.2 24.0 %fusion.4 = f32[512,3584]{1,0:T(8,128)} fusion(bf16[512,4096]{1,0:T(8,128)(2,1)} %all-gather.3.cloned.1.call-done, bf16[4096,3584]{1,0:T(8,128)(2,1)} %param.9), kind=kOutput, calls=%fused_computation.23 | convolution fusion | flops 15032385536 | bytes 40894464 | tf_op jit(solution)/shard_map/dot_general | solution.py:34
  317.3 1.1 fusion
  318.4 7.2 %convolution_add_fusion = f32[512,3584]{1,0:T(8,128)} fusion(f32[512,3584]{1,0:T(8,128)} %fusion.4, bf16[512,256]{0,1:T(8,128)(2,1)S(1)} %bitcast.43, bf16[256,3584]{1,0:T(8,128)(2,1)S(1)} %bitcast.40), kind=kOutput, calls=%fused_computation.2 | convolution fusion | flops 941359104 | bytes 16777216 | tf_op jit(solution)/shard_map/dot_general | solution.py:42
  325.6 14.6 %reduce-scatter.2.cloned.1.call-done = f32[256,3584]{1,0:T(8,128)} async-done(((f32[512,3584]{1,0:T(8,128)}), f32[256,3584]{1,0:T(8,128)}) %reduce-scatter.2.cloned.1.call-update) | async-done | bytes 3670032 | tf_op jit(solution)/shard_map/reduce_scatter | solution.py:47
  340.2 3.4 convert_element_type.15
  (29 shorter events, 0.6 us)
Async XLA Ops:
  6.5 203.8 %copy-start = (s32[256,1]{0,1:T(1,128)S(1)}, s32[256,1]{0,1:T(1,128)}, u32[]{:S(2)}) copy-start(s32[256,1]{0,1:T(1,128)} %param.12) | copy-start | bytes 3076
  6.5 279.8 %all-gather.3.cloned.1.call-start = ((), (), s32[]{:S(2)}) async-start(), calls=%async_computation.2 | async-start | bytes 4718592 | tf_op jit(solution)/shard_map/all_gather | solution.py:15
  7.3 279.1 %all-gather.5.cloned.1.call-start = ((), (), s32[]{:S(2)}) async-start(), calls=%async_computation.3 | async-start | bytes 4718592 | tf_op jit(solution)/shard_map/all_gather | solution.py:28
  189.3 17.9 %copy-start.2 = (s32[2,128]{1,0:T(2,128)S(1)}, s32[2,128]{1,0:T(2,128)}, u32[]{:S(2)}) copy-start(s32[2,128]{1,0:T(2,128)} %constant.77.clone.1) | copy-start | bytes 3076
  199.6 14.2 %copy-start.3 = (s32[8]{0:T(128)S(1)}, s32[8]{0:T(128)}, u32[]{:S(2)}) copy-start(s32[8]{0:T(128)} %param.13) | copy-start | bytes 100
  199.7 50.0 %all-to-all-start = ((bf16[8,2,57344]{2,1,0:T(2,128)(2,1)}), bf16[8,2,57344]{2,1,0:T(2,128)(2,1)S(1)}, u32[]{:S(2)}, u32[]{:S(2)}) async-start(bf16[8,2,57344]{2,1,0:T(2,128)(2,1)} %reshape.182), calls=%async_computation | async-start | bytes 3670016 | tf_op jit(solution)/shard_map/all_to_all | solution.py:38
  207.1 110.2 %all-reduce.2.cloned.1.call-start = ((), (), s32[]{:S(2)}) async-start(), calls=%async_computation.4 | async-start | bytes 2097152 | tf_op jit(solution)/shard_map/psum | solution.py:31
  293.2 47.1 %reduce-scatter.2.cloned.1.call-start = ((), (), s32[]{:S(2)}) async-start(), calls=%async_computation.5 | async-start | bytes 11010048 | tf_op jit(solution)/shard_map/reduce_scatter | solution.py:47
  325.6 18.1 %copy-start.1 = (s32[256,1]{0,1:T(1,128)S(1)}, s32[256,1]{0,1:T(1,128)}, u32[]{:S(2)}) copy-start(s32[256,1]{0,1:T(1,128)} %param.12) | copy-start | bytes 3076
Sparse Core Ops, SparseCore 0:
  9.5 76.0 all-gather.2
  87.7 71.6 all-gather.4
  293.3 18.6 all-reduce.1
  325.7 14.4 reduce-scatter.1
where the time goes:
time: 351 us; the launch traced here: 350 us
  other arithmetic  165 us (47%)
  local copies, waits for them, and re-layouts  74.9 us (21%)
  waiting for transfers between devices  51.8 us (15%)
  matrix products  38.1 us (11%)
  between operations  13.3 us (4%)
  starting transfers between devices  7.53 us (2%)
    unnamed x1, other arithmetic  157 us
    unnamed x13, local copies, waits for them, and re-layouts  42.4 us
    all_to_all x1, waiting for transfers between devices, per_device(): lax.all_to_all(own_rank, 'mp', split_axis=2, concat_axis=0, tiled=True)  35.7 us
    all_to_all x3, local copies, waits for them, and re-layouts, per_device(): lax.all_to_all(own_rank, 'mp', split_axis=2, concat_axis=0, tiled=True)  27.1 us
    dot_general x1, matrix products, per_device(): base = jnp.dot(rows_all, gate_matrix, preferred_element_type=jnp.float32)  24 us
    reduce_scatter x1, waiting for transfers between devices, per_device(): lax.psum_scatter(base + delta, 'sub', scatter_dimension=0, tiled=True)  14.6 us
    all_to_all x1, starting transfers between devices, per_device(): lax.all_to_all(own_rank, 'mp', split_axis=2, concat_axis=0, tiled=True)  7.41 us
    dot_general x1, matrix products, per_device(): jnp.dot(low_part, block_list.reshape(count * width, block_list.shape[2]),...  7.24 us
  transfers between devices with their start and end apart: 5, of which 2 were waited for; matrix products, arithmetic and copies ran while one was open for 74% of the time, Pallas kernels for 0%

commit v1 on v0

v1 whole, which is shorter than its diff:
```python
import jax
import jax.numpy as jnp
from jax import lax
from jax.experimental import pallas as pl
from jax.experimental.pallas import tpu as pltpu
from jax.sharding import PartitionSpec as P

F32 = jnp.float32
BF16 = jnp.bfloat16
ANY = pl.BlockSpec(memory_space=pl.ANY)
VMEM = pl.BlockSpec(memory_space=pltpu.VMEM)


def params(mib):
    return pltpu.CompilerParams(vmem_limit_bytes=mib << 20)


def split_panels(up, count, groups):
    rank, hidden = up.shape[1], up.shape[2]
    quarter, width = rank // 4, hidden // count

    def kernel(up_ref, out_ref, sem):
        which = 2 * lax.rem(lax.axis_index("groups"), 2) + lax.axis_index("sub")
        rows = pl.ds(pl.multiple_of(which * quarter, quarter), quarter)
        copies = [
            pltpu.make_async_copy(
                up_ref.at[0, rows, pl.ds(d * width, width)], out_ref.at[d], sem.at[d]
            )
            for d in range(count)
        ]
        for copy in copies:
            copy.start()
        for copy in copies:
            copy.wait()

    return pl.pallas_call(
        kernel,
        in_specs=[ANY],
        out_specs=ANY,
        out_shape=jax.ShapeDtypeStruct((count, quarter, width), BF16),
        scratch_shapes=[pltpu.SemaphoreType.DMA((count,))],
        name="split_panels",
        cost_estimate=pl.CostEstimate(
            flops=0, bytes_accessed=4 * count * quarter * width, transcendentals=0
        ),
    )(up)


def place(step, levels):
    index = lax.axis_index("mp")
    origin = lax.rem(index // 2 - step + levels, levels)
    keeps_first = (origin // (levels // 2)) == lax.axis_index("sub")
    return keeps_first, lax.rem(index, 2)


def load_rows(chunks, rows_ref, sem, step, levels):
    keeps_first, y = place(step, levels)
    shard = chunks[0].shape[0]
    first = jnp.where(keeps_first, 0, 2 * shard)
    starts = [
        first + y * shard,
        first + (1 - y) * shard,
        2 * shard - first + y * shard,
        2 * shard - first + (1 - y) * shard,
    ]
    copies = [
        pltpu.make_async_copy(
            chunk, rows_ref.at[pl.ds(pl.multiple_of(start, shard), shard)], sem.at[i]
        )
        for i, (chunk, start) in enumerate(zip(chunks, starts))
    ]
    for copy in copies:
        copy.start()
    for copy in copies:
        copy.wait()


def base_pair(chunks, gate, step, levels):
    shard, depth = chunks[0].shape
    width = gate.shape[1]
    tile = 512 if width % 512 == 0 else 256
    half = 2 * shard

    def kernel(c0, c1, c2, c3, gate_ref, keep_ref, send_ref, rows_ref, sem):
        @pl.when(pl.program_id(0) == 0)
        def _():
            load_rows((c0, c1, c2, c3), rows_ref, sem, step, levels)

        columns = pl.ds(pl.multiple_of(pl.program_id(0) * tile, tile), tile)
        total = jnp.dot(rows_ref[...], gate_ref[:, columns], preferred_element_type=F32)
        keep_ref[...] = total[:half]
        send_ref[...] = total[half:].astype(BF16)

    return pl.pallas_call(
        kernel,
        grid=(width // tile,),
        in_specs=[ANY] * 4 + [VMEM],
        out_specs=[pl.BlockSpec((half, tile), lambda i: (0, i))] * 2,
        out_shape=[
            jax.ShapeDtypeStruct((half, width), F32),
            jax.ShapeDtypeStruct((half, width), BF16),
        ],
        scratch_shapes=[
            pltpu.VMEM((2 * half, depth), BF16),
            pltpu.SemaphoreType.DMA((4,)),
        ],
        compiler_params=params(12),
        name="base_pair",
        cost_estimate=pl.CostEstimate(
            flops=4 * half * depth * width,
            bytes_accessed=4 * half * depth + 6 * half * width,
            transcendentals=0,
        ),
    )(*chunks, gate)


def low_pair(chunks, down, step, levels):
    shard, depth = chunks[0].shape
    rank = down.shape[2]
    half = 2 * shard

    def kernel(c0, c1, c2, c3, down_ref, keep_ref, send_ref, rows_ref, sem):
        load_rows((c0, c1, c2, c3), rows_ref, sem, step, levels)
        total = jnp.dot(rows_ref[...], down_ref[0], preferred_element_type=F32)
        keep_ref[...] = total[:half]
        send_ref[...] = total[half:]

    return pl.pallas_call(
        kernel,
        in_specs=[ANY] * 4 + [VMEM],
        out_specs=[VMEM] * 2,
        out_shape=[jax.ShapeDtypeStruct((half, rank), F32)] * 2,
        scratch_shapes=[
            pltpu.VMEM((2 * half, depth), BF16),
            pltpu.SemaphoreType.DMA((4,)),
        ],
        compiler_params=params(12),
        name="low_pair",
        cost_estimate=pl.CostEstimate(
            flops=4 * half * depth * rank,
            bytes_accessed=4 * half * depth + 2 * depth * rank,
            transcendentals=0,
        ),
    )(*chunks, down)


def low_own(keeps, receives, store_row, levels):
    half, rank = keeps[0].shape
    pairs = levels // 2

    def kernel(*refs):
        row_ref, out_ref = refs[-2], refs[-1]
        index = lax.axis_index("mp")
        for k in range(pairs):
            at = lax.rem(index // 2 - k + levels, pairs)
            rows = pl.ds(pl.multiple_of(at * half, half), half)
            total = refs[k][...] + refs[pairs + k][...]
            total = jnp.where(row_ref[rows, :] == index, total, 0.0)
            out_ref[rows, :] = total.astype(BF16)

    return pl.pallas_call(
        kernel,
        in_specs=[VMEM] * (2 * pairs + 1),
        out_specs=VMEM,
        out_shape=jax.ShapeDtypeStruct((pairs * half, rank), BF16),
        name="low_own",
        cost_estimate=pl.CostEstimate(
            flops=pairs * half * rank, bytes_accessed=10 * pairs * half * rank, transcendentals=0
        ),
    )(*keeps, *receives, store_row)


def finish(keeps, receives, low, store_row, panels, levels):
    half, width = keeps[0].shape
    pairs = levels // 2
    total_rows, rank = low.shape
    count, quarter, _ = panels[0].shape
    tile = 512 if width % 512 == 0 else 256

    def kernel(*refs):
        keep_refs, receive_refs = refs[:pairs], refs[pairs : 2 * pairs]
        low_ref, row_ref = refs[2 * pairs : 2 * pairs + 2]
        panel_refs = refs[2 * pairs + 2 : 2 * pairs + 6]
        out_ref, spread_ref = refs[-2:]

        @pl.when(pl.program_id(0) == 0)
        def _():
            group, core = lax.rem(lax.axis_index("groups"), 2), lax.axis_index("sub")
            at = lax.broadcasted_iota(jnp.int32, (rank, count * quarter), 0)
            to = lax.broadcasted_iota(jnp.int32, (rank, count * quarter), 1)
            mine = (
                lax.broadcasted_iota(jnp.int32, (total_rows, count * quarter), 1) // quarter
                == row_ref[...]
            )
            for i, (own_group, own_core) in enumerate(
                ((True, True), (False, True), (True, False), (False, False))
            ):
                which = 2 * (group if own_group else 1 - group) + (core if own_core else 1 - core)
                picks = (at == which * quarter + lax.rem(to, quarter)).astype(BF16)
                spread = jnp.dot(low_ref[...], picks, preferred_element_type=F32)
                spread_ref[i] = jnp.where(mine, spread, 0.0).astype(BF16)

        index = lax.axis_index("mp")
        for k in range(pairs):
            at = lax.rem(index // 2 - k + levels, pairs)
            rows = pl.ds(pl.multiple_of(at * half, half), half)
            spread_rows = [spread_ref[i, rows, :] for i in range(4)]
            delta = sum(
                jnp.dot(
                    spread_rows[i],
                    panel_refs[i][...].reshape(count * quarter, tile),
                    preferred_element_type=F32,
                )
                for i in range(4)
            )
            base = keep_refs[k][...] + receive_refs[k][...].astype(F32)
            out_ref[rows, :] = (base + delta).astype(BF16)

    column = lambda i: (0, i)
    return pl.pallas_call(
        kernel,
        grid=(width // tile,),
        in_specs=[pl.BlockSpec((half, tile), column)] * (2 * pairs)
        + [VMEM, VMEM]
        + [pl.BlockSpec((count, quarter, tile), lambda i: (0, 0, i))] * 4,
        out_specs=pl.BlockSpec((total_rows, tile), column),
        out_shape=jax.ShapeDtypeStruct((total_rows, width), BF16),
        scratch_shapes=[pltpu.VMEM((4, total_rows, count * quarter), BF16)],
        compiler_params=params(12),
        name="finish",
        cost_estimate=pl.CostEstimate(
            flops=2 * total_rows * count * rank * width,
            bytes_accessed=2 * count * rank * width + 8 * total_rows * width,
            transcendentals=0,
        ),
    )(*keeps, *receives, low, store_row, *panels)


def swap(axis, size):
    def move(value):
        return lax.ppermute(value, axis, [(i, i ^ 1) for i in range(size)])

    return move


def per_device(tokens, gate, down, up, request_index, store_rows):
    count = store_rows.shape[0]
    levels = count // 2
    pairs = levels // 2
    shard = tokens.shape[0]
    own_tokens = shard * count // 2
    groups = lax.axis_size("groups")
    along_y = swap("mp", count)
    other_core = swap("sub", 2)
    other_group = swap("groups", groups)

    def along_z(value):
        return lax.ppermute(value, "mp", [(i, (i + 2) % count) for i in range(count)])

    near = [tokens]
    far = [along_y(tokens)]
    for _ in range(levels - 1):
        near.append(along_z(near[-1]))
        far.append(along_y(near[-1]))

    row_of_request = jnp.sum(
        jnp.where(
            request_index == jnp.arange(count, dtype=jnp.int32)[None, :], store_rows[None, :], 0
        ),
        axis=1,
    )
    begin = lax.axis_index("sub") * (own_tokens // 2)
    row_of_request = lax.dynamic_slice_in_dim(row_of_request, begin, own_tokens // 2, 0)
    store_row = jnp.broadcast_to(row_of_request[:, None], (own_tokens // 2, 2)).reshape(
        own_tokens, 1
    )

    quarter = lax.all_to_all(
        split_panels(up, count, groups), "mp", split_axis=0, concat_axis=0, tiled=True
    )
    quarter_x = other_group(quarter)
    panels = [quarter, quarter_x, other_core(quarter), other_core(quarter_x)]

    keeps, receives, low_keeps, low_receives = [], [], [], []
    for k in range(pairs):
        chunks = (near[k], far[k], near[k + pairs], far[k + pairs])
        low_keep, low_send = low_pair(chunks, down, k, levels)
        low_keeps.append(low_keep)
        low_receives.append(other_core(low_send))
        keep, send = base_pair(chunks, gate, k, levels)
        keeps.append(keep)
        receives.append(other_core(send))

    low = low_own(low_keeps, low_receives, store_row, levels)
    bit = 1
    while bit < count:
        low = low + lax.ppermute(low, "mp", [(i, i ^ bit) for i in range(count)])
        bit *= 2
    return finish(keeps, receives, low, store_row, panels, levels)


def solution(mesh):
    return jax.shard_map(
        per_device,
        mesh=mesh,
        in_specs=(
            P(("groups", "mp"), "sub"),
            P("sub", "mp"),
            P("mp", "sub", None),
            P("mp", None, None),
            P("groups", None),
            P(),
        ),
        out_specs=P(("groups", "sub"), "mp"),
        check_vma=False,
    )
```

time: 351 us -> 191 us (0.54)
  other arithmetic: 165 us -> 0.99 us
  Pallas kernels: 0 us -> 63.8 us
  local copies, waits for them, and re-layouts: 74.9 us -> 29.4 us
  matrix products: 38.1 us -> 0 us
  starting transfers between devices: 7.53 us -> 28.6 us
  waiting for transfers between devices: 51.8 us -> 67.5 us
  between operations: 13.3 us -> 0.26 us
    unnamed x1 -> x0, other arithmetic: 157 us -> none
    ppermute x0 -> x17, waiting for transfers between devices: none -> 67.5 us  [the longest x3 49.5 us: along_z(): lax.ppermute(value, 'mp', [(i, (i + 2) % count) for i in range(count)])]
    pallas_call x0 -> x7, Pallas kernels: none -> 63.8 us  [the longest x1 29 us: split_panels(): pl.pallas_call(kernel, in_specs=[ANY], out_specs=ANY, out_shape=jax.Shape...]
    all_to_all x1, waiting for transfers between devices: 35.7 us -> 0.01 us  [per_device(): lax.all_to_all(split_panels(up, count, groups), 'mp', split_axis=0, conca...]
    dot_general x2 -> x0, matrix products: 31.3 us -> none  [the longest x1 24 us: per_device(): base = jnp.dot(rows_all, gate_matrix, preferred_element_type=jnp.float32)]
    all_to_all x3 -> x0, local copies, waits for them, and re-layouts: 27.1 us -> none  [per_device(): lax.all_to_all(own_rank, 'mp', split_axis=2, concat_axis=0, tiled=True)]
    ppermute x0 -> x17, starting transfers between devices: none -> 21.2 us  [the longest x11 8.92 us: move(): return lax.ppermute(value, axis, [(i, i ^ 1) for i in range(size)])]
    reduce_scatter x1 -> x0, waiting for transfers between devices: 14.6 us -> none  [per_device(): lax.psum_scatter(base + delta, 'sub', scatter_dimension=0, tiled=True)]
  transfers between devices with their start and end apart: 5 -> 18, of which waited for: 2 -> 7; matrix products, arithmetic and copies ran while one was open for 74% -> 2% of each run, Pallas kernels for 0% -> 14%
where the time goes in v1:
time: 191 us
  waiting for transfers between devices  67.5 us (35%)
  Pallas kernels  63.8 us (33%)
  local copies, waits for them, and re-layouts  29.4 us (15%)
  starting transfers between devices  28.6 us (15%)
    ppermute x3, waiting for transfers between devices, along_z(): lax.ppermute(value, 'mp', [(i, (i + 2) % count) for i in range(count)])  49.5 us
    pallas_call x1, Pallas kernels, split_panels(): pl.pallas_call(kernel, in_specs=[ANY], out_specs=ANY, out_shape=jax.Shape...  29 us
    unnamed x37, local copies, waits for them, and re-layouts  28.5 us
    pallas_call x2, Pallas kernels, base_pair(): pl.pallas_call(kernel, grid=(width // tile,), in_specs=[ANY] * 4 + [VMEM]...  21.6 us
    ppermute x11, waiting for transfers between devices, move(): return lax.ppermute(value, axis, [(i, i ^ 1) for i in range(size)])  9.69 us
    ppermute x11, starting transfers between devices, move(): return lax.ppermute(value, axis, [(i, i ^ 1) for i in range(size)])  8.92 us
    ppermute x3, waiting for transfers between devices, per_device(): low = low + lax.ppermute(low, 'mp', [(i, i ^ bit) for i in range(count)])  8.4 us
    pallas_call x1, Pallas kernels, finish(): pl.pallas_call(kernel, grid=(width // tile,), in_specs=[pl.BlockSpec((hal...  7.53 us
  transfers between devices with their start and end apart: 18, of which 7 were waited for; matrix products, arithmetic and copies ran while one was open for 2% of the time, Pallas kernels for 14%

profile of v1, /device:TPU:0, one launch (start us, length us, event | category | flops | bytes accessed | tf_op | source)
XLA Modules:
  0.0 190.6 jit_solution(1074669168822309344)
XLA Ops:
  0.0 29.0 %split_panels.1 = bf16[8,16,3584]{2,1,0:T(8,128)(2,1)} custom-call(bf16[1,64,28672]{2,1,0:T(8,128)(2,1)} %up_ref.1), custom_call_target="tpu_custom_call" | custom-call | bytes 1835008 | tf_op jit(solution)/shard_map/split_panels/pallas_call | solution.py:36
  29.0 7.4 %all-to-all-start = ((bf16[8,16,3584]{2,1,0:T(8,128)(2,1)}), bf16[8,16,3584]{2,1,0:T(8,128)(2,1)S(1)}, u32[]{:S(2)}, u32[]{:S(2)}) async-start(bf16[8,16,3584]{2,1,0:T(8,128)(2,1)} %split_panels.1), calls=%async_computation | async-start | bytes 1835008 | tf_op jit(solution)/shard_map/all_to_all | solution.py:278
  36.4 2.0 %collective-permute-start.1 = (bf16[64,4096]{1,0:T(8,128)(2,1)S(1)}, bf16[64,4096]{1,0:T(8,128)(2,1)S(1)}, u32[]{:S(2)}, u32[]{:S(2)}) collective-permute-start(bf16[64,4096]{1,0:T(8,128)(2,1)S(1)} %copy-done.2), channel_id=1, source_target_pairs={{0,4},{2,6},{4,8},{6,10},{8,12},{10,14},{12,0},{14,2},{1,5},{3,7},... | collective-permute-start | bytes 1572872 | tf_op jit(solution)/shard_map/ppermute | solution.py:258
  38.4 28.2 %collective-permute-done.1.c0 = bf16[64,4096]{1,0:T(8,128)(2,1)S(1)} collective-permute-done((bf16[64,4096]{1,0:T(8,128)(2,1)S(1)}, bf16[64,4096]{1,0:T(8,128)(2,1)S(1)}, u32[]{:S(2)}, u32[]{:S(2)}) %collective-permute-start.1) | collective-permute-done | bytes 524320 | tf_op jit(solution)/shard_map/ppermute | solution.py:258
  66.6 2.4 %collective-permute-start.2 = (bf16[64,4096]{1,0:T(8,128)(2,1)S(1)}, bf16[64,4096]{1,0:T(8,128)(2,1)S(1)}, u32[]{:S(2)}, u32[]{:S(2)}) collective-permute-start(bf16[64,4096]{1,0:T(8,128)(2,1)S(1)} %collective-permute-done.1.c0), channel_id=1, source_target_pairs={{0,4},{2,6},{4,8},{6,10},{8,12},{10,14},{12,0},{14,2},{1,5},{3,7},... | collective-permute-start | bytes 1572872 | tf_op jit(solution)/shard_map/ppermute | solution.py:258
  69.0 12.1 %collective-permute-done.2.c2 = bf16[64,4096]{1,0:T(8,128)(2,1)S(1)} collective-permute-done((bf16[64,4096]{1,0:T(8,128)(2,1)S(1)}, bf16[64,4096]{1,0:T(8,128)(2,1)S(1)}, u32[]{:S(2)}, u32[]{:S(2)}) %collective-permute-start.2) | collective-permute-done | bytes 524320 | tf_op jit(solution)/shard_map/ppermute | solution.py:258
  82.7 1.8 collective-permute-start
  84.8 1.8 collective-permute-start.4
  86.6 9.2 %collective-permute-done.5.c2 = bf16[64,4096]{1,0:T(8,128)(2,1)S(1)} collective-permute-done((bf16[64,4096]{1,0:T(8,128)(2,1)S(1)}, bf16[64,4096]{1,0:T(8,128)(2,1)S(1)}, u32[]{:S(2)}, u32[]{:S(2)}) %collective-permute-start.5) | collective-permute-done | bytes 524320 | tf_op jit(solution)/shard_map/ppermute | solution.py:258
  95.8 1.9 %collective-permute-start.6 = (bf16[64,4096]{1,0:T(8,128)(2,1)S(1)}, bf16[64,4096]{1,0:T(8,128)(2,1)}, u32[]{:S(2)}, u32[]{:S(2)}) collective-permute-start(bf16[64,4096]{1,0:T(8,128)(2,1)S(1)} %collective-permute-done.5.c2), channel_id=1, source_target_pairs={{0,2},{2,0},{4,6},{6,4},{8,10},{10,8},{12,14},{14,12},{1,3},{3,1},... | collective-permute-start | bytes 1572872 | tf_op jit(solution)/shard_map/ppermute | solution.py:241
  99.3 9.7 %collective-permute-done.3.c3 = bf16[64,4096]{1,0:T(8,128)(2,1)} collective-permute-done((bf16[64,4096]{1,0:T(8,128)(2,1)S(1)}, bf16[64,4096]{1,0:T(8,128)(2,1)}, u32[]{:S(2)}, u32[]{:S(2)}) %collective-permute-start.3) | collective-permute-done | bytes 524320 | tf_op jit(solution)/shard_map/ppermute | solution.py:241
  108.9 9.3 %copy-done = bf16[4096,3584]{1,0:T(8,128)(2,1)S(1)} copy-done((bf16[4096,3584]{1,0:T(8,128)(2,1)S(1)}, bf16[4096,3584]{1,0:T(8,128)(2,1)}, u32[]{:S(2)}) %copy-start) | copy-done | bytes 29360152
  118.3 10.8 %base_pair.2 = (f32[128,3584]{1,0:T(8,128)S(1)}, bf16[128,3584]{1,0:T(8,128)(2,1)}) custom-call(bf16[64,4096]{1,0:T(8,128)(2,1)S(1)} %copy-done.2, bf16[64,4096]{1,0:T(8,128)(2,1)} %collective-permute-done.c1, bf16[64,4096]{1,0:T(8,128)(2,1)S(1)} %collective-permute-done.2.c2, bf16[64,4096]{1,0:T(8,128)(2,1)} %collective-permute-done.3.c3, ...), custom_call_target="tpu_custom_call" | custom-call | flops 7516192768 | bytes 4849664 | tf_op jit(solution)/shard_map/base_pair/pallas_call | solution.py:94
  130.9 9.5 %copy-done.1 = bf16[4096,3584]{1,0:T(8,128)(2,1)S(1)} copy-done((bf16[4096,3584]{1,0:T(8,128)(2,1)S(1)}, bf16[4096,3584]{1,0:T(8,128)(2,1)}, u32[]{:S(2)}) %copy-start.1) | copy-done | bytes 29360152
  140.4 10.8 %base_pair.3 = (f32[128,3584]{1,0:T(8,128)S(1)}, bf16[128,3584]{1,0:T(8,128)(2,1)}) custom-call(bf16[64,4096]{1,0:T(8,128)(2,1)S(1)} %collective-permute-done.1.c0, bf16[64,4096]{1,0:T(8,128)(2,1)S(1)} %collective-permute-done.4.c1, bf16[64,4096]{1,0:T(8,128)(2,1)S(1)} %collective-permute-done.5.c2, bf16[64,4096]{1,0:T(8,128)(2,1)} %collective-permute-done.6.c3, ...), custom_call_target="tpu_custom_call" | custom-call | flops 7516192768 | bytes 4849664 | tf_op jit(solution)/shard_map/base_pair/pallas_call | solution.py:94
  155.5 2.0 %low_pair.2 = (f32[128,64]{1,0:T(8,128)S(1)}, f32[128,64]{1,0:T(8,128)S(1)}) custom-call(bf16[64,4096]{1,0:T(8,128)(2,1)S(1)} %copy-done.2, bf16[64,4096]{1,0:T(8,128)(2,1)} %collective-permute-done.c1, bf16[64,4096]{1,0:T(8,128)(2,1)S(1)} %copy-done.4, bf16[64,4096]{1,0:T(8,128)(2,1)} %collective-permute-done.3.c3, bf16[1,4096,64]{2,1,0:T(8,128)(2,1)S(1)} %copy.13.down_ref), custom_call_target="tpu_custom_call" | custom-call | flops 134217728 | bytes 2621440 | tf_op jit(solution)/shard_map/low_pair/pallas_call | solution.py:128
  157.7 1.9 %low_pair.3 = (f32[128,64]{1,0:T(8,128)S(1)}, f32[128,64]{1,0:T(8,128)S(1)}) custom-call(bf16[64,4096]{1,0:T(8,128)(2,1)S(1)} %collective-permute-done.1.c0, bf16[64,4096]{1,0:T(8,128)(2,1)S(1)} %copy-done.6, bf16[64,4096]{1,0:T(8,128)(2,1)S(1)} %collective-permute-done.5.c2, bf16[64,4096]{1,0:T(8,128)(2,1)} %collective-permute-done.6.c3, ...), custom_call_target="tpu_custom_call" | custom-call | flops 134217728 | bytes 2621440 | tf_op jit(solution)/shard_map/low_pair/pallas_call | solution.py:128
  163.6 1.8 collective-permute-start.11
  165.4 2.7 %collective-permute-done.11 = bf16[256,64]{1,0:T(8,128)(2,1)S(1)} collective-permute-done((bf16[256,64]{1,0:T(8,128)(2,1)}, bf16[256,64]{1,0:T(8,128)(2,1)S(1)}, u32[]{:S(2)}, u32[]{:S(2)}) %collective-permute-start.11) | collective-permute-done | bytes 32800 | tf_op jit(solution)/shard_map/ppermute | solution.py:297
  169.0 2.5 %collective-permute-start.12 = (bf16[256,64]{1,0:T(8,128)(2,1)S(1)}, bf16[256,64]{1,0:T(8,128)(2,1)S(1)}, u32[]{:S(2)}, u32[]{:S(2)}) collective-permute-start(bf16[256,64]{1,0:T(8,128)(2,1)S(1)} %add.13), channel_id=1, source_target_pairs={{0,4},{2,6},{4,0},{6,2},{8,12},{10,14},{12,8},{14,10},{1,5},{3,7},... | collective-permute-start | bytes 98312 | tf_op jit(solution)/shard_map/ppermute | solution.py:297
  171.6 2.2 %collective-permute-done.12 = bf16[256,64]{1,0:T(8,128)(2,1)S(1)} collective-permute-done((bf16[256,64]{1,0:T(8,128)(2,1)S(1)}, bf16[256,64]{1,0:T(8,128)(2,1)S(1)}, u32[]{:S(2)}, u32[]{:S(2)}) %collective-permute-start.12) | collective-permute-done | bytes 32800 | tf_op jit(solution)/shard_map/ppermute | solution.py:297
  173.8 1.8 collective-permute-start.13
  175.6 3.4 %collective-permute-done.13 = bf16[256,64]{1,0:T(8,128)(2,1)S(1)} collective-permute-done((bf16[256,64]{1,0:T(8,128)(2,1)S(1)}, bf16[256,64]{1,0:T(8,128)(2,1)S(1)}, u32[]{:S(2)}, u32[]{:S(2)}) %collective-permute-start.13) | collective-permute-done | bytes 32800 | tf_op jit(solution)/shard_map/ppermute | solution.py:297
  183.0 7.5 %finish.1 = bf16[256,3584]{1,0:T(8,128)(2,1)} custom-call(f32[128,3584]{1,0:T(8,128)S(1)} %copy-done.8, f32[128,3584]{1,0:T(8,128)S(1)} %copy-done.10, bf16[128,3584]{1,0:T(8,128)(2,1)} %collective-permute-done.7.refs_2_, bf16[128,3584]{1,0:T(8,128)(2,1)} %collective-permute-done.8.refs_3_, bf16[256,64]{1,0:T(8,128)(2,1)S(1)} %add.15.refs_4_, ...), custom_call_target="tpu_custom_call" | custom-call | flops 939524096 | bytes 11010048 | tf_op jit(solution)/shard_map/finish/pallas_call | solution.py:220
  (63 shorter events, 18.3 us)
Async XLA Ops:
  29.0 7.4 %copy-start.2 = (bf16[64,4096]{1,0:T(8,128)(2,1)S(1)}, bf16[64,4096]{1,0:T(8,128)(2,1)}, u32[]{:S(2)}) copy-start(bf16[64,4096]{1,0:T(8,128)(2,1)} %c0.3) | copy-start | bytes 1572868
  29.0 68.8 %all-to-all-start = ((bf16[8,16,3584]{2,1,0:T(8,128)(2,1)}), bf16[8,16,3584]{2,1,0:T(8,128)(2,1)S(1)}, u32[]{:S(2)}, u32[]{:S(2)}) async-start(bf16[8,16,3584]{2,1,0:T(8,128)(2,1)} %split_panels.1), calls=%async_computation | async-start | bytes 1835008 | tf_op jit(solution)/shard_map/all_to_all | solution.py:278
  36.4 30.2 %collective-permute-start.1 = (bf16[64,4096]{1,0:T(8,128)(2,1)S(1)}, bf16[64,4096]{1,0:T(8,128)(2,1)S(1)}, u32[]{:S(2)}, u32[]{:S(2)}) collective-permute-start(bf16[64,4096]{1,0:T(8,128)(2,1)S(1)} %copy-done.2), channel_id=1, source_target_pairs={{0,4},{2,6},{4,8},{6,10},{8,12},{10,14},{12,0},{14,2},{1,5},{3,7},... | collective-permute-start | bytes 1572872 | tf_op jit(solution)/shard_map/ppermute | solution.py:258
  66.6 14.4 %collective-permute-start.2 = (bf16[64,4096]{1,0:T(8,128)(2,1)S(1)}, bf16[64,4096]{1,0:T(8,128)(2,1)S(1)}, u32[]{:S(2)}, u32[]{:S(2)}) collective-permute-start(bf16[64,4096]{1,0:T(8,128)(2,1)S(1)} %collective-permute-done.1.c0), channel_id=1, source_target_pairs={{0,4},{2,6},{4,8},{6,10},{8,12},{10,14},{12,0},{14,2},{1,5},{3,7},... | collective-permute-start | bytes 1572872 | tf_op jit(solution)/shard_map/ppermute | solution.py:258
  81.0 48.1 %copy-start.3 = (bf16[64,4096]{1,0:T(8,128)(2,1)}, bf16[64,4096]{1,0:T(8,128)(2,1)S(1)}, u32[]{:S(2)}) copy-start(bf16[64,4096]{1,0:T(8,128)(2,1)S(1)} %collective-permute-done.2.c2) | copy-start | bytes 1572868
  81.0 14.8 %collective-permute-start.5 = (bf16[64,4096]{1,0:T(8,128)(2,1)S(1)}, bf16[64,4096]{1,0:T(8,128)(2,1)S(1)}, u32[]{:S(2)}, u32[]{:S(2)}) collective-permute-start(bf16[64,4096]{1,0:T(8,128)(2,1)S(1)} %collective-permute-done.2.c2), channel_id=1, source_target_pairs={{0,4},{2,6},{4,8},{6,10},{8,12},{10,14},{12,0},{14,2},{1,5},{3,7},... | collective-permute-start | bytes 1572872 | tf_op jit(solution)/shard_map/ppermute | solution.py:258
  82.7 16.5 %collective-permute-start = (bf16[64,4096]{1,0:T(8,128)(2,1)S(1)}, bf16[64,4096]{1,0:T(8,128)(2,1)}, u32[]{:S(2)}, u32[]{:S(2)}) collective-permute-start(bf16[64,4096]{1,0:T(8,128)(2,1)S(1)} %copy-done.2), channel_id=1, source_target_pairs={{0,2},{2,0},{4,6},{6,4},{8,10},{10,8},{12,14},{14,12},{1,3},{3,1},... | collective-permute-start | bytes 1572872 | tf_op jit(solution)/shard_map/ppermute | solution.py:241
  84.6 24.4 %collective-permute-start.3 = (bf16[64,4096]{1,0:T(8,128)(2,1)S(1)}, bf16[64,4096]{1,0:T(8,128)(2,1)}, u32[]{:S(2)}, u32[]{:S(2)}) collective-permute-start(bf16[64,4096]{1,0:T(8,128)(2,1)S(1)} %collective-permute-done.2.c2), channel_id=1, source_target_pairs={{0,2},{2,0},{4,6},{6,4},{8,10},{10,8},{12,14},{14,12},{1,3},{3,1},... | collective-permute-start | bytes 1572872 | tf_op jit(solution)/shard_map/ppermute | solution.py:241
  84.8 46.1 %collective-permute-start.4 = (bf16[64,4096]{1,0:T(8,128)(2,1)S(1)}, bf16[64,4096]{1,0:T(8,128)(2,1)S(1)}, u32[]{:S(2)}, u32[]{:S(2)}) collective-permute-start(bf16[64,4096]{1,0:T(8,128)(2,1)S(1)} %collective-permute-done.1.c0), channel_id=1, source_target_pairs={{0,2},{2,0},{4,6},{6,4},{8,10},{10,8},{12,14},{14,12},{1,3},{3,1},... | collective-permute-start | bytes 1572872 | tf_op jit(solution)/shard_map/ppermute | solution.py:241
  95.8 35.1 %collective-permute-start.6 = (bf16[64,4096]{1,0:T(8,128)(2,1)S(1)}, bf16[64,4096]{1,0:T(8,128)(2,1)}, u32[]{:S(2)}, u32[]{:S(2)}) collective-permute-start(bf16[64,4096]{1,0:T(8,128)(2,1)S(1)} %collective-permute-done.5.c2), channel_id=1, source_target_pairs={{0,2},{2,0},{4,6},{6,4},{8,10},{10,8},{12,14},{14,12},{1,3},{3,1},... | collective-permute-start | bytes 1572872 | tf_op jit(solution)/shard_map/ppermute | solution.py:241
  97.8 54.7 %collective-permute-start.14 = (bf16[8,16,3584]{2,1,0:T(8,128)(2,1)S(1)}, bf16[8,16,3584]{2,1,0:T(8,128)(2,1)}, u32[]{:S(2)}, u32[]{:S(2)}) collective-permute-start(bf16[8,16,3584]{2,1,0:T(8,128)(2,1)S(1)} %all-to-all-done.refs_6_), channel_id=1, source_target_pairs={{0,16},{16,0},{1,17},{17,1},{2,18},{18,2},{3,19},{19,3},{4,20},{20... | collective-permute-start | bytes 2752520 | tf_op jit(solution)/shard_map/ppermute | solution.py:241
  108.9 9.4 %copy-start = (bf16[4096,3584]{1,0:T(8,128)(2,1)S(1)}, bf16[4096,3584]{1,0:T(8,128)(2,1)}, u32[]{:S(2)}) copy-start(bf16[4096,3584]{1,0:T(8,128)(2,1)} %gate_ref.3) | copy-start | bytes 88080384
  130.4 48.7 %collective-permute-start.7 = (bf16[128,3584]{1,0:T(8,128)(2,1)}, bf16[128,3584]{1,0:T(8,128)(2,1)}, u32[]{:S(2)}, u32[]{:S(2)}) collective-permute-start(bf16[128,3584]{1,0:T(8,128)(2,1)} %get-tuple-element.15), channel_id=1, source_target_pairs={{0,1},{1,0},{2,3},{3,2},{4,5},{5,4},{6,7},{7,6},{8,9},{9,8},{10,11... | collective-permute-start | bytes 2752520 | tf_op jit(solution)/shard_map/ppermute | solution.py:241
  130.4 48.7 %collective-permute-start.15 = (bf16[8,16,3584]{2,1,0:T(8,128)(2,1)S(1)}, bf16[8,16,3584]{2,1,0:T(8,128)(2,1)}, u32[]{:S(2)}, u32[]{:S(2)}) collective-permute-start(bf16[8,16,3584]{2,1,0:T(8,128)(2,1)S(1)} %all-to-all-done.refs_6_), channel_id=1, source_target_pairs={{0,1},{1,0},{2,3},{3,2},{4,5},{5,4},{6,7},{7,6},{8,9},{9,8},{10,11... | collective-permute-start | bytes 2752520 | tf_op jit(solution)/shard_map/ppermute | solution.py:241
  130.9 20.3 %copy-start.5 = (bf16[64,4096]{1,0:T(8,128)(2,1)}, bf16[64,4096]{1,0:T(8,128)(2,1)S(1)}, u32[]{:S(2)}) copy-start(bf16[64,4096]{1,0:T(8,128)(2,1)S(1)} %collective-permute-done.4.c1) | copy-start | bytes 1572868
  130.9 9.5 %copy-start.1 = (bf16[4096,3584]{1,0:T(8,128)(2,1)S(1)}, bf16[4096,3584]{1,0:T(8,128)(2,1)}, u32[]{:S(2)}) copy-start(bf16[4096,3584]{1,0:T(8,128)(2,1)} %gate_ref.3) | copy-start | bytes 88080384
  152.5 26.7 %collective-permute-start.8 = (bf16[128,3584]{1,0:T(8,128)(2,1)}, bf16[128,3584]{1,0:T(8,128)(2,1)}, u32[]{:S(2)}, u32[]{:S(2)}) collective-permute-start(bf16[128,3584]{1,0:T(8,128)(2,1)} %get-tuple-element.16), channel_id=1, source_target_pairs={{0,1},{1,0},{2,3},{3,2},{4,5},{5,4},{6,7},{7,6},{8,9},{9,8},{10,11... | collective-permute-start | bytes 2752520 | tf_op jit(solution)/shard_map/ppermute | solution.py:241
  152.5 26.7 %collective-permute-start.16 = (bf16[8,16,3584]{2,1,0:T(8,128)(2,1)}, bf16[8,16,3584]{2,1,0:T(8,128)(2,1)}, u32[]{:S(2)}, u32[]{:S(2)}) collective-permute-start(bf16[8,16,3584]{2,1,0:T(8,128)(2,1)} %collective-permute-done.14.refs_7_), channel_id=1, source_target_pairs={{0,1},{1,0},{2,3},{3,2},{4,5},{5,4},{6,7},{7,6},{8,9},{9,8},{10,11... | collective-permute-start | bytes 2752520 | tf_op jit(solution)/shard_map/ppermute | solution.py:241
  157.6 2.6 %copy-start.16 = (s32[256,1]{0,1:T(1,128)S(1)}, s32[256,1]{0,1:T(1,128)}, u32[]{:S(2)}) copy-start(s32[256,1]{0,1:T(1,128)} %param.10) | copy-start | bytes 3076
  157.6 2.0 %collective-permute-start.9 = (f32[128,64]{1,0:T(8,128)S(1)}, f32[128,64]{1,0:T(8,128)S(1)}, u32[]{:S(2)}, u32[]{:S(2)}) collective-permute-start(f32[128,64]{1,0:T(8,128)S(1)} %get-tuple-element.19), channel_id=1, source_target_pairs={{0,1},{1,0},{2,3},{3,2},{4,5},{5,4},{6,7},{7,6},{8,9},{9,8},{10,11... | collective-permute-start | bytes 98312 | tf_op jit(solution)/shard_map/ppermute | solution.py:241
  159.7 1.5 collective-permute-start.10
  163.6 4.6 %collective-permute-start.11 = (bf16[256,64]{1,0:T(8,128)(2,1)}, bf16[256,64]{1,0:T(8,128)(2,1)S(1)}, u32[]{:S(2)}, u32[]{:S(2)}) collective-permute-start(bf16[256,64]{1,0:T(8,128)(2,1)} %low_own.1), channel_id=1, source_target_pairs={{0,2},{2,0},{4,6},{6,4},{8,10},{10,8},{12,14},{14,12},{1,3},{3,1},... | collective-permute-start | bytes 98312 | tf_op jit(solution)/shard_map/ppermute | solution.py:297
  169.0 4.8 %collective-permute-start.12 = (bf16[256,64]{1,0:T(8,128)(2,1)S(1)}, bf16[256,64]{1,0:T(8,128)(2,1)S(1)}, u32[]{:S(2)}, u32[]{:S(2)}) collective-permute-start(bf16[256,64]{1,0:T(8,128)(2,1)S(1)} %add.13), channel_id=1, source_target_pairs={{0,4},{2,6},{4,0},{6,2},{8,12},{10,14},{12,8},{14,10},{1,5},{3,7},... | collective-permute-start | bytes 98312 | tf_op jit(solution)/shard_map/ppermute | solution.py:297
  173.8 5.2 %collective-permute-start.13 = (bf16[256,64]{1,0:T(8,128)(2,1)S(1)}, bf16[256,64]{1,0:T(8,128)(2,1)S(1)}, u32[]{:S(2)}, u32[]{:S(2)}) collective-permute-start(bf16[256,64]{1,0:T(8,128)(2,1)S(1)} %add.14), channel_id=1, source_target_pairs={{0,8},{2,10},{4,12},{6,14},{8,0},{10,2},{12,4},{14,6},{1,9},{3,11}... | collective-permute-start | bytes 98312 | tf_op jit(solution)/shard_map/ppermute | solution.py:297
  (12 other events, 18.0 us)

commit v2 on v0

v2 whole, which is shorter than its diff:
```python
import jax
import jax.numpy as jnp
from jax import lax
from jax.experimental import pallas as pl
from jax.experimental.pallas import tpu as pltpu
from jax.sharding import PartitionSpec as P

F32 = jnp.float32
BF16 = jnp.bfloat16
ANY = pl.BlockSpec(memory_space=pl.ANY)
VMEM = pl.BlockSpec(memory_space=pltpu.VMEM)
ROWS_BY_ROWS = (((1,), (1,)), ((), ()))


def in_vmem(*values):
    return [pltpu.with_memory_space_constraint(value, pltpu.VMEM) for value in values]


def params(mib):
    return pltpu.CompilerParams(vmem_limit_bytes=mib << 20)


def run_copies(copies):
    for copy in copies:
        copy.start()
    for copy in copies:
        copy.wait()


def in_hbm(*values):
    return [pltpu.with_memory_space_constraint(value, pltpu.HBM) for value in values]


def position(levels):
    index = lax.axis_index("mp")
    return index // 2, lax.rem(index, 2)


def rows_of_tokens(requests, store_rows, tokens):
    count = requests.shape[1]

    def kernel(requests_ref, rows_ref, out_ref):
        request = requests_ref[...]
        row = jnp.zeros_like(request)
        for i in range(store_rows.shape[0]):
            row = jnp.where(request == i, rows_ref[i], row)
        token = lax.axis_index("sub") * tokens + lax.broadcasted_iota(
            jnp.int32, (tokens, count), 0
        )
        own = token // 2 == lax.broadcasted_iota(jnp.int32, (tokens, count), 1)
        chosen = jnp.where(own, row.astype(F32), 0.0)
        out_ref[...] = jnp.sum(chosen, axis=1, keepdims=True).astype(jnp.int32)

    return pl.pallas_call(
        kernel,
        in_specs=[VMEM, pl.BlockSpec(memory_space=pltpu.SMEM)],
        out_specs=VMEM,
        out_shape=jax.ShapeDtypeStruct((tokens, 1), jnp.int32),
        compiler_params=params(6),
        name="rows_of_tokens",
    )(requests, store_rows)


def split_panels(up, offsets, levels):
    rank, hidden = up.shape[1], up.shape[2]
    quarter, width = rank // 4, hidden // (2 * levels)

    def kernel(up_ref, *refs):
        out_refs, sem = refs[:-1], refs[-1]
        z, y = position(levels)
        which = 2 * lax.rem(lax.axis_index("groups"), 2) + lax.axis_index("sub")
        rows = pl.ds(pl.multiple_of(which * quarter, quarter), quarter)
        copies = []
        for i, (dz, dy) in enumerate(offsets):
            to = 2 * lax.rem(z + dz, levels) + (1 - y if dy else y)
            columns = pl.ds(pl.multiple_of(to * width, 128), width)
            copies.append(
                pltpu.make_async_copy(up_ref.at[0, rows, columns], out_refs[i], sem.at[i])
            )
        run_copies(copies)

    return pl.pallas_call(
        kernel,
        in_specs=[ANY],
        out_specs=[VMEM] * len(offsets),
        out_shape=[jax.ShapeDtypeStruct((quarter, width), BF16)] * len(offsets),
        scratch_shapes=[pltpu.SemaphoreType.DMA((len(offsets),))],
        compiler_params=params(6),
        name="split_panels",
    )(*in_hbm(up))


def stack(blocks):
    count = len(blocks)

    def kernel(*refs):
        run_copies(
            [pltpu.make_async_copy(refs[i], refs[count].at[i], refs[-1].at[i]) for i in range(count)]
        )

    return pl.pallas_call(
        kernel,
        in_specs=[ANY] * count,
        out_specs=VMEM,
        out_shape=jax.ShapeDtypeStruct((count, *blocks[0].shape), BF16),
        scratch_shapes=[pltpu.SemaphoreType.DMA((count,))],
        compiler_params=params(6),
        name="stack",
    )(*blocks)


HELD, PARTS = 5, 7


def hold_gate(gate):
    depth, width = gate.shape
    columns = width // PARTS * HELD
    pieces = 8

    def kernel(gate_ref, out_ref, mark_ref, sem):
        mark_ref[...] = jnp.zeros_like(mark_ref)
        size = depth // pieces
        run_copies(
            [
                pltpu.make_async_copy(
                    gate_ref.at[pl.ds(i * size, size), pl.ds(0, columns)],
                    out_ref.at[pl.ds(i * size, size)],
                    sem.at[i],
                )
                for i in range(pieces)
            ]
        )

    return pl.pallas_call(
        kernel,
        in_specs=[ANY],
        out_specs=[VMEM, VMEM],
        out_shape=[pltpu.VMEM((depth, columns), BF16), jax.ShapeDtypeStruct((8, 128), F32)],
        scratch_shapes=[pltpu.SemaphoreType.DMA((pieces,))],
        compiler_params=params(6),
        name="hold_gate",
    )(gate)


def keeps_first(step, levels):
    origin = lax.rem(position(levels)[0] - step + levels, levels)
    return (origin // (levels // 2)) == lax.axis_index("sub")


def pair_rows(step, levels, half):
    at = lax.rem(position(levels)[0] - step + levels, levels // 2)
    return pl.ds(pl.multiple_of(at * half, half), half)


def load_rows(near_ref, far_ref, rows_ref):
    shard = near_ref.shape[0]
    y = position(2)[1]
    rows_ref[pl.ds(pl.multiple_of(y * shard, shard), shard), :] = near_ref[...]
    rows_ref[pl.ds(pl.multiple_of((1 - y) * shard, shard), shard), :] = far_ref[...]


def base_chunk(near, far, gate, held, pair, down, step, levels, after=None):
    shard, depth = near.shape
    width = gate.shape[1]
    tile = width // PARTS
    piece = tile // 2
    pieces = 2 * (PARTS - HELD)
    assert pieces < HELD
    half = 2 * shard
    inputs = in_vmem(*pair, held) + [gate, near, far]
    outputs = [pltpu.VMEM((half, width), F32), pltpu.VMEM((half, width), BF16)]
    if after is not None:
        inputs.append(after)
    if down is not None:
        inputs.append(down)
        outputs.append(jax.ShapeDtypeStruct((half, down.shape[1]), F32))

    def kernel(*refs):
        held_ref, gate_ref, near_ref, far_ref = refs[len(pair) : len(pair) + 4]
        out_refs, (rows_ref, piece_ref, sem) = refs[len(inputs) : -3], refs[-3:]
        mine = keeps_first(step, levels)
        at = pl.program_id(0)

        def fetch(i):
            begin = pl.multiple_of(HELD * tile + i * piece, piece)
            slot = lax.rem(i, 2)
            return pltpu.make_async_copy(
                gate_ref.at[:, pl.ds(begin, piece)], piece_ref.at[slot], sem.at[slot]
            )

        def put(begin, size, total):
            columns = pl.ds(pl.multiple_of(begin, size), size)

            @pl.when(mine)
            def _():
                out_refs[0][:, columns] = total

            @pl.when(jnp.logical_not(mine))
            def _():
                out_refs[1][:, columns] = total.astype(BF16)

        @pl.when(at == 0)
        def _():
            fetch(0).start()
            fetch(1).start()
            load_rows(near_ref, far_ref, rows_ref)
            if down is not None:
                out_refs[-1][...] = lax.dot_general(
                    rows_ref[...],
                    refs[len(inputs) - 1][0],
                    ROWS_BY_ROWS,
                    preferred_element_type=F32,
                )

        columns = pl.ds(pl.multiple_of(at * tile, tile), tile)
        put(
            at * tile,
            tile,
            jnp.dot(rows_ref[...], held_ref[:, columns], preferred_element_type=F32),
        )

        @pl.when((at > 0) & (at <= pieces))
        def _():
            fetch(at - 1).wait()
            total = jnp.dot(
                rows_ref[...], piece_ref[lax.rem(at - 1, 2)], preferred_element_type=F32
            )
            put(HELD * tile + (at - 1) * piece, piece, total)

            @pl.when(at + 1 < pieces)
            def _():
                fetch(at + 1).start()

    return pl.pallas_call(
        kernel,
        grid=(HELD,),
        in_specs=[VMEM] * (len(pair) + 1) + [ANY] + [VMEM] * (len(inputs) - len(pair) - 2),
        out_specs=[VMEM] * len(outputs),
        out_shape=outputs,
        scratch_shapes=[
            pltpu.VMEM((half, depth), BF16),
            pltpu.VMEM((2, depth, piece), BF16),
            pltpu.SemaphoreType.DMA((2,)),
        ],
        input_output_aliases={0: 0, 1: 1} if pair else {},
        compiler_params=params(10),
        name="base_chunk",
    )(*inputs)


def low_last(near, far, down, lows, levels):
    shard, depth = near.shape
    rank = down.shape[1]
    half = 2 * shard
    pairs = levels // 2

    def kernel(*refs):
        near_ref, far_ref, down_ref = refs[:3]
        low_refs = refs[3 : 2 + levels]
        keep_ref, send_ref, rows_ref = refs[2 + levels :]
        load_rows(near_ref, far_ref, rows_ref)
        last = lax.dot_general(
            rows_ref[...], down_ref[0], ROWS_BY_ROWS, preferred_element_type=F32
        )
        for k in range(pairs):
            rows = pair_rows(k, levels, half)
            first = low_refs[k][...]
            second = last if k == pairs - 1 else low_refs[k + pairs][...]
            mine = keeps_first(k, levels)
            keep_ref[rows, :] = jnp.where(mine, first, second)
            send_ref[rows, :] = jnp.where(mine, second, first)

    return pl.pallas_call(
        kernel,
        in_specs=[VMEM] * (2 + levels),
        out_specs=[VMEM] * 2,
        out_shape=[jax.ShapeDtypeStruct((pairs * half, rank), F32)] * 2,
        scratch_shapes=[pltpu.VMEM((half, depth), BF16)],
        compiler_params=params(6),
        name="low_last",
    )(near, far, down, *lows)


def low_own(keep, receive, store_row):
    def kernel(keep_ref, receive_ref, row_ref, out_ref):
        total = keep_ref[...] + receive_ref[...]
        out_ref[...] = jnp.where(row_ref[...] == lax.axis_index("mp"), total, 0.0).astype(BF16)

    return pl.pallas_call(
        kernel,
        in_specs=[VMEM] * 3,
        out_specs=VMEM,
        out_shape=jax.ShapeDtypeStruct(keep.shape, BF16),
        compiler_params=params(6),
        name="low_own",
    )(keep, receive, store_row)


def add(one, two):
    def kernel(one_ref, two_ref, out_ref):
        out_ref[...] = one_ref[...] + two_ref[...]

    return pl.pallas_call(
        kernel,
        in_specs=[VMEM] * 2,
        out_specs=VMEM,
        out_shape=jax.ShapeDtypeStruct(one.shape, one.dtype),
        compiler_params=params(6),
        name="add",
    )(one, two)


def finish(keeps, receives, lows, store_row, panels, offsets, levels):
    half, width = keeps[0].shape
    pairs = levels // 2
    total_rows, rank = lows[0].shape
    quarter = rank // 4
    parts = len(panels[0])
    blocks = len(offsets)
    tile = 512 if width % 512 == 0 else 256
    flat = [array for group in panels for array in group]

    def kernel(*refs):
        keep_refs, receive_refs = refs[:pairs], refs[pairs : 2 * pairs]
        row_ref = refs[2 * pairs]
        panel_refs = refs[2 * pairs + 1 : 2 * pairs + 1 + len(flat)]
        low_refs = refs[2 * pairs + 1 + len(flat) : -2]
        out_ref, spread_ref = refs[-2:]

        @pl.when(pl.program_id(0) == 0)
        def _():
            low = low_refs[0][...]
            for other in low_refs[1:]:
                low = low + other[...]
            group, core = lax.rem(lax.axis_index("groups"), 2), lax.axis_index("sub")
            z, y = position(levels)
            span = blocks * quarter
            at = lax.broadcasted_iota(jnp.int32, (rank, span), 0)
            to = lax.broadcasted_iota(jnp.int32, (rank, span), 1)
            block = lax.broadcasted_iota(jnp.int32, (total_rows, span), 1) // quarter
            row = jnp.zeros((total_rows, span), jnp.int32)
            for i, (dz, dy) in enumerate(offsets):
                source = 2 * lax.rem(z - dz + levels, levels) + (1 - y if dy else y)
                row = jnp.where(block == i, source, row)
            mine = row == row_ref[...]
            for i, (own_group, own_core) in enumerate(
                ((True, True), (False, True), (True, False), (False, False))
            ):
                which = 2 * (group if own_group else 1 - group) + (core if own_core else 1 - core)
                picks = (at == which * quarter + lax.rem(to, quarter)).astype(BF16)
                spread = jnp.dot(low, picks, preferred_element_type=F32)
                spread = jnp.where(mine, spread, 0.0).astype(BF16)
                spread_ref[:, i * span : (i + 1) * span] = spread

        panel = jnp.concatenate(
            [ref[...].reshape(ref.shape[0] * quarter, tile) for ref in panel_refs], axis=0
        )
        columns = pl.ds(pl.multiple_of(pl.program_id(0) * tile, tile), tile)
        for k in range(pairs):
            rows = pair_rows(k, levels, half)
            delta = jnp.dot(spread_ref[rows, :], panel, preferred_element_type=F32)
            base = keep_refs[k][:, columns] + receive_refs[k][...].astype(F32)
            out_ref[rows, :] = (base + delta).astype(BF16)

    column = lambda i: (0, i)
    return pl.pallas_call(
        kernel,
        grid=(width // tile,),
        in_specs=[VMEM] * pairs
        + [pl.BlockSpec((half, tile), column)] * pairs
        + [VMEM]
        + [pl.BlockSpec((array.shape[0], quarter, tile), lambda i: (0, 0, i)) for array in flat]
        + [VMEM] * len(lows),
        out_specs=pl.BlockSpec((total_rows, tile), column),
        out_shape=jax.ShapeDtypeStruct((total_rows, width), BF16),
        scratch_shapes=[pltpu.VMEM((total_rows, blocks * rank), BF16)],
        compiler_params=params(10),
        name="finish",
    )(*in_vmem(*keeps), *receives, store_row, *flat, *lows)


def swap(axis, size):
    def move(value):
        return lax.ppermute(value, axis, [(i, i ^ 1) for i in range(size)])

    return move


def per_device(tokens, gate, down, up, request_index, store_rows):
    count = store_rows.shape[0]
    levels = count // 2
    pairs = levels // 2
    shard = tokens.shape[0]
    own_tokens = shard * count // 2
    along_y = swap("mp", count)
    other_core = swap("sub", 2)
    other_group = swap("groups", lax.axis_size("groups"))
    together = lax.optimization_barrier
    down = jnp.swapaxes(down, 1, 2)

    def along_mp(value, dz, dy=0):
        pairs_of = [(i, 2 * ((i // 2 + dz) % levels) + ((i % 2) ^ dy)) for i in range(count)]
        return lax.ppermute(value, "mp", pairs_of)

    store_row = rows_of_tokens(request_index.reshape(1, -1), store_rows, own_tokens)

    straight = [(dz, 0) for dz in range(levels) if dz != pairs]
    crossing = [(dz, 1) for dz in range(levels) if dz != pairs]
    middle = [(pairs, 0), (pairs, 1)]
    offsets = straight + crossing + middle
    blocks = dict(zip(offsets, split_panels(up, offsets, levels)))

    def move_blocks(chosen):
        for dz, dy in chosen:
            if (dz, dy) != (0, 0):
                blocks[dz, dy] = along_mp(blocks[dz, dy], dz, dy)

    held, mark = hold_gate(gate)
    pair_left, lows, keeps, receives, chunks = {}, [], [], [], []

    def multiply(k, near, far, down, after=None):
        made = base_chunk(near, far, gate, held, pair_left.get(k % pairs, ()), down, k, levels, after)
        pair_left[k % pairs] = made[:2]
        if down is not None:
            lows.append(made[-1])
        if k >= pairs:
            keeps.append(made[0])
            receives.append(other_core(made[1]))

    near = tokens
    for stage in range(levels):
        far = along_y(near)
        after = along_mp(near, 1) if stage < levels - 1 else near
        if stage == 0:
            move_blocks(straight + crossing[:1])
            bound = [store_row, mark]
        else:
            multiply(stage - 1, *chunks[-1], down, mark if stage == 1 else None)
            bound = [lows[-1]]
        if stage == levels - 1:
            first = stack([blocks[offset] for offset in straight + crossing])
            first_x, first_c = other_group(first), other_core(first)
            move_blocks(middle)
        elif stage > 0:
            move_blocks(crossing[stage : stage + 1])
        names = list(blocks)
        near, after, far, moved, bound = together(
            (near, after, far, [blocks[name] for name in names], bound)
        )
        blocks = dict(zip(names, moved))
        if stage == 0:
            store_row, mark = bound
        else:
            lows[-1] = bound[0]
        chunks.append((near, far))
        near = after

    near, far = chunks[-1]
    low_keep, low_send = low_last(near, far, down, lows, levels)
    low_send, second = together((low_send, stack([blocks[offset] for offset in middle])))
    second_x, second_c = other_group(second), other_core(second)
    low = low_own(low_keep, other_core(low_send), store_row)
    low, second_x, near, far = together((add(low, along_y(low)), second_x, near, far))
    parts = [low] + [along_mp(low, j) for j in range(1, levels)]
    multiply(levels - 1, near, far, None)
    panels = [
        (first, second),
        (first_x, second_x),
        (first_c, second_c),
        (other_core(first_x), other_core(second_x)),
    ]
    return finish(keeps, receives, parts, store_row, panels, offsets, levels)


def solution(mesh):
    return jax.shard_map(
        per_device,
        mesh=mesh,
        in_specs=(
            P(("groups", "mp"), "sub"),
            P("sub", "mp"),
            P("mp", "sub", None),
            P("mp", None, None),
            P("groups", None),
            P(),
        ),
        out_specs=P(("groups", "sub"), "mp"),
        check_vma=False,
    )
```

time: 351 us -> 111 us (0.32)
  other arithmetic: 165 us -> 0 us
  local copies, waits for them, and re-layouts: 74.9 us -> 0.01 us
  Pallas kernels: 0 us -> 41.1 us
  matrix products: 38.1 us -> 0 us
  starting transfers between devices: 7.53 us -> 29.4 us
  between operations: 13.3 us -> 0.18 us
  waiting for transfers between devices: 51.8 us -> 40.3 us
    unnamed x1 -> x0, other arithmetic: 157 us -> none
    unnamed x13 -> x8, local copies, waits for them, and re-layouts: 42.4 us -> 0.01 us
    pallas_call x0 -> x13, Pallas kernels: none -> 41.1 us  [the longest x4 25.3 us: base_chunk(): pl.pallas_call(kernel, grid=(HELD,), in_specs=[VMEM] * (len(pair) + 1) +...]
    ppermute x0 -> x27, waiting for transfers between devices: none -> 40.3 us  [the longest x13 32.4 us: along_mp(): return lax.ppermute(value, 'mp', pairs_of)]
    all_to_all x1 -> x0, waiting for transfers between devices: 35.7 us -> none  [per_device(): lax.all_to_all(own_rank, 'mp', split_axis=2, concat_axis=0, tiled=True)]
    dot_general x2 -> x0, matrix products: 31.3 us -> none  [the longest x1 24 us: per_device(): base = jnp.dot(rows_all, gate_matrix, preferred_element_type=jnp.float32)]
    ppermute x0 -> x27, starting transfers between devices: none -> 29.4 us  [the longest x13 18.7 us: along_mp(): return lax.ppermute(value, 'mp', pairs_of)]
    all_to_all x3 -> x0, local copies, waits for them, and re-layouts: 27.1 us -> none  [per_device(): lax.all_to_all(own_rank, 'mp', split_axis=2, concat_axis=0, tiled=True)]
  transfers between devices with their start and end apart: 5 -> 27, of which waited for: 2 -> 11; matrix products, arithmetic and copies ran while one was open for 74% -> 0% of each run, Pallas kernels for 0% -> 33%
where the time goes in v2:
time: 111 us
  Pallas kernels  41.1 us (37%)
  waiting for transfers between devices  40.3 us (36%)
  starting transfers between devices  29.4 us (26%)
    ppermute x13, waiting for transfers between devices, along_mp(): return lax.ppermute(value, 'mp', pairs_of)  32.4 us
    pallas_call x4, Pallas kernels, base_chunk(): pl.pallas_call(kernel, grid=(HELD,), in_specs=[VMEM] * (len(pair) + 1) +...  25.3 us
    ppermute x13, starting transfers between devices, along_mp(): return lax.ppermute(value, 'mp', pairs_of)  18.7 us
    ppermute x14, starting transfers between devices, move(): return lax.ppermute(value, axis, [(i, i ^ 1) for i in range(size)])  10.7 us
    ppermute x14, waiting for transfers between devices, move(): return lax.ppermute(value, axis, [(i, i ^ 1) for i in range(size)])  7.83 us
    pallas_call x1, Pallas kernels, hold_gate(): pl.pallas_call(kernel, in_specs=[ANY], out_specs=[VMEM, VMEM], out_shape=...  7.11 us
    pallas_call x1, Pallas kernels, finish(): pl.pallas_call(kernel, grid=(width // tile,), in_specs=[VMEM] * pairs + [...  4.76 us
  transfers between devices with their start and end apart: 27, of which 11 were waited for; matrix products, arithmetic and copies ran while one was open for 0% of the time, Pallas kernels for 33%

profile of v2, /device:TPU:0, one launch (start us, length us, event | category | flops | bytes accessed | tf_op | source)
XLA Modules:
  0.0 111.0 jit_solution(6870937593775739511)
XLA Ops:
  0.0 3.0 %collective-permute-start = (bf16[64,4096]{1,0:T(8,128)(2,1)}, bf16[64,4096]{1,0:T(8,128)(2,1)S(1)}, u32[]{:S(2)}, u32[]{:S(2)}) collective-permute-start(bf16[64,4096]{1,0:T(8,128)(2,1)} %refs_2_), channel_id=1, source_target_pairs={{0,4},{2,6},{4,8},{6,10},{8,12},{10,14},{12,0},{14,2},{1,5},{3,7},... | collective-permute-start | bytes 1572872 | tf_op jit(solution)/shard_map/ppermute | solution.py:403
  5.9 1.6 %collective-permute-start.2 = (bf16[16,3584]{1,0:T(8,128)(2,1)S(1)}, bf16[16,3584]{1,0:T(8,128)(2,1)S(1)}, u32[]{:S(2)}, u32[]{:S(2)}) collective-permute-start(bf16[16,3584]{1,0:T(8,128)(2,1)S(1)} %get-tuple-element.78), channel_id=1, source_target_pairs={{0,4},{2,6},{4,8},{6,10},{8,12},{10,14},{12,0},{14,2},{1,5},{3,7},... | collective-permute-start | bytes 344072 | tf_op jit(solution)/shard_map/ppermute | solution.py:403
  7.5 2.2 %collective-permute-start.3 = (bf16[16,3584]{1,0:T(8,128)(2,1)S(1)}, bf16[16,3584]{1,0:T(8,128)(2,1)S(1)}, u32[]{:S(2)}, u32[]{:S(2)}) collective-permute-start(bf16[16,3584]{1,0:T(8,128)(2,1)S(1)} %get-tuple-element.79), channel_id=1, source_target_pairs={{0,12},{2,14},{4,0},{6,2},{8,4},{10,6},{12,8},{14,10},{1,13},{3,15... | collective-permute-start | bytes 344072 | tf_op jit(solution)/shard_map/ppermute | solution.py:403
  10.3 7.1 %hold_gate.1 = (bf16[4096,2560]{1,0:T(8,128)(2,1)S(1)}, f32[8,128]{1,0:T(8,128)S(1)}) custom-call(bf16[4096,3584]{1,0:T(8,128)(2,1)} %refs_3_.3), custom_call_target="tpu_custom_call" | custom-call | tf_op jit(solution)/shard_map/hold_gate/pallas_call | solution.py:134
  18.2 2.3 %collective-permute-done.2.refs_1_ = bf16[16,3584]{1,0:T(8,128)(2,1)S(1)} collective-permute-done((bf16[16,3584]{1,0:T(8,128)(2,1)S(1)}, bf16[16,3584]{1,0:T(8,128)(2,1)S(1)}, u32[]{:S(2)}, u32[]{:S(2)}) %collective-permute-start.2) | collective-permute-done | bytes 114720 | tf_op jit(solution)/shard_map/ppermute | solution.py:403
  20.5 1.6 %collective-permute-done.3.refs_2_ = bf16[16,3584]{1,0:T(8,128)(2,1)S(1)} collective-permute-done((bf16[16,3584]{1,0:T(8,128)(2,1)S(1)}, bf16[16,3584]{1,0:T(8,128)(2,1)S(1)}, u32[]{:S(2)}, u32[]{:S(2)}) %collective-permute-start.3) | collective-permute-done | bytes 114720 | tf_op jit(solution)/shard_map/ppermute | solution.py:403
  22.1 1.6 %collective-permute-start.6 = (bf16[64,4096]{1,0:T(8,128)(2,1)S(1)}, bf16[64,4096]{1,0:T(8,128)(2,1)S(1)}, u32[]{:S(2)}, u32[]{:S(2)}) collective-permute-start(bf16[64,4096]{1,0:T(8,128)(2,1)S(1)} %collective-permute-done.refs_2_), channel_id=1, source_target_pairs={{0,2},{2,0},{4,6},{6,4},{8,10},{10,8},{12,14},{14,12},{1,3},{3,1},... | collective-permute-start | bytes 1572872 | tf_op jit(solution)/shard_map/ppermute | solution.py:384
  24.9 6.4 %base_chunk.4 = (f32[128,3584]{1,0:T(8,128)S(1)}, bf16[128,3584]{1,0:T(8,128)(2,1)S(1)}, f32[128,64]{1,0:T(8,128)S(1)}) custom-call(bf16[4096,2560]{1,0:T(8,128)(2,1)S(1)} %get-tuple-element.76.refs_0_.refs_2_, bf16[4096,3584]{1,0:T(8,128)(2,1)} %refs_3_.3, bf16[64,4096]{1,0:T(8,128)(2,1)S(1)} %copy-done.1, ...), custom_call_target="tpu_custom_call" | custom-call | tf_op jit(solution)/shard_map/base_chunk/pallas_call | solution.py:234
  31.4 10.0 %collective-permute-done.7.refs_4_ = bf16[16,3584]{1,0:T(8,128)(2,1)S(1)} collective-permute-done((bf16[16,3584]{1,0:T(8,128)(2,1)S(1)}, bf16[16,3584]{1,0:T(8,128)(2,1)S(1)}, u32[]{:S(2)}, u32[]{:S(2)}) %collective-permute-start.7) | collective-permute-done | bytes 114720 | tf_op jit(solution)/shard_map/ppermute | solution.py:403
  42.9 3.8 %collective-permute-start.10 = (bf16[16,3584]{1,0:T(8,128)(2,1)S(1)}, bf16[16,3584]{1,0:T(8,128)(2,1)S(1)}, u32[]{:S(2)}, u32[]{:S(2)}) collective-permute-start(bf16[16,3584]{1,0:T(8,128)(2,1)S(1)} %get-tuple-element.107), channel_id=1, source_target_pairs={{0,14},{2,12},{4,2},{6,0},{8,6},{10,4},{12,10},{14,8},{1,15},{3,13... | collective-permute-start | bytes 344072 | tf_op jit(solution)/shard_map/ppermute | solution.py:403
  46.7 6.5 %base_chunk.5 = (f32[128,3584]{1,0:T(8,128)S(1)}, bf16[128,3584]{1,0:T(8,128)(2,1)S(1)}, f32[128,64]{1,0:T(8,128)S(1)}) custom-call(bf16[4096,2560]{1,0:T(8,128)(2,1)S(1)} %get-tuple-element.76.refs_0_.refs_2_, bf16[4096,3584]{1,0:T(8,128)(2,1)} %refs_3_.3, bf16[64,4096]{1,0:T(8,128)(2,1)S(1)} %collective-permute-done.refs_2_, ...), custom_call_target="tpu_custom_call" | custom-call | tf_op jit(solution)/shard_map/base_chunk/pallas_call | solution.py:234
  53.2 5.3 %collective-permute-done.10.refs_5_ = bf16[16,3584]{1,0:T(8,128)(2,1)S(1)} collective-permute-done((bf16[16,3584]{1,0:T(8,128)(2,1)S(1)}, bf16[16,3584]{1,0:T(8,128)(2,1)S(1)}, u32[]{:S(2)}, u32[]{:S(2)}) %collective-permute-start.10) | collective-permute-done | bytes 114720 | tf_op jit(solution)/shard_map/ppermute | solution.py:403
  60.5 1.6 %collective-permute-start.19 = (bf16[6,16,3584]{2,1,0:T(8,128)(2,1)S(1)}, bf16[6,16,3584]{2,1,0:T(8,128)(2,1)S(1)}, u32[]{:S(2)}, u32[]{:S(2)}) collective-permute-start(bf16[6,16,3584]{2,1,0:T(8,128)(2,1)S(1)} %stack.3.refs_5_), channel_id=1, source_target_pairs={{0,16},{16,0},{1,17},{17,1},{2,18},{18,2},{3,19},{19,3},{4,20},{20... | collective-permute-start | bytes 2064392 | tf_op jit(solution)/shard_map/ppermute | solution.py:384
  62.1 1.8 %collective-permute-start.12 = (bf16[16,3584]{1,0:T(8,128)(2,1)S(1)}, bf16[16,3584]{1,0:T(8,128)(2,1)S(1)}, u32[]{:S(2)}, u32[]{:S(2)}) collective-permute-start(bf16[16,3584]{1,0:T(8,128)(2,1)S(1)} %get-tuple-element.125), channel_id=1, source_target_pairs={{0,8},{2,10},{4,12},{6,14},{8,0},{10,2},{12,4},{14,6},{1,9},{3,11}... | collective-permute-start | bytes 344072 | tf_op jit(solution)/shard_map/ppermute | solution.py:403
  65.3 6.5 %base_chunk.6 = (f32[128,3584]{1,0:T(8,128)S(1)}, bf16[128,3584]{1,0:T(8,128)(2,1)S(1)}, f32[128,64]{1,0:T(8,128)S(1)}) custom-call(f32[128,3584]{1,0:T(8,128)S(1)} %get-tuple-element.89.refs_0_, bf16[128,3584]{1,0:T(8,128)(2,1)S(1)} %get-tuple-element.90.refs_1_, ...), custom_call_target="tpu_custom_call", output_to_operand_aliasing={{0}: (0, {}), {1}: (1, {})} | custom-call | tf_op jit(solution)/shard_map/base_chunk/pallas_call | solution.py:234
  72.7 1.6 %collective-permute-start.16 = (bf16[2,16,3584]{2,1,0:T(8,128)(2,1)S(1)}, bf16[2,16,3584]{2,1,0:T(8,128)(2,1)S(1)}, u32[]{:S(2)}, u32[]{:S(2)}) collective-permute-start(bf16[2,16,3584]{2,1,0:T(8,128)(2,1)S(1)} %stack.2.refs_6_), channel_id=1, source_target_pairs={{0,16},{16,0},{1,17},{17,1},{2,18},{18,2},{3,19},{19,3},{4,20},{20... | collective-permute-start | bytes 688136 | tf_op jit(solution)/shard_map/ppermute | solution.py:384
  76.5 3.6 %collective-permute-done.15.two_ref = bf16[256,64]{1,0:T(8,128)(2,1)S(1)} collective-permute-done((bf16[256,64]{1,0:T(8,128)(2,1)S(1)}, bf16[256,64]{1,0:T(8,128)(2,1)S(1)}, u32[]{:S(2)}, u32[]{:S(2)}) %collective-permute-start.15) | collective-permute-done | bytes 32800 | tf_op jit(solution)/shard_map/ppermute | solution.py:384
  80.1 6.0 %base_chunk.7 = (f32[128,3584]{1,0:T(8,128)S(1)}, bf16[128,3584]{1,0:T(8,128)(2,1)S(1)}) custom-call(f32[128,3584]{1,0:T(8,128)S(1)} %get-tuple-element.116.refs_0_, bf16[128,3584]{1,0:T(8,128)(2,1)S(1)} %get-tuple-element.117.refs_1_, bf16[4096,2560]{1,0:T(8,128)(2,1)S(1)} %get-tuple-element.76.refs_0_.refs_2_, ...), custom_call_target="tpu_custom_call", output_to_operand_aliasing={{0}: (0, {}), {1}: (1, {})} | custom-call | tf_op jit(solution)/shard_map/base_chunk/pallas_call | solution.py:234
  87.2 2.8 %collective-permute-done.21.refs_10_ = bf16[2,16,3584]{2,1,0:T(8,128)(2,1)S(1)} collective-permute-done((bf16[2,16,3584]{2,1,0:T(8,128)(2,1)S(1)}, bf16[2,16,3584]{2,1,0:T(8,128)(2,1)S(1)}, u32[]{:S(2)}, u32[]{:S(2)}) %collective-permute-start.21) | collective-permute-done | bytes 229408 | tf_op jit(solution)/shard_map/ppermute | solution.py:384
  91.2 3.0 %collective-permute-done.26.refs_16_ = bf16[256,64]{1,0:T(8,128)(2,1)S(1)} collective-permute-done((bf16[256,64]{1,0:T(8,128)(2,1)S(1)}, bf16[256,64]{1,0:T(8,128)(2,1)S(1)}, u32[]{:S(2)}, u32[]{:S(2)}) %collective-permute-start.26) | collective-permute-done | bytes 32800 | tf_op jit(solution)/shard_map/ppermute | solution.py:403
  94.2 1.6 %collective-permute-start.25 = (bf16[256,64]{1,0:T(8,128)(2,1)S(1)}, bf16[256,64]{1,0:T(8,128)(2,1)S(1)}, u32[]{:S(2)}, u32[]{:S(2)}) collective-permute-start(bf16[256,64]{1,0:T(8,128)(2,1)S(1)} %add.1.refs_13_), channel_id=1, source_target_pairs={{0,8},{2,10},{4,12},{6,14},{8,0},{10,2},{12,4},{14,6},{1,9},{3,11}... | collective-permute-start | bytes 98312 | tf_op jit(solution)/shard_map/ppermute | solution.py:403
  95.9 4.2 %collective-permute-done.25.refs_15_ = bf16[256,64]{1,0:T(8,128)(2,1)S(1)} collective-permute-done((bf16[256,64]{1,0:T(8,128)(2,1)S(1)}, bf16[256,64]{1,0:T(8,128)(2,1)S(1)}, u32[]{:S(2)}, u32[]{:S(2)}) %collective-permute-start.25) | collective-permute-done | bytes 32800 | tf_op jit(solution)/shard_map/ppermute | solution.py:403
  100.2 6.0 %collective-permute-done.24.refs_14_ = bf16[256,64]{1,0:T(8,128)(2,1)S(1)} collective-permute-done((bf16[256,64]{1,0:T(8,128)(2,1)S(1)}, bf16[256,64]{1,0:T(8,128)(2,1)S(1)}, u32[]{:S(2)}, u32[]{:S(2)}) %collective-permute-start.24) | collective-permute-done | bytes 32800 | tf_op jit(solution)/shard_map/ppermute | solution.py:403
  106.2 4.8 %finish.1 = bf16[256,3584]{1,0:T(8,128)(2,1)} custom-call(f32[128,3584]{1,0:T(8,128)S(1)} %get-tuple-element.115.refs_0_, f32[128,3584]{1,0:T(8,128)S(1)} %get-tuple-element.142.refs_1_, bf16[128,3584]{1,0:T(8,128)(2,1)S(1)} %collective-permute-done.17.refs_2_, bf16[128,3584]{1,0:T(8,128)(2,1)S(1)} %collective-permute-done.18.refs_3_, ...), custom_call_target="tpu_custom_call" | custom-call | tf_op jit(solution)/shard_map/finish/pallas_call | solution.py:366
  (51 shorter events, 16.0 us)
Async XLA Ops:
  0.0 22.1 %collective-permute-start = (bf16[64,4096]{1,0:T(8,128)(2,1)}, bf16[64,4096]{1,0:T(8,128)(2,1)S(1)}, u32[]{:S(2)}, u32[]{:S(2)}) collective-permute-start(bf16[64,4096]{1,0:T(8,128)(2,1)} %refs_2_), channel_id=1, source_target_pairs={{0,4},{2,6},{4,8},{6,10},{8,12},{10,14},{12,0},{14,2},{1,5},{3,7},... | collective-permute-start | bytes 1572872 | tf_op jit(solution)/shard_map/ppermute | solution.py:403
  3.0 19.1 %collective-permute-start.1 = (bf16[64,4096]{1,0:T(8,128)(2,1)}, bf16[64,4096]{1,0:T(8,128)(2,1)S(1)}, u32[]{:S(2)}, u32[]{:S(2)}) collective-permute-start(bf16[64,4096]{1,0:T(8,128)(2,1)} %refs_2_), channel_id=1, source_target_pairs={{0,2},{2,0},{4,6},{6,4},{8,10},{10,8},{12,14},{14,12},{1,3},{3,1},... | collective-permute-start | bytes 1572872 | tf_op jit(solution)/shard_map/ppermute | solution.py:384
  5.9 14.6 %collective-permute-start.2 = (bf16[16,3584]{1,0:T(8,128)(2,1)S(1)}, bf16[16,3584]{1,0:T(8,128)(2,1)S(1)}, u32[]{:S(2)}, u32[]{:S(2)}) collective-permute-start(bf16[16,3584]{1,0:T(8,128)(2,1)S(1)} %get-tuple-element.78), channel_id=1, source_target_pairs={{0,4},{2,6},{4,8},{6,10},{8,12},{10,14},{12,0},{14,2},{1,5},{3,7},... | collective-permute-start | bytes 344072 | tf_op jit(solution)/shard_map/ppermute | solution.py:403
  7.5 14.6 %collective-permute-start.3 = (bf16[16,3584]{1,0:T(8,128)(2,1)S(1)}, bf16[16,3584]{1,0:T(8,128)(2,1)S(1)}, u32[]{:S(2)}, u32[]{:S(2)}) collective-permute-start(bf16[16,3584]{1,0:T(8,128)(2,1)S(1)} %get-tuple-element.79), channel_id=1, source_target_pairs={{0,12},{2,14},{4,0},{6,2},{8,4},{10,6},{12,8},{14,10},{1,13},{3,15... | collective-permute-start | bytes 344072 | tf_op jit(solution)/shard_map/ppermute | solution.py:403
  9.8 12.3 %collective-permute-start.4 = (bf16[16,3584]{1,0:T(8,128)(2,1)S(1)}, bf16[16,3584]{1,0:T(8,128)(2,1)S(1)}, u32[]{:S(2)}, u32[]{:S(2)}) collective-permute-start(bf16[16,3584]{1,0:T(8,128)(2,1)S(1)} %get-tuple-element.80), channel_id=1, source_target_pairs={{0,2},{2,0},{4,6},{6,4},{8,10},{10,8},{12,14},{14,12},{1,3},{3,1},... | collective-permute-start | bytes 344072 | tf_op jit(solution)/shard_map/ppermute | solution.py:403
  22.1 19.3 %collective-permute-start.6 = (bf16[64,4096]{1,0:T(8,128)(2,1)S(1)}, bf16[64,4096]{1,0:T(8,128)(2,1)S(1)}, u32[]{:S(2)}, u32[]{:S(2)}) collective-permute-start(bf16[64,4096]{1,0:T(8,128)(2,1)S(1)} %collective-permute-done.refs_2_), channel_id=1, source_target_pairs={{0,2},{2,0},{4,6},{6,4},{8,10},{10,8},{12,14},{14,12},{1,3},{3,1},... | collective-permute-start | bytes 1572872 | tf_op jit(solution)/shard_map/ppermute | solution.py:384
  23.7 17.7 %collective-permute-start.5 = (bf16[64,4096]{1,0:T(8,128)(2,1)S(1)}, bf16[64,4096]{1,0:T(8,128)(2,1)S(1)}, u32[]{:S(2)}, u32[]{:S(2)}) collective-permute-start(bf16[64,4096]{1,0:T(8,128)(2,1)S(1)} %collective-permute-done.refs_2_), channel_id=1, source_target_pairs={{0,4},{2,6},{4,8},{6,10},{8,12},{10,14},{12,0},{14,2},{1,5},{3,7},... | collective-permute-start | bytes 1572872 | tf_op jit(solution)/shard_map/ppermute | solution.py:403
  24.3 17.2 %collective-permute-start.7 = (bf16[16,3584]{1,0:T(8,128)(2,1)S(1)}, bf16[16,3584]{1,0:T(8,128)(2,1)S(1)}, u32[]{:S(2)}, u32[]{:S(2)}) collective-permute-start(bf16[16,3584]{1,0:T(8,128)(2,1)S(1)} %get-tuple-element.96), channel_id=1, source_target_pairs={{0,6},{2,4},{4,10},{6,8},{8,14},{10,12},{12,2},{14,0},{1,7},{3,5},... | collective-permute-start | bytes 344072 | tf_op jit(solution)/shard_map/ppermute | solution.py:403
  41.4 17.0 %collective-permute-start.9 = (bf16[64,4096]{1,0:T(8,128)(2,1)S(1)}, bf16[64,4096]{1,0:T(8,128)(2,1)S(1)}, u32[]{:S(2)}, u32[]{:S(2)}) collective-permute-start(bf16[64,4096]{1,0:T(8,128)(2,1)S(1)} %collective-permute-done.5.refs_4_), channel_id=1, source_target_pairs={{0,2},{2,0},{4,6},{6,4},{8,10},{10,8},{12,14},{14,12},{1,3},{3,1},... | collective-permute-start | bytes 1572872 | tf_op jit(solution)/shard_map/ppermute | solution.py:384
  42.9 15.5 %collective-permute-start.8 = (bf16[64,4096]{1,0:T(8,128)(2,1)S(1)}, bf16[64,4096]{1,0:T(8,128)(2,1)S(1)}, u32[]{:S(2)}, u32[]{:S(2)}) collective-permute-start(bf16[64,4096]{1,0:T(8,128)(2,1)S(1)} %collective-permute-done.5.refs_4_), channel_id=1, source_target_pairs={{0,4},{2,6},{4,8},{6,10},{8,12},{10,14},{12,0},{14,2},{1,5},{3,7},... | collective-permute-start | bytes 1572872 | tf_op jit(solution)/shard_map/ppermute | solution.py:403
  42.9 15.5 %collective-permute-start.10 = (bf16[16,3584]{1,0:T(8,128)(2,1)S(1)}, bf16[16,3584]{1,0:T(8,128)(2,1)S(1)}, u32[]{:S(2)}, u32[]{:S(2)}) collective-permute-start(bf16[16,3584]{1,0:T(8,128)(2,1)S(1)} %get-tuple-element.107), channel_id=1, source_target_pairs={{0,14},{2,12},{4,2},{6,0},{8,6},{10,4},{12,10},{14,8},{1,15},{3,13... | collective-permute-start | bytes 344072 | tf_op jit(solution)/shard_map/ppermute | solution.py:403
  58.5 13.4 %collective-permute-start.11 = (bf16[64,4096]{1,0:T(8,128)(2,1)S(1)}, bf16[64,4096]{1,0:T(8,128)(2,1)S(1)}, u32[]{:S(2)}, u32[]{:S(2)}) collective-permute-start(bf16[64,4096]{1,0:T(8,128)(2,1)S(1)} %collective-permute-done.8.refs_0_.refs_4_), channel_id=1, source_target_pairs={{0,2},{2,0},{4,6},{6,4},{8,10},{10,8},{12,14},{14,12},{1,3},{3,1},... | collective-permute-start | bytes 1572872 | tf_op jit(solution)/shard_map/ppermute | solution.py:384
  60.5 25.7 %collective-permute-start.19 = (bf16[6,16,3584]{2,1,0:T(8,128)(2,1)S(1)}, bf16[6,16,3584]{2,1,0:T(8,128)(2,1)S(1)}, u32[]{:S(2)}, u32[]{:S(2)}) collective-permute-start(bf16[6,16,3584]{2,1,0:T(8,128)(2,1)S(1)} %stack.3.refs_5_), channel_id=1, source_target_pairs={{0,16},{16,0},{1,17},{17,1},{2,18},{18,2},{3,19},{19,3},{4,20},{20... | collective-permute-start | bytes 2064392 | tf_op jit(solution)/shard_map/ppermute | solution.py:384
  62.1 9.7 %collective-permute-start.12 = (bf16[16,3584]{1,0:T(8,128)(2,1)S(1)}, bf16[16,3584]{1,0:T(8,128)(2,1)S(1)}, u32[]{:S(2)}, u32[]{:S(2)}) collective-permute-start(bf16[16,3584]{1,0:T(8,128)(2,1)S(1)} %get-tuple-element.125), channel_id=1, source_target_pairs={{0,8},{2,10},{4,12},{6,14},{8,0},{10,2},{12,4},{14,6},{1,9},{3,11}... | collective-permute-start | bytes 344072 | tf_op jit(solution)/shard_map/ppermute | solution.py:403
  63.9 7.9 %collective-permute-start.13 = (bf16[16,3584]{1,0:T(8,128)(2,1)S(1)}, bf16[16,3584]{1,0:T(8,128)(2,1)S(1)}, u32[]{:S(2)}, u32[]{:S(2)}) collective-permute-start(bf16[16,3584]{1,0:T(8,128)(2,1)S(1)} %get-tuple-element.126), channel_id=1, source_target_pairs={{0,10},{2,8},{4,14},{6,12},{8,2},{10,0},{12,6},{14,4},{1,11},{3,9}... | collective-permute-start | bytes 344072 | tf_op jit(solution)/shard_map/ppermute | solution.py:403
  72.7 7.4 %collective-permute-start.16 = (bf16[2,16,3584]{2,1,0:T(8,128)(2,1)S(1)}, bf16[2,16,3584]{2,1,0:T(8,128)(2,1)S(1)}, u32[]{:S(2)}, u32[]{:S(2)}) collective-permute-start(bf16[2,16,3584]{2,1,0:T(8,128)(2,1)S(1)} %stack.2.refs_6_), channel_id=1, source_target_pairs={{0,16},{16,0},{1,17},{17,1},{2,18},{18,2},{3,19},{19,3},{4,20},{20... | collective-permute-start | bytes 688136 | tf_op jit(solution)/shard_map/ppermute | solution.py:384
  75.7 4.3 %collective-permute-start.15 = (bf16[256,64]{1,0:T(8,128)(2,1)S(1)}, bf16[256,64]{1,0:T(8,128)(2,1)S(1)}, u32[]{:S(2)}, u32[]{:S(2)}) collective-permute-start(bf16[256,64]{1,0:T(8,128)(2,1)S(1)} %low_own.1.one_ref), channel_id=1, source_target_pairs={{0,2},{2,0},{4,6},{6,4},{8,10},{10,8},{12,14},{14,12},{1,3},{3,1},... | collective-permute-start | bytes 98312 | tf_op jit(solution)/shard_map/ppermute | solution.py:384
  75.9 10.8 %collective-permute-start.20 = (bf16[6,16,3584]{2,1,0:T(8,128)(2,1)S(1)}, bf16[6,16,3584]{2,1,0:T(8,128)(2,1)S(1)}, u32[]{:S(2)}, u32[]{:S(2)}) collective-permute-start(bf16[6,16,3584]{2,1,0:T(8,128)(2,1)S(1)} %stack.3.refs_5_), channel_id=1, source_target_pairs={{0,1},{1,0},{2,3},{3,2},{4,5},{5,4},{6,7},{7,6},{8,9},{9,8},{10,11... | collective-permute-start | bytes 2064392 | tf_op jit(solution)/shard_map/ppermute | solution.py:384
  76.0 30.1 %collective-permute-start.17 = (bf16[128,3584]{1,0:T(8,128)(2,1)S(1)}, bf16[128,3584]{1,0:T(8,128)(2,1)S(1)}, u32[]{:S(2)}, u32[]{:S(2)}) collective-permute-start(bf16[128,3584]{1,0:T(8,128)(2,1)S(1)} %get-tuple-element.143), channel_id=1, source_target_pairs={{0,1},{1,0},{2,3},{3,2},{4,5},{5,4},{6,7},{7,6},{8,9},{9,8},{10,11... | collective-permute-start | bytes 2752520 | tf_op jit(solution)/shard_map/ppermute | solution.py:384
  86.1 20.1 %collective-permute-start.18 = (bf16[128,3584]{1,0:T(8,128)(2,1)S(1)}, bf16[128,3584]{1,0:T(8,128)(2,1)S(1)}, u32[]{:S(2)}, u32[]{:S(2)}) collective-permute-start(bf16[128,3584]{1,0:T(8,128)(2,1)S(1)} %get-tuple-element.144), channel_id=1, source_target_pairs={{0,1},{1,0},{2,3},{3,2},{4,5},{5,4},{6,7},{7,6},{8,9},{9,8},{10,11... | collective-permute-start | bytes 2752520 | tf_op jit(solution)/shard_map/ppermute | solution.py:384
  86.2 20.0 %collective-permute-start.22 = (bf16[6,16,3584]{2,1,0:T(8,128)(2,1)S(1)}, bf16[6,16,3584]{2,1,0:T(8,128)(2,1)S(1)}, u32[]{:S(2)}, u32[]{:S(2)}) collective-permute-start(bf16[6,16,3584]{2,1,0:T(8,128)(2,1)S(1)} %collective-permute-done.19.refs_7_), channel_id=1, source_target_pairs={{0,1},{1,0},{2,3},{3,2},{4,5},{5,4},{6,7},{7,6},{8,9},{9,8},{10,11... | collective-permute-start | bytes 2064392 | tf_op jit(solution)/shard_map/ppermute | solution.py:384
  86.8 19.4 %collective-permute-start.23 = (bf16[2,16,3584]{2,1,0:T(8,128)(2,1)S(1)}, bf16[2,16,3584]{2,1,0:T(8,128)(2,1)S(1)}, u32[]{:S(2)}, u32[]{:S(2)}) collective-permute-start(bf16[2,16,3584]{2,1,0:T(8,128)(2,1)S(1)} %collective-permute-done.16.refs_8_), channel_id=1, source_target_pairs={{0,1},{1,0},{2,3},{3,2},{4,5},{5,4},{6,7},{7,6},{8,9},{9,8},{10,11... | collective-permute-start | bytes 688136 | tf_op jit(solution)/shard_map/ppermute | solution.py:384
  94.2 5.9 %collective-permute-start.25 = (bf16[256,64]{1,0:T(8,128)(2,1)S(1)}, bf16[256,64]{1,0:T(8,128)(2,1)S(1)}, u32[]{:S(2)}, u32[]{:S(2)}) collective-permute-start(bf16[256,64]{1,0:T(8,128)(2,1)S(1)} %add.1.refs_13_), channel_id=1, source_target_pairs={{0,8},{2,10},{4,12},{6,14},{8,0},{10,2},{12,4},{14,6},{1,9},{3,11}... | collective-permute-start | bytes 98312 | tf_op jit(solution)/shard_map/ppermute | solution.py:403
  100.1 6.1 %collective-permute-start.24 = (bf16[256,64]{1,0:T(8,128)(2,1)S(1)}, bf16[256,64]{1,0:T(8,128)(2,1)S(1)}, u32[]{:S(2)}, u32[]{:S(2)}) collective-permute-start(bf16[256,64]{1,0:T(8,128)(2,1)S(1)} %add.1.refs_13_), channel_id=1, source_target_pairs={{0,4},{2,6},{4,8},{6,10},{8,12},{10,14},{12,0},{14,2},{1,5},{3,7},... | collective-permute-start | bytes 98312 | tf_op jit(solution)/shard_map/ppermute | solution.py:403
  (7 other events, 54.7 us)

commit v3 on v2

--- a/solution.py
+++ b/solution.py
@@ -159,7 +159,7 @@
     rows_ref[pl.ds(pl.multiple_of((1 - y) * shard, shard), shard), :] = far_ref[...]
 
 
-def base_chunk(near, far, gate, held, pair, down, step, levels, after=None):
+def base_chunk(near, far, gate, held, pair, down, step, levels, after=None, tiles="all"):
     shard, depth = near.shape
     width = gate.shape[1]
     tile = width // PARTS
@@ -201,8 +201,9 @@
 
         @pl.when(at == 0)
         def _():
-            fetch(0).start()
-            fetch(1).start()
+            if tiles != "held":
+                fetch(0).start()
+                fetch(1).start()
             load_rows(near_ref, far_ref, rows_ref)
             if down is not None:
                 out_refs[-1][...] = lax.dot_general(
@@ -212,28 +213,32 @@
                     preferred_element_type=F32,
                 )
 
-        columns = pl.ds(pl.multiple_of(at * tile, tile), tile)
-        put(
-            at * tile,
-            tile,
-            jnp.dot(rows_ref[...], held_ref[:, columns], preferred_element_type=F32),
-        )
-
-        @pl.when((at > 0) & (at <= pieces))
-        def _():
-            fetch(at - 1).wait()
-            total = jnp.dot(
-                rows_ref[...], piece_ref[lax.rem(at - 1, 2)], preferred_element_type=F32
+        if tiles != "streamed":
+            columns = pl.ds(pl.multiple_of(at * tile, tile), tile)
+            put(
+                at * tile,
+                tile,
+                jnp.dot(rows_ref[...], held_ref[:, columns], preferred_element_type=F32),
             )
-            put(HELD * tile + (at - 1) * piece, piece, total)
-
-            @pl.when(at + 1 < pieces)
+
+        if tiles != "held":
+            turn = at if tiles == "streamed" else at - 1
+
+            @pl.when((turn >= 0) & (turn < pieces))
             def _():
-                fetch(at + 1).start()
-
-    return pl.pallas_call(
-        kernel,
-        grid=(HELD,),
+                fetch(turn).wait()
+                total = jnp.dot(
+                    rows_ref[...], piece_ref[lax.rem(turn, 2)], preferred_element_type=F32
+                )
+                put(HELD * tile + turn * piece, piece, total)
+
+                @pl.when(turn + 2 < pieces)
+                def _():
+                    fetch(turn + 2).start()
+
+    return pl.pallas_call(
+        kernel,
+        grid=(pieces if tiles == "streamed" else HELD,),
         in_specs=[VMEM] * (len(pair) + 1) + [ANY] + [VMEM] * (len(inputs) - len(pair) - 2),
         out_specs=[VMEM] * len(outputs),
         out_shape=outputs,
@@ -317,7 +322,7 @@
     quarter = rank // 4
     parts = len(panels[0])
     blocks = len(offsets)
-    tile = 512 if width % 512 == 0 else 256
+    tile = width // 2
     flat = [array for group in panels for array in group]
 
     def kernel(*refs):
@@ -374,7 +379,7 @@
         out_specs=pl.BlockSpec((total_rows, tile), column),
         out_shape=jax.ShapeDtypeStruct((total_rows, width), BF16),
         scratch_shapes=[pltpu.VMEM((total_rows, blocks * rank), BF16)],
-        compiler_params=params(10),
+        compiler_params=params(16),
         name="finish",
     )(*in_vmem(*keeps), *receives, store_row, *flat, *lows)
 
@@ -404,10 +409,13 @@
 
     store_row = rows_of_tokens(request_index.reshape(1, -1), store_rows, own_tokens)
 
-    straight = [(dz, 0) for dz in range(levels) if dz != pairs]
-    crossing = [(dz, 1) for dz in range(levels) if dz != pairs]
-    middle = [(pairs, 0), (pairs, 1)]
-    offsets = straight + crossing + middle
+    early = [(1, 0), (0, 1)]
+    crossing = [(dz, 1) for dz in range(1, levels) if dz != pairs]
+    beside_last = [(dz, 0) for dz in range(2, levels)]
+    late = [(pairs, 1)]
+    first_offsets = [(0, 0)] + early + crossing
+    second_offsets = beside_last + late
+    offsets = first_offsets + second_offsets
     blocks = dict(zip(offsets, split_panels(up, offsets, levels)))
 
     def move_blocks(chosen):
@@ -416,33 +424,30 @@
                 blocks[dz, dy] = along_mp(blocks[dz, dy], dz, dy)
 
     held, mark = hold_gate(gate)
-    pair_left, lows, keeps, receives, chunks = {}, [], [], [], []
-
-    def multiply(k, near, far, down, after=None):
-        made = base_chunk(near, far, gate, held, pair_left.get(k % pairs, ()), down, k, levels, after)
+    pair_left, lows, chunks = {}, [], []
+
+    def multiply(k, near, far, down, after=None, tiles="all"):
+        pair = pair_left.get(k % pairs, ())
+        made = base_chunk(near, far, gate, held, pair, down, k, levels, after, tiles)
         pair_left[k % pairs] = made[:2]
         if down is not None:
             lows.append(made[-1])
-        if k >= pairs:
-            keeps.append(made[0])
-            receives.append(other_core(made[1]))
 
     near = tokens
     for stage in range(levels):
         far = along_y(near)
         after = along_mp(near, 1) if stage < levels - 1 else near
         if stage == 0:
-            move_blocks(straight + crossing[:1])
+            move_blocks(early)
             bound = [store_row, mark]
         else:
             multiply(stage - 1, *chunks[-1], down, mark if stage == 1 else None)
             bound = [lows[-1]]
         if stage == levels - 1:
-            first = stack([blocks[offset] for offset in straight + crossing])
             first_x, first_c = other_group(first), other_core(first)
-            move_blocks(middle)
+            move_blocks(beside_last)
         elif stage > 0:
-            move_blocks(crossing[stage : stage + 1])
+            move_blocks(crossing[stage - 1 : stage])
         names = list(blocks)
         near, after, far, moved, bound = together(
             (near, after, far, [blocks[name] for name in names], bound)
@@ -452,22 +457,45 @@
             store_row, mark = bound
         else:
             lows[-1] = bound[0]
+        if stage == levels - 2:
+            first = stack([blocks[offset] for offset in first_offsets])
         chunks.append((near, far))
         near = after
 
     near, far = chunks[-1]
+    last = levels - 1
+    move_blocks(late)
     low_keep, low_send = low_last(near, far, down, lows, levels)
-    low_send, second = together((low_send, stack([blocks[offset] for offset in middle])))
+    low = low_own(low_keep, other_core(low_send), store_row)
+
+    crossed = along_y(low)
+    multiply(last, near, far, None, tiles="held")
+    moved = [blocks[offset] for offset in second_offsets]
+    low, crossed, pair_left[last % pairs], moved, first, first_x, first_c = together(
+        (low, crossed, pair_left[last % pairs], moved, first, first_x, first_c)
+    )
+    first_xc = other_core(first_x)
+    second = stack(moved)
     second_x, second_c = other_group(second), other_core(second)
-    low = low_own(low_keep, other_core(low_send), store_row)
-    low, second_x, near, far = together((add(low, along_y(low)), second_x, near, far))
-    parts = [low] + [along_mp(low, j) for j in range(1, levels)]
-    multiply(levels - 1, near, far, None)
+    low = add(low, crossed)
+    bit = 1
+    while bit < levels:
+        crossed = lax.ppermute(low, "mp", [(i, i ^ (2 * bit)) for i in range(count)])
+        if bit == 1:
+            multiply(last, near, far, None, tiles="streamed")
+            low, crossed, pair_left[last % pairs], second_x = together(
+                (low, crossed, pair_left[last % pairs], second_x)
+            )
+            receives = [other_core(pair_left[k][1]) for k in range(pairs)]
+        low = add(low, crossed)
+        bit *= 2
+    keeps = [pair_left[k][0] for k in range(pairs)]
+    parts = [low]
     panels = [
         (first, second),
         (first_x, second_x),
         (first_c, second_c),
-        (other_core(first_x), other_core(second_x)),
+        (first_xc, other_core(second_x)),
     ]
     return finish(keeps, receives, parts, store_row, panels, offsets, levels)
 

time: 111 us -> 96.7 us (0.87)
  waiting for transfers between devices: 40.3 us -> 24 us
  Pallas kernels: 41.1 us -> 42.4 us
    ppermute x13 -> x10, waiting for transfers between devices: 32.4 us -> 15.7 us  [along_mp(): return lax.ppermute(value, 'mp', pairs_of)]
    ppermute x0 -> x2, starting transfers between devices: none -> 4.64 us  [per_device(): crossed = lax.ppermute(low, 'mp', [(i, i ^ 2 * bit) for i in range(count)])]
    ppermute x13 -> x10, starting transfers between devices: 18.7 us -> 15.4 us  [along_mp(): return lax.ppermute(value, 'mp', pairs_of)]
    ppermute x0 -> x2, waiting for transfers between devices: none -> 3.19 us  [per_device(): crossed = lax.ppermute(low, 'mp', [(i, i ^ 2 * bit) for i in range(count)])]
    pallas_call x4 -> x5, Pallas kernels: 25.3 us -> 28.4 us  [base_chunk(): pl.pallas_call(kernel, grid=(pieces if tiles == 'streamed' else HELD,), i...]
    ppermute x14, waiting for transfers between devices: 7.83 us -> 5.11 us  [move(): return lax.ppermute(value, axis, [(i, i ^ 1) for i in range(size)])]
    pallas_call x1, Pallas kernels: 4.76 us -> 2.98 us  [finish(): pl.pallas_call(kernel, grid=(width // tile,), in_specs=[VMEM] * pairs + [...]
  transfers between devices with their start and end apart: 27 -> 26, of which waited for: 11 -> 11; matrix products, arithmetic and copies ran while one was open for 0% -> 0% of each run, Pallas kernels for 33% -> 40%
where the time goes in v3:
time: 96.7 us; the launch traced here: 96.3 us
  Pallas kernels  42.4 us (44%)
  starting transfers between devices  29.6 us (31%)
  waiting for transfers between devices  24 us (25%)
    pallas_call x5, Pallas kernels, base_chunk(): pl.pallas_call(kernel, grid=(pieces if tiles == 'streamed' else HELD,), i...  28.4 us
    ppermute x10, waiting for transfers between devices, along_mp(): return lax.ppermute(value, 'mp', pairs_of)  15.7 us
    ppermute x10, starting transfers between devices, along_mp(): return lax.ppermute(value, 'mp', pairs_of)  15.4 us
    ppermute x14, starting transfers between devices, move(): return lax.ppermute(value, axis, [(i, i ^ 1) for i in range(size)])  9.62 us
    pallas_call x1, Pallas kernels, hold_gate(): pl.pallas_call(kernel, in_specs=[ANY], out_specs=[VMEM, VMEM], out_shape=...  7.11 us
    ppermute x14, waiting for transfers between devices, move(): return lax.ppermute(value, axis, [(i, i ^ 1) for i in range(size)])  5.11 us
    ppermute x2, starting transfers between devices, per_device(): crossed = lax.ppermute(low, 'mp', [(i, i ^ 2 * bit) for i in range(count)])  4.64 us
    ppermute x2, waiting for transfers between devices, per_device(): crossed = lax.ppermute(low, 'mp', [(i, i ^ 2 * bit) for i in range(count)])  3.19 us
  transfers between devices with their start and end apart: 26, of which 11 were waited for; matrix products, arithmetic and copies ran while one was open for 0% of the time, Pallas kernels for 40%

profile of v3, /device:TPU:0, one launch (start us, length us, event | category | flops | bytes accessed | tf_op | source)
XLA Modules:
  0.0 96.3 jit_solution(5668597402264602298)
XLA Ops:
  0.0 3.0 %collective-permute-start = (bf16[64,4096]{1,0:T(8,128)(2,1)}, bf16[64,4096]{1,0:T(8,128)(2,1)S(1)}, u32[]{:S(2)}, u32[]{:S(2)}) collective-permute-start(bf16[64,4096]{1,0:T(8,128)(2,1)} %refs_2_), channel_id=1, source_target_pairs={{0,4},{2,6},{4,8},{6,10},{8,12},{10,14},{12,0},{14,2},{1,5},{3,7},... | collective-permute-start | bytes 1572872 | tf_op jit(solution)/shard_map/ppermute | solution.py:408
  3.0 1.5 %collective-permute-start.1 = (bf16[64,4096]{1,0:T(8,128)(2,1)}, bf16[64,4096]{1,0:T(8,128)(2,1)S(1)}, u32[]{:S(2)}, u32[]{:S(2)}) collective-permute-start(bf16[64,4096]{1,0:T(8,128)(2,1)} %refs_2_), channel_id=1, source_target_pairs={{0,2},{2,0},{4,6},{6,4},{8,10},{10,8},{12,14},{14,12},{1,3},{3,1},... | collective-permute-start | bytes 1572872 | tf_op jit(solution)/shard_map/ppermute | solution.py:389
  4.5 1.3 %split_panels.1 = (bf16[16,3584]{1,0:T(8,128)(2,1)S(1)}, bf16[16,3584]{1,0:T(8,128)(2,1)S(1)}, bf16[16,3584]{1,0:T(8,128)(2,1)S(1)}, bf16[16,3584]{1,0:T(8,128)(...) custom-call(bf16[1,64,28672]{2,1,0:T(8,128)(2,1)} %up_ref.1), custom_call_target="tpu_custom_call" | custom-call | tf_op jit(solution)/shard_map/split_panels/pallas_call | solution.py:82
  5.9 1.6 %collective-permute-start.2 = (bf16[16,3584]{1,0:T(8,128)(2,1)S(1)}, bf16[16,3584]{1,0:T(8,128)(2,1)S(1)}, u32[]{:S(2)}, u32[]{:S(2)}) collective-permute-start(bf16[16,3584]{1,0:T(8,128)(2,1)S(1)} %get-tuple-element.90), channel_id=1, source_target_pairs={{0,4},{2,6},{4,8},{6,10},{8,12},{10,14},{12,0},{14,2},{1,5},{3,7},... | collective-permute-start | bytes 344072 | tf_op jit(solution)/shard_map/ppermute | solution.py:408
  8.1 7.1 %hold_gate.1 = (bf16[4096,2560]{1,0:T(8,128)(2,1)S(1)}, f32[8,128]{1,0:T(8,128)S(1)}) custom-call(bf16[4096,3584]{1,0:T(8,128)(2,1)} %refs_3_.5), custom_call_target="tpu_custom_call" | custom-call | tf_op jit(solution)/shard_map/hold_gate/pallas_call | solution.py:134
  16.0 3.7 %collective-permute-done.2.refs_1_ = bf16[16,3584]{1,0:T(8,128)(2,1)S(1)} collective-permute-done((bf16[16,3584]{1,0:T(8,128)(2,1)S(1)}, bf16[16,3584]{1,0:T(8,128)(2,1)S(1)}, u32[]{:S(2)}, u32[]{:S(2)}) %collective-permute-start.2) | collective-permute-done | bytes 114720 | tf_op jit(solution)/shard_map/ppermute | solution.py:408
  19.7 1.6 %collective-permute-start.5 = (bf16[64,4096]{1,0:T(8,128)(2,1)S(1)}, bf16[64,4096]{1,0:T(8,128)(2,1)S(1)}, u32[]{:S(2)}, u32[]{:S(2)}) collective-permute-start(bf16[64,4096]{1,0:T(8,128)(2,1)S(1)} %collective-permute-done.refs_2_), channel_id=1, source_target_pairs={{0,2},{2,0},{4,6},{6,4},{8,10},{10,8},{12,14},{14,12},{1,3},{3,1},... | collective-permute-start | bytes 1572872 | tf_op jit(solution)/shard_map/ppermute | solution.py:389
  22.2 1.5 %collective-permute-start.6 = (bf16[16,3584]{1,0:T(8,128)(2,1)S(1)}, bf16[16,3584]{1,0:T(8,128)(2,1)S(1)}, u32[]{:S(2)}, u32[]{:S(2)}) collective-permute-start(bf16[16,3584]{1,0:T(8,128)(2,1)S(1)} %get-tuple-element.107), channel_id=1, source_target_pairs={{0,6},{2,4},{4,10},{6,8},{8,14},{10,12},{12,2},{14,0},{1,7},{3,5},... | collective-permute-start | bytes 344072 | tf_op jit(solution)/shard_map/ppermute | solution.py:408
  23.7 6.4 %base_chunk.5 = (f32[128,3584]{1,0:T(8,128)S(1)}, bf16[128,3584]{1,0:T(8,128)(2,1)S(1)}, f32[128,64]{1,0:T(8,128)S(1)}) custom-call(bf16[4096,2560]{1,0:T(8,128)(2,1)S(1)} %get-tuple-element.88.refs_0_.refs_2_, bf16[4096,3584]{1,0:T(8,128)(2,1)} %refs_3_.5, bf16[64,4096]{1,0:T(8,128)(2,1)S(1)} %copy-done.1, ...), custom_call_target="tpu_custom_call" | custom-call | tf_op jit(solution)/shard_map/base_chunk/pallas_call | solution.py:239
  30.1 8.1 %collective-permute-done.6.refs_3_ = bf16[16,3584]{1,0:T(8,128)(2,1)S(1)} collective-permute-done((bf16[16,3584]{1,0:T(8,128)(2,1)S(1)}, bf16[16,3584]{1,0:T(8,128)(2,1)S(1)}, u32[]{:S(2)}, u32[]{:S(2)}) %collective-permute-start.6) | collective-permute-done | bytes 114720 | tf_op jit(solution)/shard_map/ppermute | solution.py:408
  39.6 4.0 %collective-permute-start.9 = (bf16[16,3584]{1,0:T(8,128)(2,1)S(1)}, bf16[16,3584]{1,0:T(8,128)(2,1)S(1)}, u32[]{:S(2)}, u32[]{:S(2)}) collective-permute-start(bf16[16,3584]{1,0:T(8,128)(2,1)S(1)} %get-tuple-element.118), channel_id=1, source_target_pairs={{0,14},{2,12},{4,2},{6,0},{8,6},{10,4},{12,10},{14,8},{1,15},{3,13... | collective-permute-start | bytes 344072 | tf_op jit(solution)/shard_map/ppermute | solution.py:408
  43.6 6.4 %base_chunk.6 = (f32[128,3584]{1,0:T(8,128)S(1)}, bf16[128,3584]{1,0:T(8,128)(2,1)S(1)}, f32[128,64]{1,0:T(8,128)S(1)}) custom-call(bf16[4096,2560]{1,0:T(8,128)(2,1)S(1)} %get-tuple-element.88.refs_0_.refs_2_, bf16[4096,3584]{1,0:T(8,128)(2,1)} %refs_3_.5, bf16[64,4096]{1,0:T(8,128)(2,1)S(1)} %collective-permute-done.refs_2_, ...), custom_call_target="tpu_custom_call" | custom-call | tf_op jit(solution)/shard_map/base_chunk/pallas_call | solution.py:239
  50.0 1.8 %collective-permute-done.9.refs_4_ = bf16[16,3584]{1,0:T(8,128)(2,1)S(1)} collective-permute-done((bf16[16,3584]{1,0:T(8,128)(2,1)S(1)}, bf16[16,3584]{1,0:T(8,128)(2,1)S(1)}, u32[]{:S(2)}, u32[]{:S(2)}) %collective-permute-start.9) | collective-permute-done | bytes 114720 | tf_op jit(solution)/shard_map/ppermute | solution.py:408
  56.7 2.8 %collective-permute-start.11 = (bf16[16,3584]{1,0:T(8,128)(2,1)S(1)}, bf16[16,3584]{1,0:T(8,128)(2,1)S(1)}, u32[]{:S(2)}, u32[]{:S(2)}) collective-permute-start(bf16[16,3584]{1,0:T(8,128)(2,1)S(1)} %get-tuple-element.134), channel_id=1, source_target_pairs={{0,8},{2,10},{4,12},{6,14},{8,0},{10,2},{12,4},{14,6},{1,9},{3,11}... | collective-permute-start | bytes 344072 | tf_op jit(solution)/shard_map/ppermute | solution.py:408
  59.5 6.5 %base_chunk.7 = (f32[128,3584]{1,0:T(8,128)S(1)}, bf16[128,3584]{1,0:T(8,128)(2,1)S(1)}, f32[128,64]{1,0:T(8,128)S(1)}) custom-call(f32[128,3584]{1,0:T(8,128)S(1)} %get-tuple-element.101.refs_0_, bf16[128,3584]{1,0:T(8,128)(2,1)S(1)} %get-tuple-element.102.refs_1_, ...), custom_call_target="tpu_custom_call", output_to_operand_aliasing={{0}: (0, {}), {1}: (1, {})} | custom-call | tf_op jit(solution)/shard_map/base_chunk/pallas_call | solution.py:239
  68.2 1.3 %collective-permute-done.13.receive_ref = f32[256,64]{1,0:T(8,128)S(1)} collective-permute-done((f32[256,64]{1,0:T(8,128)S(1)}, f32[256,64]{1,0:T(8,128)S(1)}, u32[]{:S(2)}, u32[]{:S(2)}) %collective-permute-start.13) | collective-permute-done | bytes 65568 | tf_op jit(solution)/shard_map/ppermute | solution.py:389
  69.7 1.6 %collective-permute-start.14 = (bf16[256,64]{1,0:T(8,128)(2,1)S(1)}, bf16[256,64]{1,0:T(8,128)(2,1)S(1)}, u32[]{:S(2)}, u32[]{:S(2)}) collective-permute-start(bf16[256,64]{1,0:T(8,128)(2,1)S(1)} %low_own.1.one_ref), channel_id=1, source_target_pairs={{0,2},{2,0},{4,6},{6,4},{8,10},{10,8},{12,14},{14,12},{1,3},{3,1},... | collective-permute-start | bytes 98312 | tf_op jit(solution)/shard_map/ppermute | solution.py:389
  71.3 4.1 %base_chunk.8 = (f32[128,3584]{1,0:T(8,128)S(1)}, bf16[128,3584]{1,0:T(8,128)(2,1)S(1)}) custom-call(f32[128,3584]{1,0:T(8,128)S(1)} %get-tuple-element.146.refs_0_, bf16[128,3584]{1,0:T(8,128)(2,1)S(1)} %get-tuple-element.147.refs_1_, bf16[4096,2560]{1,0:T(8,128)(2,1)S(1)} %get-tuple-element.88.refs_0_.refs_2_, ...), custom_call_target="tpu_custom_call", output_to_operand_aliasing={{0}: (0, {}), {1}: (1, {})} | custom-call | tf_op jit(solution)/shard_map/base_chunk/pallas_call | solution.py:239
  77.1 2.6 %collective-permute-start.18 = (bf16[256,64]{1,0:T(8,128)(2,1)S(1)}, bf16[256,64]{1,0:T(8,128)(2,1)S(1)}, u32[]{:S(2)}, u32[]{:S(2)}) collective-permute-start(bf16[256,64]{1,0:T(8,128)(2,1)S(1)} %add.3.one_ref), channel_id=1, source_target_pairs={{0,4},{2,6},{4,0},{6,2},{8,12},{10,14},{12,8},{14,10},{1,5},{3,7},... | collective-permute-start | bytes 98312 | tf_op jit(solution)/shard_map/ppermute | solution.py:483
  79.7 4.9 %base_chunk.9 = (f32[128,3584]{1,0:T(8,128)S(1)}, bf16[128,3584]{1,0:T(8,128)(2,1)S(1)}) custom-call(f32[128,3584]{1,0:T(8,128)S(1)} %get-tuple-element.155.refs_0_, bf16[128,3584]{1,0:T(8,128)(2,1)S(1)} %get-tuple-element.156.refs_1_, bf16[4096,2560]{1,0:T(8,128)(2,1)S(1)} %get-tuple-element.88.refs_0_.refs_2_, ...), custom_call_target="tpu_custom_call", output_to_operand_aliasing={{0}: (0, {}), {1}: (1, {})} | custom-call | tf_op jit(solution)/shard_map/base_chunk/pallas_call | solution.py:239
  86.4 2.0 %collective-permute-start.25 = (bf16[256,64]{1,0:T(8,128)(2,1)S(1)}, bf16[256,64]{1,0:T(8,128)(2,1)S(1)}, u32[]{:S(2)}, u32[]{:S(2)}) collective-permute-start(bf16[256,64]{1,0:T(8,128)(2,1)S(1)} %add.4.one_ref), channel_id=1, source_target_pairs={{0,8},{2,10},{4,12},{6,14},{8,0},{10,2},{12,4},{14,6},{1,9},{3,11}... | collective-permute-start | bytes 98312 | tf_op jit(solution)/shard_map/ppermute | solution.py:483
  88.4 3.2 %collective-permute-done.25.two_ref = bf16[256,64]{1,0:T(8,128)(2,1)S(1)} collective-permute-done((bf16[256,64]{1,0:T(8,128)(2,1)S(1)}, bf16[256,64]{1,0:T(8,128)(2,1)S(1)}, u32[]{:S(2)}, u32[]{:S(2)}) %collective-permute-start.25) | collective-permute-done | bytes 32800 | tf_op jit(solution)/shard_map/ppermute | solution.py:483
  91.7 1.6 %collective-permute-done.24.refs_12_ = bf16[3,16,3584]{2,1,0:T(8,128)(2,1)S(1)} collective-permute-done((bf16[3,16,3584]{2,1,0:T(8,128)(2,1)S(1)}, bf16[3,16,3584]{2,1,0:T(8,128)(2,1)S(1)}, u32[]{:S(2)}, u32[]{:S(2)}) %collective-permute-start.24) | collective-permute-done | bytes 344096 | tf_op jit(solution)/shard_map/ppermute | solution.py:389
  93.3 3.0 %finish.1 = bf16[256,3584]{1,0:T(8,128)(2,1)} custom-call(f32[128,3584]{1,0:T(8,128)S(1)} %get-tuple-element.127.refs_0_, f32[128,3584]{1,0:T(8,128)S(1)} %get-tuple-element.162.refs_1_, bf16[128,3584]{1,0:T(8,128)(2,1)S(1)} %collective-permute-done.20.refs_2_, bf16[128,3584]{1,0:T(8,128)(2,1)S(1)} %collective-permute-done.21.refs_3_, ...), custom_call_target="tpu_custom_call" | custom-call | tf_op jit(solution)/shard_map/finish/pallas_call | solution.py:371
  (52 shorter events, 14.2 us)
Async XLA Ops:
  0.0 19.6 %collective-permute-start = (bf16[64,4096]{1,0:T(8,128)(2,1)}, bf16[64,4096]{1,0:T(8,128)(2,1)S(1)}, u32[]{:S(2)}, u32[]{:S(2)}) collective-permute-start(bf16[64,4096]{1,0:T(8,128)(2,1)} %refs_2_), channel_id=1, source_target_pairs={{0,4},{2,6},{4,8},{6,10},{8,12},{10,14},{12,0},{14,2},{1,5},{3,7},... | collective-permute-start | bytes 1572872 | tf_op jit(solution)/shard_map/ppermute | solution.py:408
  3.0 16.6 %collective-permute-start.1 = (bf16[64,4096]{1,0:T(8,128)(2,1)}, bf16[64,4096]{1,0:T(8,128)(2,1)S(1)}, u32[]{:S(2)}, u32[]{:S(2)}) collective-permute-start(bf16[64,4096]{1,0:T(8,128)(2,1)} %refs_2_), channel_id=1, source_target_pairs={{0,2},{2,0},{4,6},{6,4},{8,10},{10,8},{12,14},{14,12},{1,3},{3,1},... | collective-permute-start | bytes 1572872 | tf_op jit(solution)/shard_map/ppermute | solution.py:389
  5.9 13.8 %collective-permute-start.2 = (bf16[16,3584]{1,0:T(8,128)(2,1)S(1)}, bf16[16,3584]{1,0:T(8,128)(2,1)S(1)}, u32[]{:S(2)}, u32[]{:S(2)}) collective-permute-start(bf16[16,3584]{1,0:T(8,128)(2,1)S(1)} %get-tuple-element.90), channel_id=1, source_target_pairs={{0,4},{2,6},{4,8},{6,10},{8,12},{10,14},{12,0},{14,2},{1,5},{3,7},... | collective-permute-start | bytes 344072 | tf_op jit(solution)/shard_map/ppermute | solution.py:408
  7.5 12.1 %collective-permute-start.3 = (bf16[16,3584]{1,0:T(8,128)(2,1)S(1)}, bf16[16,3584]{1,0:T(8,128)(2,1)S(1)}, u32[]{:S(2)}, u32[]{:S(2)}) collective-permute-start(bf16[16,3584]{1,0:T(8,128)(2,1)S(1)} %get-tuple-element.91), channel_id=1, source_target_pairs={{0,2},{2,0},{4,6},{6,4},{8,10},{10,8},{12,14},{14,12},{1,3},{3,1},... | collective-permute-start | bytes 344072 | tf_op jit(solution)/shard_map/ppermute | solution.py:408
  19.7 18.6 %collective-permute-start.5 = (bf16[64,4096]{1,0:T(8,128)(2,1)S(1)}, bf16[64,4096]{1,0:T(8,128)(2,1)S(1)}, u32[]{:S(2)}, u32[]{:S(2)}) collective-permute-start(bf16[64,4096]{1,0:T(8,128)(2,1)S(1)} %collective-permute-done.refs_2_), channel_id=1, source_target_pairs={{0,2},{2,0},{4,6},{6,4},{8,10},{10,8},{12,14},{14,12},{1,3},{3,1},... | collective-permute-start | bytes 1572872 | tf_op jit(solution)/shard_map/ppermute | solution.py:389
  21.2 17.0 %collective-permute-start.4 = (bf16[64,4096]{1,0:T(8,128)(2,1)S(1)}, bf16[64,4096]{1,0:T(8,128)(2,1)S(1)}, u32[]{:S(2)}, u32[]{:S(2)}) collective-permute-start(bf16[64,4096]{1,0:T(8,128)(2,1)S(1)} %collective-permute-done.refs_2_), channel_id=1, source_target_pairs={{0,4},{2,6},{4,8},{6,10},{8,12},{10,14},{12,0},{14,2},{1,5},{3,7},... | collective-permute-start | bytes 1572872 | tf_op jit(solution)/shard_map/ppermute | solution.py:408
  22.2 16.1 %collective-permute-start.6 = (bf16[16,3584]{1,0:T(8,128)(2,1)S(1)}, bf16[16,3584]{1,0:T(8,128)(2,1)S(1)}, u32[]{:S(2)}, u32[]{:S(2)}) collective-permute-start(bf16[16,3584]{1,0:T(8,128)(2,1)S(1)} %get-tuple-element.107), channel_id=1, source_target_pairs={{0,6},{2,4},{4,10},{6,8},{8,14},{10,12},{12,2},{14,0},{1,7},{3,5},... | collective-permute-start | bytes 344072 | tf_op jit(solution)/shard_map/ppermute | solution.py:408
  38.3 14.4 %collective-permute-start.8 = (bf16[64,4096]{1,0:T(8,128)(2,1)S(1)}, bf16[64,4096]{1,0:T(8,128)(2,1)S(1)}, u32[]{:S(2)}, u32[]{:S(2)}) collective-permute-start(bf16[64,4096]{1,0:T(8,128)(2,1)S(1)} %collective-permute-done.4.refs_4_), channel_id=1, source_target_pairs={{0,2},{2,0},{4,6},{6,4},{8,10},{10,8},{12,14},{14,12},{1,3},{3,1},... | collective-permute-start | bytes 1572872 | tf_op jit(solution)/shard_map/ppermute | solution.py:389
  39.5 14.2 %collective-permute-start.7 = (bf16[64,4096]{1,0:T(8,128)(2,1)S(1)}, bf16[64,4096]{1,0:T(8,128)(2,1)S(1)}, u32[]{:S(2)}, u32[]{:S(2)}) collective-permute-start(bf16[64,4096]{1,0:T(8,128)(2,1)S(1)} %collective-permute-done.4.refs_4_), channel_id=1, source_target_pairs={{0,4},{2,6},{4,8},{6,10},{8,12},{10,14},{12,0},{14,2},{1,5},{3,7},... | collective-permute-start | bytes 1572872 | tf_op jit(solution)/shard_map/ppermute | solution.py:408
  39.6 12.2 %collective-permute-start.9 = (bf16[16,3584]{1,0:T(8,128)(2,1)S(1)}, bf16[16,3584]{1,0:T(8,128)(2,1)S(1)}, u32[]{:S(2)}, u32[]{:S(2)}) collective-permute-start(bf16[16,3584]{1,0:T(8,128)(2,1)S(1)} %get-tuple-element.118), channel_id=1, source_target_pairs={{0,14},{2,12},{4,2},{6,0},{8,6},{10,4},{12,10},{14,8},{1,15},{3,13... | collective-permute-start | bytes 344072 | tf_op jit(solution)/shard_map/ppermute | solution.py:408
  53.7 13.1 %collective-permute-start.10 = (bf16[64,4096]{1,0:T(8,128)(2,1)S(1)}, bf16[64,4096]{1,0:T(8,128)(2,1)S(1)}, u32[]{:S(2)}, u32[]{:S(2)}) collective-permute-start(bf16[64,4096]{1,0:T(8,128)(2,1)S(1)} %collective-permute-done.7.refs_0_.refs_4_), channel_id=1, source_target_pairs={{0,2},{2,0},{4,6},{6,4},{8,10},{10,8},{12,14},{14,12},{1,3},{3,1},... | collective-permute-start | bytes 1572872 | tf_op jit(solution)/shard_map/ppermute | solution.py:389
  55.5 19.9 %collective-permute-start.17 = (bf16[5,16,3584]{2,1,0:T(8,128)(2,1)S(1)}, bf16[5,16,3584]{2,1,0:T(8,128)(2,1)S(1)}, u32[]{:S(2)}, u32[]{:S(2)}) collective-permute-start(bf16[5,16,3584]{2,1,0:T(8,128)(2,1)S(1)} %stack.2.refs_5_), channel_id=1, source_target_pairs={{0,1},{1,0},{2,3},{3,2},{4,5},{5,4},{6,7},{7,6},{8,9},{9,8},{10,11... | collective-permute-start | bytes 1720328 | tf_op jit(solution)/shard_map/ppermute | solution.py:389
  55.5 19.9 %collective-permute-start.16 = (bf16[5,16,3584]{2,1,0:T(8,128)(2,1)S(1)}, bf16[5,16,3584]{2,1,0:T(8,128)(2,1)S(1)}, u32[]{:S(2)}, u32[]{:S(2)}) collective-permute-start(bf16[5,16,3584]{2,1,0:T(8,128)(2,1)S(1)} %stack.2.refs_5_), channel_id=1, source_target_pairs={{0,16},{16,0},{1,17},{17,1},{2,18},{18,2},{3,19},{19,3},{4,20},{20... | collective-permute-start | bytes 1720328 | tf_op jit(solution)/shard_map/ppermute | solution.py:389
  56.7 9.3 %collective-permute-start.11 = (bf16[16,3584]{1,0:T(8,128)(2,1)S(1)}, bf16[16,3584]{1,0:T(8,128)(2,1)S(1)}, u32[]{:S(2)}, u32[]{:S(2)}) collective-permute-start(bf16[16,3584]{1,0:T(8,128)(2,1)S(1)} %get-tuple-element.134), channel_id=1, source_target_pairs={{0,8},{2,10},{4,12},{6,14},{8,0},{10,2},{12,4},{14,6},{1,9},{3,11}... | collective-permute-start | bytes 344072 | tf_op jit(solution)/shard_map/ppermute | solution.py:408
  59.5 7.3 %collective-permute-start.12 = (bf16[16,3584]{1,0:T(8,128)(2,1)S(1)}, bf16[16,3584]{1,0:T(8,128)(2,1)S(1)}, u32[]{:S(2)}, u32[]{:S(2)}) collective-permute-start(bf16[16,3584]{1,0:T(8,128)(2,1)S(1)} %get-tuple-element.135), channel_id=1, source_target_pairs={{0,12},{2,14},{4,0},{6,2},{8,4},{10,6},{12,8},{14,10},{1,13},{3,15... | collective-permute-start | bytes 344072 | tf_op jit(solution)/shard_map/ppermute | solution.py:408
  66.8 8.9 %collective-permute-start.15 = (bf16[16,3584]{1,0:T(8,128)(2,1)S(1)}, bf16[16,3584]{1,0:T(8,128)(2,1)S(1)}, u32[]{:S(2)}, u32[]{:S(2)}) collective-permute-start(bf16[16,3584]{1,0:T(8,128)(2,1)S(1)} %get-tuple-element.152), channel_id=1, source_target_pairs={{0,10},{2,8},{4,14},{6,12},{8,2},{10,0},{12,6},{14,4},{1,11},{3,9}... | collective-permute-start | bytes 344072 | tf_op jit(solution)/shard_map/ppermute | solution.py:408
  69.7 5.7 %collective-permute-start.14 = (bf16[256,64]{1,0:T(8,128)(2,1)S(1)}, bf16[256,64]{1,0:T(8,128)(2,1)S(1)}, u32[]{:S(2)}, u32[]{:S(2)}) collective-permute-start(bf16[256,64]{1,0:T(8,128)(2,1)S(1)} %low_own.1.one_ref), channel_id=1, source_target_pairs={{0,2},{2,0},{4,6},{6,4},{8,10},{10,8},{12,14},{14,12},{1,3},{3,1},... | collective-permute-start | bytes 98312 | tf_op jit(solution)/shard_map/ppermute | solution.py:389
  76.2 9.7 %collective-permute-start.19 = (bf16[3,16,3584]{2,1,0:T(8,128)(2,1)S(1)}, bf16[3,16,3584]{2,1,0:T(8,128)(2,1)S(1)}, u32[]{:S(2)}, u32[]{:S(2)}) collective-permute-start(bf16[3,16,3584]{2,1,0:T(8,128)(2,1)S(1)} %stack.3.refs_6_), channel_id=1, source_target_pairs={{0,16},{16,0},{1,17},{17,1},{2,18},{18,2},{3,19},{19,3},{4,20},{20... | collective-permute-start | bytes 1032200 | tf_op jit(solution)/shard_map/ppermute | solution.py:389
  77.1 7.5 %collective-permute-start.18 = (bf16[256,64]{1,0:T(8,128)(2,1)S(1)}, bf16[256,64]{1,0:T(8,128)(2,1)S(1)}, u32[]{:S(2)}, u32[]{:S(2)}) collective-permute-start(bf16[256,64]{1,0:T(8,128)(2,1)S(1)} %add.3.one_ref), channel_id=1, source_target_pairs={{0,4},{2,6},{4,0},{6,2},{8,12},{10,14},{12,8},{14,10},{1,5},{3,7},... | collective-permute-start | bytes 98312 | tf_op jit(solution)/shard_map/ppermute | solution.py:483
  79.7 12.0 %collective-permute-start.20 = (bf16[128,3584]{1,0:T(8,128)(2,1)S(1)}, bf16[128,3584]{1,0:T(8,128)(2,1)S(1)}, u32[]{:S(2)}, u32[]{:S(2)}) collective-permute-start(bf16[128,3584]{1,0:T(8,128)(2,1)S(1)} %get-tuple-element.163), channel_id=1, source_target_pairs={{0,1},{1,0},{2,3},{3,2},{4,5},{5,4},{6,7},{7,6},{8,9},{9,8},{10,11... | collective-permute-start | bytes 2752520 | tf_op jit(solution)/shard_map/ppermute | solution.py:389
  85.8 7.4 %collective-permute-start.21 = (bf16[128,3584]{1,0:T(8,128)(2,1)S(1)}, bf16[128,3584]{1,0:T(8,128)(2,1)S(1)}, u32[]{:S(2)}, u32[]{:S(2)}) collective-permute-start(bf16[128,3584]{1,0:T(8,128)(2,1)S(1)} %get-tuple-element.164), channel_id=1, source_target_pairs={{0,1},{1,0},{2,3},{3,2},{4,5},{5,4},{6,7},{7,6},{8,9},{9,8},{10,11... | collective-permute-start | bytes 2752520 | tf_op jit(solution)/shard_map/ppermute | solution.py:389
  85.9 5.8 %collective-permute-start.23 = (bf16[5,16,3584]{2,1,0:T(8,128)(2,1)S(1)}, bf16[5,16,3584]{2,1,0:T(8,128)(2,1)S(1)}, u32[]{:S(2)}, u32[]{:S(2)}) collective-permute-start(bf16[5,16,3584]{2,1,0:T(8,128)(2,1)S(1)} %collective-permute-done.16.refs_7_), channel_id=1, source_target_pairs={{0,1},{1,0},{2,3},{3,2},{4,5},{5,4},{6,7},{7,6},{8,9},{9,8},{10,11... | collective-permute-start | bytes 1720328 | tf_op jit(solution)/shard_map/ppermute | solution.py:389
  86.4 5.2 %collective-permute-start.25 = (bf16[256,64]{1,0:T(8,128)(2,1)S(1)}, bf16[256,64]{1,0:T(8,128)(2,1)S(1)}, u32[]{:S(2)}, u32[]{:S(2)}) collective-permute-start(bf16[256,64]{1,0:T(8,128)(2,1)S(1)} %add.4.one_ref), channel_id=1, source_target_pairs={{0,8},{2,10},{4,12},{6,14},{8,0},{10,2},{12,4},{14,6},{1,9},{3,11}... | collective-permute-start | bytes 98312 | tf_op jit(solution)/shard_map/ppermute | solution.py:483
  88.4 3.2 %collective-permute-start.22 = (bf16[3,16,3584]{2,1,0:T(8,128)(2,1)S(1)}, bf16[3,16,3584]{2,1,0:T(8,128)(2,1)S(1)}, u32[]{:S(2)}, u32[]{:S(2)}) collective-permute-start(bf16[3,16,3584]{2,1,0:T(8,128)(2,1)S(1)} %stack.3.refs_6_), channel_id=1, source_target_pairs={{0,1},{1,0},{2,3},{3,2},{4,5},{5,4},{6,7},{7,6},{8,9},{9,8},{10,11... | collective-permute-start | bytes 1032200 | tf_op jit(solution)/shard_map/ppermute | solution.py:389
  (6 other events, 50.9 us)

commit v4 on v3

--- a/solution.py
+++ b/solution.py
@@ -478,19 +478,14 @@
     second = stack(moved)
     second_x, second_c = other_group(second), other_core(second)
     low = add(low, crossed)
-    bit = 1
-    while bit < levels:
-        crossed = lax.ppermute(low, "mp", [(i, i ^ (2 * bit)) for i in range(count)])
-        if bit == 1:
-            multiply(last, near, far, None, tiles="streamed")
-            low, crossed, pair_left[last % pairs], second_x = together(
-                (low, crossed, pair_left[last % pairs], second_x)
-            )
-            receives = [other_core(pair_left[k][1]) for k in range(pairs)]
-        low = add(low, crossed)
-        bit *= 2
+    parts = [along_mp(low, j) for j in range(1, levels)]
+    multiply(last, near, far, None, tiles="streamed")
+    low, parts, pair_left[last % pairs], second_x, second_c = together(
+        (low, parts, pair_left[last % pairs], second_x, second_c)
+    )
+    parts = [low] + parts
+    receives = [other_core(pair_left[k][1]) for k in range(pairs)]
     keeps = [pair_left[k][0] for k in range(pairs)]
-    parts = [low]
     panels = [
         (first, second),
         (first_x, second_x),

time: 96.7 us -> 94.7 us (0.979)
  waiting for transfers between devices: 24 us -> 22.7 us
    ppermute x2 -> x0, starting transfers between devices: 4.64 us -> none  [per_device(): crossed = lax.ppermute(low, 'mp', [(i, i ^ 2 * bit) for i in range(count)])]
    ppermute x10 -> x13, starting transfers between devices: 15.4 us -> 19.4 us  [along_mp(): return lax.ppermute(value, 'mp', pairs_of)]
    ppermute x2 -> x0, waiting for transfers between devices: 3.19 us -> none  [per_device(): crossed = lax.ppermute(low, 'mp', [(i, i ^ 2 * bit) for i in range(count)])]
    ppermute x10 -> x13, waiting for transfers between devices: 15.7 us -> 17.2 us  [along_mp(): return lax.ppermute(value, 'mp', pairs_of)]
  transfers between devices with their start and end apart: 26 -> 27, of which waited for: 11 -> 12; matrix products, arithmetic and copies ran while one was open for 0% -> 0% of each run, Pallas kernels for 40% -> 41%
where the time goes in v4:
time: 94.7 us; the launch traced here: 94.5 us
  Pallas kernels  42.3 us (45%)
  starting transfers between devices  29.3 us (31%)
  waiting for transfers between devices  22.7 us (24%)
    pallas_call x5, Pallas kernels, base_chunk(): pl.pallas_call(kernel, grid=(pieces if tiles == 'streamed' else HELD,), i...  28.3 us
    ppermute x13, starting transfers between devices, along_mp(): return lax.ppermute(value, 'mp', pairs_of)  19.4 us
    ppermute x13, waiting for transfers between devices, along_mp(): return lax.ppermute(value, 'mp', pairs_of)  17.2 us
    ppermute x14, starting transfers between devices, move(): return lax.ppermute(value, axis, [(i, i ^ 1) for i in range(size)])  9.89 us
    pallas_call x1, Pallas kernels, hold_gate(): pl.pallas_call(kernel, in_specs=[ANY], out_specs=[VMEM, VMEM], out_shape=...  7.11 us
    ppermute x14, waiting for transfers between devices, move(): return lax.ppermute(value, axis, [(i, i ^ 1) for i in range(size)])  5.48 us
    pallas_call x1, Pallas kernels, finish(): pl.pallas_call(kernel, grid=(width // tile,), in_specs=[VMEM] * pairs + [...  2.99 us
  transfers between devices with their start and end apart: 27, of which 12 were waited for; matrix products, arithmetic and copies ran while one was open for 0% of the time, Pallas kernels for 41%

profile of v4, /device:TPU:0, one launch (start us, length us, event | category | flops | bytes accessed | tf_op | source)
XLA Modules:
  0.0 94.5 jit_solution(12373899713707432761)
XLA Ops:
  0.0 3.0 %collective-permute-start = (bf16[64,4096]{1,0:T(8,128)(2,1)}, bf16[64,4096]{1,0:T(8,128)(2,1)S(1)}, u32[]{:S(2)}, u32[]{:S(2)}) collective-permute-start(bf16[64,4096]{1,0:T(8,128)(2,1)} %refs_2_), channel_id=1, source_target_pairs={{0,4},{2,6},{4,8},{6,10},{8,12},{10,14},{12,0},{14,2},{1,5},{3,7},... | collective-permute-start | bytes 1572872 | tf_op jit(solution)/shard_map/ppermute | solution.py:408
  3.0 1.5 %collective-permute-start.1 = (bf16[64,4096]{1,0:T(8,128)(2,1)}, bf16[64,4096]{1,0:T(8,128)(2,1)S(1)}, u32[]{:S(2)}, u32[]{:S(2)}) collective-permute-start(bf16[64,4096]{1,0:T(8,128)(2,1)} %refs_2_), channel_id=1, source_target_pairs={{0,2},{2,0},{4,6},{6,4},{8,10},{10,8},{12,14},{14,12},{1,3},{3,1},... | collective-permute-start | bytes 1572872 | tf_op jit(solution)/shard_map/ppermute | solution.py:389
  4.5 1.3 %split_panels.1 = (bf16[16,3584]{1,0:T(8,128)(2,1)S(1)}, bf16[16,3584]{1,0:T(8,128)(2,1)S(1)}, bf16[16,3584]{1,0:T(8,128)(2,1)S(1)}, bf16[16,3584]{1,0:T(8,128)(...) custom-call(bf16[1,64,28672]{2,1,0:T(8,128)(2,1)} %up_ref.1), custom_call_target="tpu_custom_call" | custom-call | tf_op jit(solution)/shard_map/split_panels/pallas_call | solution.py:82
  5.9 1.6 %collective-permute-start.2 = (bf16[16,3584]{1,0:T(8,128)(2,1)S(1)}, bf16[16,3584]{1,0:T(8,128)(2,1)S(1)}, u32[]{:S(2)}, u32[]{:S(2)}) collective-permute-start(bf16[16,3584]{1,0:T(8,128)(2,1)S(1)} %get-tuple-element.93), channel_id=1, source_target_pairs={{0,4},{2,6},{4,8},{6,10},{8,12},{10,14},{12,0},{14,2},{1,5},{3,7},... | collective-permute-start | bytes 344072 | tf_op jit(solution)/shard_map/ppermute | solution.py:408
  8.1 7.1 %hold_gate.1 = (bf16[4096,2560]{1,0:T(8,128)(2,1)S(1)}, f32[8,128]{1,0:T(8,128)S(1)}) custom-call(bf16[4096,3584]{1,0:T(8,128)(2,1)} %refs_3_.5), custom_call_target="tpu_custom_call" | custom-call | tf_op jit(solution)/shard_map/hold_gate/pallas_call | solution.py:134
  16.0 3.7 %collective-permute-done.2.refs_1_ = bf16[16,3584]{1,0:T(8,128)(2,1)S(1)} collective-permute-done((bf16[16,3584]{1,0:T(8,128)(2,1)S(1)}, bf16[16,3584]{1,0:T(8,128)(2,1)S(1)}, u32[]{:S(2)}, u32[]{:S(2)}) %collective-permute-start.2) | collective-permute-done | bytes 114720 | tf_op jit(solution)/shard_map/ppermute | solution.py:408
  19.7 1.6 %collective-permute-start.5 = (bf16[64,4096]{1,0:T(8,128)(2,1)S(1)}, bf16[64,4096]{1,0:T(8,128)(2,1)S(1)}, u32[]{:S(2)}, u32[]{:S(2)}) collective-permute-start(bf16[64,4096]{1,0:T(8,128)(2,1)S(1)} %collective-permute-done.refs_2_), channel_id=1, source_target_pairs={{0,2},{2,0},{4,6},{6,4},{8,10},{10,8},{12,14},{14,12},{1,3},{3,1},... | collective-permute-start | bytes 1572872 | tf_op jit(solution)/shard_map/ppermute | solution.py:389
  22.2 1.5 %collective-permute-start.6 = (bf16[16,3584]{1,0:T(8,128)(2,1)S(1)}, bf16[16,3584]{1,0:T(8,128)(2,1)S(1)}, u32[]{:S(2)}, u32[]{:S(2)}) collective-permute-start(bf16[16,3584]{1,0:T(8,128)(2,1)S(1)} %get-tuple-element.110), channel_id=1, source_target_pairs={{0,6},{2,4},{4,10},{6,8},{8,14},{10,12},{12,2},{14,0},{1,7},{3,5},... | collective-permute-start | bytes 344072 | tf_op jit(solution)/shard_map/ppermute | solution.py:408
  23.7 6.4 %base_chunk.5 = (f32[128,3584]{1,0:T(8,128)S(1)}, bf16[128,3584]{1,0:T(8,128)(2,1)S(1)}, f32[128,64]{1,0:T(8,128)S(1)}) custom-call(bf16[4096,2560]{1,0:T(8,128)(2,1)S(1)} %get-tuple-element.91.refs_0_.refs_2_, bf16[4096,3584]{1,0:T(8,128)(2,1)} %refs_3_.5, bf16[64,4096]{1,0:T(8,128)(2,1)S(1)} %copy-done.1, ...), custom_call_target="tpu_custom_call" | custom-call | tf_op jit(solution)/shard_map/base_chunk/pallas_call | solution.py:239
  30.1 8.1 %collective-permute-done.6.refs_3_ = bf16[16,3584]{1,0:T(8,128)(2,1)S(1)} collective-permute-done((bf16[16,3584]{1,0:T(8,128)(2,1)S(1)}, bf16[16,3584]{1,0:T(8,128)(2,1)S(1)}, u32[]{:S(2)}, u32[]{:S(2)}) %collective-permute-start.6) | collective-permute-done | bytes 114720 | tf_op jit(solution)/shard_map/ppermute | solution.py:408
  38.3 1.3 %collective-permute-start.8 = (bf16[64,4096]{1,0:T(8,128)(2,1)S(1)}, bf16[64,4096]{1,0:T(8,128)(2,1)S(1)}, u32[]{:S(2)}, u32[]{:S(2)}) collective-permute-start(bf16[64,4096]{1,0:T(8,128)(2,1)S(1)} %collective-permute-done.4.refs_4_), channel_id=1, source_target_pairs={{0,2},{2,0},{4,6},{6,4},{8,10},{10,8},{12,14},{14,12},{1,3},{3,1},... | collective-permute-start | bytes 1572872 | tf_op jit(solution)/shard_map/ppermute | solution.py:389
  39.6 4.0 %collective-permute-start.9 = (bf16[16,3584]{1,0:T(8,128)(2,1)S(1)}, bf16[16,3584]{1,0:T(8,128)(2,1)S(1)}, u32[]{:S(2)}, u32[]{:S(2)}) collective-permute-start(bf16[16,3584]{1,0:T(8,128)(2,1)S(1)} %get-tuple-element.121), channel_id=1, source_target_pairs={{0,14},{2,12},{4,2},{6,0},{8,6},{10,4},{12,10},{14,8},{1,15},{3,13... | collective-permute-start | bytes 344072 | tf_op jit(solution)/shard_map/ppermute | solution.py:408
  43.6 6.4 %base_chunk.6 = (f32[128,3584]{1,0:T(8,128)S(1)}, bf16[128,3584]{1,0:T(8,128)(2,1)S(1)}, f32[128,64]{1,0:T(8,128)S(1)}) custom-call(bf16[4096,2560]{1,0:T(8,128)(2,1)S(1)} %get-tuple-element.91.refs_0_.refs_2_, bf16[4096,3584]{1,0:T(8,128)(2,1)} %refs_3_.5, bf16[64,4096]{1,0:T(8,128)(2,1)S(1)} %collective-permute-done.refs_2_, ...), custom_call_target="tpu_custom_call" | custom-call | tf_op jit(solution)/shard_map/base_chunk/pallas_call | solution.py:239
  50.0 1.8 %collective-permute-done.9.refs_4_ = bf16[16,3584]{1,0:T(8,128)(2,1)S(1)} collective-permute-done((bf16[16,3584]{1,0:T(8,128)(2,1)S(1)}, bf16[16,3584]{1,0:T(8,128)(2,1)S(1)}, u32[]{:S(2)}, u32[]{:S(2)}) %collective-permute-start.9) | collective-permute-done | bytes 114720 | tf_op jit(solution)/shard_map/ppermute | solution.py:408
  56.7 2.8 %collective-permute-start.11 = (bf16[16,3584]{1,0:T(8,128)(2,1)S(1)}, bf16[16,3584]{1,0:T(8,128)(2,1)S(1)}, u32[]{:S(2)}, u32[]{:S(2)}) collective-permute-start(bf16[16,3584]{1,0:T(8,128)(2,1)S(1)} %get-tuple-element.137), channel_id=1, source_target_pairs={{0,8},{2,10},{4,12},{6,14},{8,0},{10,2},{12,4},{14,6},{1,9},{3,11}... | collective-permute-start | bytes 344072 | tf_op jit(solution)/shard_map/ppermute | solution.py:408
  59.5 6.4 %base_chunk.7 = (f32[128,3584]{1,0:T(8,128)S(1)}, bf16[128,3584]{1,0:T(8,128)(2,1)S(1)}, f32[128,64]{1,0:T(8,128)S(1)}) custom-call(f32[128,3584]{1,0:T(8,128)S(1)} %get-tuple-element.104.refs_0_, bf16[128,3584]{1,0:T(8,128)(2,1)S(1)} %get-tuple-element.105.refs_1_, ...), custom_call_target="tpu_custom_call", output_to_operand_aliasing={{0}: (0, {}), {1}: (1, {})} | custom-call | tf_op jit(solution)/shard_map/base_chunk/pallas_call | solution.py:239
  68.2 1.3 %collective-permute-done.13.receive_ref = f32[256,64]{1,0:T(8,128)S(1)} collective-permute-done((f32[256,64]{1,0:T(8,128)S(1)}, f32[256,64]{1,0:T(8,128)S(1)}, u32[]{:S(2)}, u32[]{:S(2)}) %collective-permute-start.13) | collective-permute-done | bytes 65568 | tf_op jit(solution)/shard_map/ppermute | solution.py:389
  69.6 1.6 %collective-permute-start.14 = (bf16[256,64]{1,0:T(8,128)(2,1)S(1)}, bf16[256,64]{1,0:T(8,128)(2,1)S(1)}, u32[]{:S(2)}, u32[]{:S(2)}) collective-permute-start(bf16[256,64]{1,0:T(8,128)(2,1)S(1)} %low_own.1.one_ref), channel_id=1, source_target_pairs={{0,2},{2,0},{4,6},{6,4},{8,10},{10,8},{12,14},{14,12},{1,3},{3,1},... | collective-permute-start | bytes 98312 | tf_op jit(solution)/shard_map/ppermute | solution.py:389
  71.2 4.1 %base_chunk.8 = (f32[128,3584]{1,0:T(8,128)S(1)}, bf16[128,3584]{1,0:T(8,128)(2,1)S(1)}) custom-call(f32[128,3584]{1,0:T(8,128)S(1)} %get-tuple-element.149.refs_0_, bf16[128,3584]{1,0:T(8,128)(2,1)S(1)} %get-tuple-element.150.refs_1_, bf16[4096,2560]{1,0:T(8,128)(2,1)S(1)} %get-tuple-element.91.refs_0_.refs_2_, ...), custom_call_target="tpu_custom_call", output_to_operand_aliasing={{0}: (0, {}), {1}: (1, {})} | custom-call | tf_op jit(solution)/shard_map/base_chunk/pallas_call | solution.py:239
  77.2 3.1 %collective-permute-start.20 = (bf16[256,64]{1,0:T(8,128)(2,1)S(1)}, bf16[256,64]{1,0:T(8,128)(2,1)S(1)}, u32[]{:S(2)}, u32[]{:S(2)}) collective-permute-start(bf16[256,64]{1,0:T(8,128)(2,1)S(1)} %add.1.refs_13_), channel_id=1, source_target_pairs={{0,12},{2,14},{4,0},{6,2},{8,4},{10,6},{12,8},{14,10},{1,13},{3,15... | collective-permute-start | bytes 98312 | tf_op jit(solution)/shard_map/ppermute | solution.py:408
  81.2 4.9 %base_chunk.9 = (f32[128,3584]{1,0:T(8,128)S(1)}, bf16[128,3584]{1,0:T(8,128)(2,1)S(1)}) custom-call(f32[128,3584]{1,0:T(8,128)S(1)} %get-tuple-element.158.refs_0_, bf16[128,3584]{1,0:T(8,128)(2,1)S(1)} %get-tuple-element.159.refs_1_, bf16[4096,2560]{1,0:T(8,128)(2,1)S(1)} %get-tuple-element.91.refs_0_.refs_2_, ...), custom_call_target="tpu_custom_call", output_to_operand_aliasing={{0}: (0, {}), {1}: (1, {})} | custom-call | tf_op jit(solution)/shard_map/base_chunk/pallas_call | solution.py:239
  86.2 1.4 %collective-permute-done.19.refs_15_ = bf16[256,64]{1,0:T(8,128)(2,1)S(1)} collective-permute-done((bf16[256,64]{1,0:T(8,128)(2,1)S(1)}, bf16[256,64]{1,0:T(8,128)(2,1)S(1)}, u32[]{:S(2)}, u32[]{:S(2)}) %collective-permute-start.19) | collective-permute-done | bytes 32800 | tf_op jit(solution)/shard_map/ppermute | solution.py:408
  88.7 2.3 %collective-permute-done.25.refs_11_ = bf16[5,16,3584]{2,1,0:T(8,128)(2,1)S(1)} collective-permute-done((bf16[5,16,3584]{2,1,0:T(8,128)(2,1)S(1)}, bf16[5,16,3584]{2,1,0:T(8,128)(2,1)S(1)}, u32[]{:S(2)}, u32[]{:S(2)}) %collective-permute-start.25) | collective-permute-done | bytes 573472 | tf_op jit(solution)/shard_map/ppermute | solution.py:389
  91.5 3.0 %finish.1 = bf16[256,3584]{1,0:T(8,128)(2,1)} custom-call(f32[128,3584]{1,0:T(8,128)S(1)} %get-tuple-element.130.refs_0_, f32[128,3584]{1,0:T(8,128)S(1)} %get-tuple-element.165.refs_1_, bf16[128,3584]{1,0:T(8,128)(2,1)S(1)} %collective-permute-done.23.refs_2_, bf16[128,3584]{1,0:T(8,128)(2,1)S(1)} %collective-permute-done.24.refs_3_, ...), custom_call_target="tpu_custom_call" | custom-call | tf_op jit(solution)/shard_map/finish/pallas_call | solution.py:371
  (52 shorter events, 13.8 us)
Async XLA Ops:
  0.0 19.6 %collective-permute-start = (bf16[64,4096]{1,0:T(8,128)(2,1)}, bf16[64,4096]{1,0:T(8,128)(2,1)S(1)}, u32[]{:S(2)}, u32[]{:S(2)}) collective-permute-start(bf16[64,4096]{1,0:T(8,128)(2,1)} %refs_2_), channel_id=1, source_target_pairs={{0,4},{2,6},{4,8},{6,10},{8,12},{10,14},{12,0},{14,2},{1,5},{3,7},... | collective-permute-start | bytes 1572872 | tf_op jit(solution)/shard_map/ppermute | solution.py:408
  3.0 16.6 %collective-permute-start.1 = (bf16[64,4096]{1,0:T(8,128)(2,1)}, bf16[64,4096]{1,0:T(8,128)(2,1)S(1)}, u32[]{:S(2)}, u32[]{:S(2)}) collective-permute-start(bf16[64,4096]{1,0:T(8,128)(2,1)} %refs_2_), channel_id=1, source_target_pairs={{0,2},{2,0},{4,6},{6,4},{8,10},{10,8},{12,14},{14,12},{1,3},{3,1},... | collective-permute-start | bytes 1572872 | tf_op jit(solution)/shard_map/ppermute | solution.py:389
  5.9 13.8 %collective-permute-start.2 = (bf16[16,3584]{1,0:T(8,128)(2,1)S(1)}, bf16[16,3584]{1,0:T(8,128)(2,1)S(1)}, u32[]{:S(2)}, u32[]{:S(2)}) collective-permute-start(bf16[16,3584]{1,0:T(8,128)(2,1)S(1)} %get-tuple-element.93), channel_id=1, source_target_pairs={{0,4},{2,6},{4,8},{6,10},{8,12},{10,14},{12,0},{14,2},{1,5},{3,7},... | collective-permute-start | bytes 344072 | tf_op jit(solution)/shard_map/ppermute | solution.py:408
  7.5 12.1 %collective-permute-start.3 = (bf16[16,3584]{1,0:T(8,128)(2,1)S(1)}, bf16[16,3584]{1,0:T(8,128)(2,1)S(1)}, u32[]{:S(2)}, u32[]{:S(2)}) collective-permute-start(bf16[16,3584]{1,0:T(8,128)(2,1)S(1)} %get-tuple-element.94), channel_id=1, source_target_pairs={{0,2},{2,0},{4,6},{6,4},{8,10},{10,8},{12,14},{14,12},{1,3},{3,1},... | collective-permute-start | bytes 344072 | tf_op jit(solution)/shard_map/ppermute | solution.py:408
  19.7 18.6 %collective-permute-start.5 = (bf16[64,4096]{1,0:T(8,128)(2,1)S(1)}, bf16[64,4096]{1,0:T(8,128)(2,1)S(1)}, u32[]{:S(2)}, u32[]{:S(2)}) collective-permute-start(bf16[64,4096]{1,0:T(8,128)(2,1)S(1)} %collective-permute-done.refs_2_), channel_id=1, source_target_pairs={{0,2},{2,0},{4,6},{6,4},{8,10},{10,8},{12,14},{14,12},{1,3},{3,1},... | collective-permute-start | bytes 1572872 | tf_op jit(solution)/shard_map/ppermute | solution.py:389
  21.2 17.0 %collective-permute-start.4 = (bf16[64,4096]{1,0:T(8,128)(2,1)S(1)}, bf16[64,4096]{1,0:T(8,128)(2,1)S(1)}, u32[]{:S(2)}, u32[]{:S(2)}) collective-permute-start(bf16[64,4096]{1,0:T(8,128)(2,1)S(1)} %collective-permute-done.refs_2_), channel_id=1, source_target_pairs={{0,4},{2,6},{4,8},{6,10},{8,12},{10,14},{12,0},{14,2},{1,5},{3,7},... | collective-permute-start | bytes 1572872 | tf_op jit(solution)/shard_map/ppermute | solution.py:408
  22.2 16.1 %collective-permute-start.6 = (bf16[16,3584]{1,0:T(8,128)(2,1)S(1)}, bf16[16,3584]{1,0:T(8,128)(2,1)S(1)}, u32[]{:S(2)}, u32[]{:S(2)}) collective-permute-start(bf16[16,3584]{1,0:T(8,128)(2,1)S(1)} %get-tuple-element.110), channel_id=1, source_target_pairs={{0,6},{2,4},{4,10},{6,8},{8,14},{10,12},{12,2},{14,0},{1,7},{3,5},... | collective-permute-start | bytes 344072 | tf_op jit(solution)/shard_map/ppermute | solution.py:408
  38.3 14.4 %collective-permute-start.8 = (bf16[64,4096]{1,0:T(8,128)(2,1)S(1)}, bf16[64,4096]{1,0:T(8,128)(2,1)S(1)}, u32[]{:S(2)}, u32[]{:S(2)}) collective-permute-start(bf16[64,4096]{1,0:T(8,128)(2,1)S(1)} %collective-permute-done.4.refs_4_), channel_id=1, source_target_pairs={{0,2},{2,0},{4,6},{6,4},{8,10},{10,8},{12,14},{14,12},{1,3},{3,1},... | collective-permute-start | bytes 1572872 | tf_op jit(solution)/shard_map/ppermute | solution.py:389
  39.5 14.2 %collective-permute-start.7 = (bf16[64,4096]{1,0:T(8,128)(2,1)S(1)}, bf16[64,4096]{1,0:T(8,128)(2,1)S(1)}, u32[]{:S(2)}, u32[]{:S(2)}) collective-permute-start(bf16[64,4096]{1,0:T(8,128)(2,1)S(1)} %collective-permute-done.4.refs_4_), channel_id=1, source_target_pairs={{0,4},{2,6},{4,8},{6,10},{8,12},{10,14},{12,0},{14,2},{1,5},{3,7},... | collective-permute-start | bytes 1572872 | tf_op jit(solution)/shard_map/ppermute | solution.py:408
  39.6 12.2 %collective-permute-start.9 = (bf16[16,3584]{1,0:T(8,128)(2,1)S(1)}, bf16[16,3584]{1,0:T(8,128)(2,1)S(1)}, u32[]{:S(2)}, u32[]{:S(2)}) collective-permute-start(bf16[16,3584]{1,0:T(8,128)(2,1)S(1)} %get-tuple-element.121), channel_id=1, source_target_pairs={{0,14},{2,12},{4,2},{6,0},{8,6},{10,4},{12,10},{14,8},{1,15},{3,13... | collective-permute-start | bytes 344072 | tf_op jit(solution)/shard_map/ppermute | solution.py:408
  53.7 13.1 %collective-permute-start.10 = (bf16[64,4096]{1,0:T(8,128)(2,1)S(1)}, bf16[64,4096]{1,0:T(8,128)(2,1)S(1)}, u32[]{:S(2)}, u32[]{:S(2)}) collective-permute-start(bf16[64,4096]{1,0:T(8,128)(2,1)S(1)} %collective-permute-done.7.refs_0_.refs_4_), channel_id=1, source_target_pairs={{0,2},{2,0},{4,6},{6,4},{8,10},{10,8},{12,14},{14,12},{1,3},{3,1},... | collective-permute-start | bytes 1572872 | tf_op jit(solution)/shard_map/ppermute | solution.py:389
  55.5 19.9 %collective-permute-start.17 = (bf16[5,16,3584]{2,1,0:T(8,128)(2,1)S(1)}, bf16[5,16,3584]{2,1,0:T(8,128)(2,1)S(1)}, u32[]{:S(2)}, u32[]{:S(2)}) collective-permute-start(bf16[5,16,3584]{2,1,0:T(8,128)(2,1)S(1)} %stack.2.refs_5_), channel_id=1, source_target_pairs={{0,1},{1,0},{2,3},{3,2},{4,5},{5,4},{6,7},{7,6},{8,9},{9,8},{10,11... | collective-permute-start | bytes 1720328 | tf_op jit(solution)/shard_map/ppermute | solution.py:389
  55.5 19.8 %collective-permute-start.16 = (bf16[5,16,3584]{2,1,0:T(8,128)(2,1)S(1)}, bf16[5,16,3584]{2,1,0:T(8,128)(2,1)S(1)}, u32[]{:S(2)}, u32[]{:S(2)}) collective-permute-start(bf16[5,16,3584]{2,1,0:T(8,128)(2,1)S(1)} %stack.2.refs_5_), channel_id=1, source_target_pairs={{0,16},{16,0},{1,17},{17,1},{2,18},{18,2},{3,19},{19,3},{4,20},{20... | collective-permute-start | bytes 1720328 | tf_op jit(solution)/shard_map/ppermute | solution.py:389
  56.7 9.3 %collective-permute-start.11 = (bf16[16,3584]{1,0:T(8,128)(2,1)S(1)}, bf16[16,3584]{1,0:T(8,128)(2,1)S(1)}, u32[]{:S(2)}, u32[]{:S(2)}) collective-permute-start(bf16[16,3584]{1,0:T(8,128)(2,1)S(1)} %get-tuple-element.137), channel_id=1, source_target_pairs={{0,8},{2,10},{4,12},{6,14},{8,0},{10,2},{12,4},{14,6},{1,9},{3,11}... | collective-permute-start | bytes 344072 | tf_op jit(solution)/shard_map/ppermute | solution.py:408
  59.5 7.3 %collective-permute-start.12 = (bf16[16,3584]{1,0:T(8,128)(2,1)S(1)}, bf16[16,3584]{1,0:T(8,128)(2,1)S(1)}, u32[]{:S(2)}, u32[]{:S(2)}) collective-permute-start(bf16[16,3584]{1,0:T(8,128)(2,1)S(1)} %get-tuple-element.138), channel_id=1, source_target_pairs={{0,12},{2,14},{4,0},{6,2},{8,4},{10,6},{12,8},{14,10},{1,13},{3,15... | collective-permute-start | bytes 344072 | tf_op jit(solution)/shard_map/ppermute | solution.py:408
  66.8 8.9 %collective-permute-start.15 = (bf16[16,3584]{1,0:T(8,128)(2,1)S(1)}, bf16[16,3584]{1,0:T(8,128)(2,1)S(1)}, u32[]{:S(2)}, u32[]{:S(2)}) collective-permute-start(bf16[16,3584]{1,0:T(8,128)(2,1)S(1)} %get-tuple-element.155), channel_id=1, source_target_pairs={{0,10},{2,8},{4,14},{6,12},{8,2},{10,0},{12,6},{14,4},{1,11},{3,9}... | collective-permute-start | bytes 344072 | tf_op jit(solution)/shard_map/ppermute | solution.py:408
  69.6 5.7 %collective-permute-start.14 = (bf16[256,64]{1,0:T(8,128)(2,1)S(1)}, bf16[256,64]{1,0:T(8,128)(2,1)S(1)}, u32[]{:S(2)}, u32[]{:S(2)}) collective-permute-start(bf16[256,64]{1,0:T(8,128)(2,1)S(1)} %low_own.1.one_ref), channel_id=1, source_target_pairs={{0,2},{2,0},{4,6},{6,4},{8,10},{10,8},{12,14},{14,12},{1,3},{3,1},... | collective-permute-start | bytes 98312 | tf_op jit(solution)/shard_map/ppermute | solution.py:389
  76.2 11.5 %collective-permute-start.22 = (bf16[3,16,3584]{2,1,0:T(8,128)(2,1)S(1)}, bf16[3,16,3584]{2,1,0:T(8,128)(2,1)S(1)}, u32[]{:S(2)}, u32[]{:S(2)}) collective-permute-start(bf16[3,16,3584]{2,1,0:T(8,128)(2,1)S(1)} %stack.3.refs_6_), channel_id=1, source_target_pairs={{0,1},{1,0},{2,3},{3,2},{4,5},{5,4},{6,7},{7,6},{8,9},{9,8},{10,11... | collective-permute-start | bytes 1032200 | tf_op jit(solution)/shard_map/ppermute | solution.py:389
  76.3 11.4 %collective-permute-start.21 = (bf16[3,16,3584]{2,1,0:T(8,128)(2,1)S(1)}, bf16[3,16,3584]{2,1,0:T(8,128)(2,1)S(1)}, u32[]{:S(2)}, u32[]{:S(2)}) collective-permute-start(bf16[3,16,3584]{2,1,0:T(8,128)(2,1)S(1)} %stack.3.refs_6_), channel_id=1, source_target_pairs={{0,16},{16,0},{1,17},{17,1},{2,18},{18,2},{3,19},{19,3},{4,20},{20... | collective-permute-start | bytes 1032200 | tf_op jit(solution)/shard_map/ppermute | solution.py:389
  77.2 9.0 %collective-permute-start.20 = (bf16[256,64]{1,0:T(8,128)(2,1)S(1)}, bf16[256,64]{1,0:T(8,128)(2,1)S(1)}, u32[]{:S(2)}, u32[]{:S(2)}) collective-permute-start(bf16[256,64]{1,0:T(8,128)(2,1)S(1)} %add.1.refs_13_), channel_id=1, source_target_pairs={{0,12},{2,14},{4,0},{6,2},{8,4},{10,6},{12,8},{14,10},{1,13},{3,15... | collective-permute-start | bytes 98312 | tf_op jit(solution)/shard_map/ppermute | solution.py:408
  80.2 7.4 %collective-permute-start.19 = (bf16[256,64]{1,0:T(8,128)(2,1)S(1)}, bf16[256,64]{1,0:T(8,128)(2,1)S(1)}, u32[]{:S(2)}, u32[]{:S(2)}) collective-permute-start(bf16[256,64]{1,0:T(8,128)(2,1)S(1)} %add.1.refs_13_), channel_id=1, source_target_pairs={{0,8},{2,10},{4,12},{6,14},{8,0},{10,2},{12,4},{14,6},{1,9},{3,11}... | collective-permute-start | bytes 98312 | tf_op jit(solution)/shard_map/ppermute | solution.py:408
  81.2 6.5 %collective-permute-start.18 = (bf16[256,64]{1,0:T(8,128)(2,1)S(1)}, bf16[256,64]{1,0:T(8,128)(2,1)S(1)}, u32[]{:S(2)}, u32[]{:S(2)}) collective-permute-start(bf16[256,64]{1,0:T(8,128)(2,1)S(1)} %add.1.refs_13_), channel_id=1, source_target_pairs={{0,4},{2,6},{4,8},{6,10},{8,12},{10,14},{12,0},{14,2},{1,5},{3,7},... | collective-permute-start | bytes 98312 | tf_op jit(solution)/shard_map/ppermute | solution.py:408
  87.7 3.9 %collective-permute-start.24 = (bf16[128,3584]{1,0:T(8,128)(2,1)S(1)}, bf16[128,3584]{1,0:T(8,128)(2,1)S(1)}, u32[]{:S(2)}, u32[]{:S(2)}) collective-permute-start(bf16[128,3584]{1,0:T(8,128)(2,1)S(1)} %get-tuple-element.167), channel_id=1, source_target_pairs={{0,1},{1,0},{2,3},{3,2},{4,5},{5,4},{6,7},{7,6},{8,9},{9,8},{10,11... | collective-permute-start | bytes 2752520 | tf_op jit(solution)/shard_map/ppermute | solution.py:389
  87.8 3.3 %collective-permute-start.25 = (bf16[5,16,3584]{2,1,0:T(8,128)(2,1)S(1)}, bf16[5,16,3584]{2,1,0:T(8,128)(2,1)S(1)}, u32[]{:S(2)}, u32[]{:S(2)}) collective-permute-start(bf16[5,16,3584]{2,1,0:T(8,128)(2,1)S(1)} %collective-permute-done.16.refs_7_), channel_id=1, source_target_pairs={{0,1},{1,0},{2,3},{3,2},{4,5},{5,4},{6,7},{7,6},{8,9},{9,8},{10,11... | collective-permute-start | bytes 1720328 | tf_op jit(solution)/shard_map/ppermute | solution.py:389
  (7 other events, 55.1 us)

commit v5 on v4

--- a/solution.py
+++ b/solution.py
@@ -166,6 +166,7 @@
     piece = tile // 2
     pieces = 2 * (PARTS - HELD)
     assert pieces < HELD
+    slots = pieces if tiles == "streamed" else 2
     half = 2 * shard
     inputs = in_vmem(*pair, held) + [gate, near, far]
     outputs = [pltpu.VMEM((half, width), F32), pltpu.VMEM((half, width), BF16)]
@@ -183,7 +184,7 @@
 
         def fetch(i):
             begin = pl.multiple_of(HELD * tile + i * piece, piece)
-            slot = lax.rem(i, 2)
+            slot = lax.rem(i, slots)
             return pltpu.make_async_copy(
                 gate_ref.at[:, pl.ds(begin, piece)], piece_ref.at[slot], sem.at[slot]
             )
@@ -202,8 +203,8 @@
         @pl.when(at == 0)
         def _():
             if tiles != "held":
-                fetch(0).start()
-                fetch(1).start()
+                for i in range(slots):
+                    fetch(i).start()
             load_rows(near_ref, far_ref, rows_ref)
             if down is not None:
                 out_refs[-1][...] = lax.dot_general(
@@ -228,13 +229,13 @@
             def _():
                 fetch(turn).wait()
                 total = jnp.dot(
-                    rows_ref[...], piece_ref[lax.rem(turn, 2)], preferred_element_type=F32
+                    rows_ref[...], piece_ref[lax.rem(turn, slots)], preferred_element_type=F32
                 )
                 put(HELD * tile + turn * piece, piece, total)
 
-                @pl.when(turn + 2 < pieces)
+                @pl.when(turn + slots < pieces)
                 def _():
-                    fetch(turn + 2).start()
+                    fetch(turn + slots).start()
 
     return pl.pallas_call(
         kernel,
@@ -244,11 +245,11 @@
         out_shape=outputs,
         scratch_shapes=[
             pltpu.VMEM((half, depth), BF16),
-            pltpu.VMEM((2, depth, piece), BF16),
-            pltpu.SemaphoreType.DMA((2,)),
+            pltpu.VMEM((slots, depth, piece), BF16),
+            pltpu.SemaphoreType.DMA((slots,)),
         ],
         input_output_aliases={0: 0, 1: 1} if pair else {},
-        compiler_params=params(10),
+        compiler_params=params(14 if tiles == "streamed" else 10),
         name="base_chunk",
     )(*inputs)
 
@@ -466,15 +467,16 @@
     last = levels - 1
     move_blocks(late)
     low_keep, low_send = low_last(near, far, down, lows, levels)
+    low_send, first_x = together((low_send, first_x))
+    first_xc = other_core(first_x)
     low = low_own(low_keep, other_core(low_send), store_row)
 
     crossed = along_y(low)
     multiply(last, near, far, None, tiles="held")
     moved = [blocks[offset] for offset in second_offsets]
-    low, crossed, pair_left[last % pairs], moved, first, first_x, first_c = together(
-        (low, crossed, pair_left[last % pairs], moved, first, first_x, first_c)
+    low, crossed, pair_left[last % pairs], moved, first, first_xc, first_c = together(
+        (low, crossed, pair_left[last % pairs], moved, first, first_xc, first_c)
     )
-    first_xc = other_core(first_x)
     second = stack(moved)
     second_x, second_c = other_group(second), other_core(second)
     low = add(low, crossed)

time: 94.7 us -> 93.3 us (0.985)
  Pallas kernels: 42.3 us -> 40.3 us
    pallas_call x5, Pallas kernels: 28.3 us -> 26.3 us  [base_chunk(): pl.pallas_call(kernel, grid=(pieces if tiles == 'streamed' else HELD,), i...]
    ppermute x13, waiting for transfers between devices: 17.2 us -> 18.3 us  [along_mp(): return lax.ppermute(value, 'mp', pairs_of)]
  transfers between devices with their start and end apart: 27 -> 27, of which waited for: 12 -> 11; matrix products, arithmetic and copies ran while one was open for 0% -> 0% of each run, Pallas kernels for 41% -> 39%
where the time goes in v5:
time: 93.3 us; the launch traced here: 93.2 us
  Pallas kernels  40.3 us (43%)
  starting transfers between devices  29.6 us (32%)
  waiting for transfers between devices  23.1 us (25%)
    pallas_call x5, Pallas kernels, base_chunk(): pl.pallas_call(kernel, grid=(pieces if tiles == 'streamed' else HELD,), i...  26.3 us
    ppermute x13, starting transfers between devices, along_mp(): return lax.ppermute(value, 'mp', pairs_of)  20.2 us
    ppermute x13, waiting for transfers between devices, along_mp(): return lax.ppermute(value, 'mp', pairs_of)  18.3 us
    ppermute x14, starting transfers between devices, move(): return lax.ppermute(value, axis, [(i, i ^ 1) for i in range(size)])  9.4 us
    pallas_call x1, Pallas kernels, hold_gate(): pl.pallas_call(kernel, in_specs=[ANY], out_specs=[VMEM, VMEM], out_shape=...  7.11 us
    ppermute x14, waiting for transfers between devices, move(): return lax.ppermute(value, axis, [(i, i ^ 1) for i in range(size)])  4.73 us
    pallas_call x1, Pallas kernels, finish(): pl.pallas_call(kernel, grid=(width // tile,), in_specs=[VMEM] * pairs + [...  2.99 us
  transfers between devices with their start and end apart: 27, of which 11 were waited for; matrix products, arithmetic and copies ran while one was open for 0% of the time, Pallas kernels for 39%

profile of v5, /device:TPU:0, one launch (start us, length us, event | category | flops | bytes accessed | tf_op | source)
XLA Modules:
  0.0 93.2 jit_solution(4590739895721929275)
XLA Ops:
  0.0 3.0 %collective-permute-start = (bf16[64,4096]{1,0:T(8,128)(2,1)}, bf16[64,4096]{1,0:T(8,128)(2,1)S(1)}, u32[]{:S(2)}, u32[]{:S(2)}) collective-permute-start(bf16[64,4096]{1,0:T(8,128)(2,1)} %refs_2_), channel_id=1, source_target_pairs={{0,4},{2,6},{4,8},{6,10},{8,12},{10,14},{12,0},{14,2},{1,5},{3,7},... | collective-permute-start | bytes 1572872 | tf_op jit(solution)/shard_map/ppermute | solution.py:409
  3.0 1.5 %collective-permute-start.1 = (bf16[64,4096]{1,0:T(8,128)(2,1)}, bf16[64,4096]{1,0:T(8,128)(2,1)S(1)}, u32[]{:S(2)}, u32[]{:S(2)}) collective-permute-start(bf16[64,4096]{1,0:T(8,128)(2,1)} %refs_2_), channel_id=1, source_target_pairs={{0,2},{2,0},{4,6},{6,4},{8,10},{10,8},{12,14},{14,12},{1,3},{3,1},... | collective-permute-start | bytes 1572872 | tf_op jit(solution)/shard_map/ppermute | solution.py:390
  4.5 1.3 %split_panels.1 = (bf16[16,3584]{1,0:T(8,128)(2,1)S(1)}, bf16[16,3584]{1,0:T(8,128)(2,1)S(1)}, bf16[16,3584]{1,0:T(8,128)(2,1)S(1)}, bf16[16,3584]{1,0:T(8,128)(...) custom-call(bf16[1,64,28672]{2,1,0:T(8,128)(2,1)} %up_ref.1), custom_call_target="tpu_custom_call" | custom-call | tf_op jit(solution)/shard_map/split_panels/pallas_call | solution.py:82
  5.9 1.6 %collective-permute-start.2 = (bf16[16,3584]{1,0:T(8,128)(2,1)S(1)}, bf16[16,3584]{1,0:T(8,128)(2,1)S(1)}, u32[]{:S(2)}, u32[]{:S(2)}) collective-permute-start(bf16[16,3584]{1,0:T(8,128)(2,1)S(1)} %get-tuple-element.95), channel_id=1, source_target_pairs={{0,4},{2,6},{4,8},{6,10},{8,12},{10,14},{12,0},{14,2},{1,5},{3,7},... | collective-permute-start | bytes 344072 | tf_op jit(solution)/shard_map/ppermute | solution.py:409
  8.1 7.1 %hold_gate.1 = (bf16[4096,2560]{1,0:T(8,128)(2,1)S(1)}, f32[8,128]{1,0:T(8,128)S(1)}) custom-call(bf16[4096,3584]{1,0:T(8,128)(2,1)} %refs_3_.5), custom_call_target="tpu_custom_call" | custom-call | tf_op jit(solution)/shard_map/hold_gate/pallas_call | solution.py:134
  16.0 3.7 %collective-permute-done.2.refs_1_ = bf16[16,3584]{1,0:T(8,128)(2,1)S(1)} collective-permute-done((bf16[16,3584]{1,0:T(8,128)(2,1)S(1)}, bf16[16,3584]{1,0:T(8,128)(2,1)S(1)}, u32[]{:S(2)}, u32[]{:S(2)}) %collective-permute-start.2) | collective-permute-done | bytes 114720 | tf_op jit(solution)/shard_map/ppermute | solution.py:409
  19.7 1.6 %collective-permute-start.5 = (bf16[64,4096]{1,0:T(8,128)(2,1)S(1)}, bf16[64,4096]{1,0:T(8,128)(2,1)S(1)}, u32[]{:S(2)}, u32[]{:S(2)}) collective-permute-start(bf16[64,4096]{1,0:T(8,128)(2,1)S(1)} %collective-permute-done.refs_2_), channel_id=1, source_target_pairs={{0,2},{2,0},{4,6},{6,4},{8,10},{10,8},{12,14},{14,12},{1,3},{3,1},... | collective-permute-start | bytes 1572872 | tf_op jit(solution)/shard_map/ppermute | solution.py:390
  22.2 1.5 %collective-permute-start.6 = (bf16[16,3584]{1,0:T(8,128)(2,1)S(1)}, bf16[16,3584]{1,0:T(8,128)(2,1)S(1)}, u32[]{:S(2)}, u32[]{:S(2)}) collective-permute-start(bf16[16,3584]{1,0:T(8,128)(2,1)S(1)} %get-tuple-element.112), channel_id=1, source_target_pairs={{0,6},{2,4},{4,10},{6,8},{8,14},{10,12},{12,2},{14,0},{1,7},{3,5},... | collective-permute-start | bytes 344072 | tf_op jit(solution)/shard_map/ppermute | solution.py:409
  23.7 6.1 %base_chunk.5 = (f32[128,3584]{1,0:T(8,128)S(1)}, bf16[128,3584]{1,0:T(8,128)(2,1)S(1)}, f32[128,64]{1,0:T(8,128)S(1)}) custom-call(bf16[4096,2560]{1,0:T(8,128)(2,1)S(1)} %get-tuple-element.93.refs_0_.refs_2_, bf16[4096,3584]{1,0:T(8,128)(2,1)} %refs_3_.5, bf16[64,4096]{1,0:T(8,128)(2,1)S(1)} %copy-done.1, ...), custom_call_target="tpu_custom_call" | custom-call | tf_op jit(solution)/shard_map/base_chunk/pallas_call | solution.py:240
  29.8 8.4 %collective-permute-done.6.refs_3_ = bf16[16,3584]{1,0:T(8,128)(2,1)S(1)} collective-permute-done((bf16[16,3584]{1,0:T(8,128)(2,1)S(1)}, bf16[16,3584]{1,0:T(8,128)(2,1)S(1)}, u32[]{:S(2)}, u32[]{:S(2)}) %collective-permute-start.6) | collective-permute-done | bytes 114720 | tf_op jit(solution)/shard_map/ppermute | solution.py:409
  39.6 4.0 %collective-permute-start.9 = (bf16[16,3584]{1,0:T(8,128)(2,1)S(1)}, bf16[16,3584]{1,0:T(8,128)(2,1)S(1)}, u32[]{:S(2)}, u32[]{:S(2)}) collective-permute-start(bf16[16,3584]{1,0:T(8,128)(2,1)S(1)} %get-tuple-element.123), channel_id=1, source_target_pairs={{0,14},{2,12},{4,2},{6,0},{8,6},{10,4},{12,10},{14,8},{1,15},{3,13... | collective-permute-start | bytes 344072 | tf_op jit(solution)/shard_map/ppermute | solution.py:409
  43.6 6.1 %base_chunk.6 = (f32[128,3584]{1,0:T(8,128)S(1)}, bf16[128,3584]{1,0:T(8,128)(2,1)S(1)}, f32[128,64]{1,0:T(8,128)S(1)}) custom-call(bf16[4096,2560]{1,0:T(8,128)(2,1)S(1)} %get-tuple-element.93.refs_0_.refs_2_, bf16[4096,3584]{1,0:T(8,128)(2,1)} %refs_3_.5, bf16[64,4096]{1,0:T(8,128)(2,1)S(1)} %collective-permute-done.refs_2_, ...), custom_call_target="tpu_custom_call" | custom-call | tf_op jit(solution)/shard_map/base_chunk/pallas_call | solution.py:240
  49.7 2.1 %collective-permute-done.9.refs_4_ = bf16[16,3584]{1,0:T(8,128)(2,1)S(1)} collective-permute-done((bf16[16,3584]{1,0:T(8,128)(2,1)S(1)}, bf16[16,3584]{1,0:T(8,128)(2,1)S(1)}, u32[]{:S(2)}, u32[]{:S(2)}) %collective-permute-start.9) | collective-permute-done | bytes 114720 | tf_op jit(solution)/shard_map/ppermute | solution.py:409
  52.3 1.4 %collective-permute-done.7.refs_0_.refs_4_ = bf16[64,4096]{1,0:T(8,128)(2,1)S(1)} collective-permute-done((bf16[64,4096]{1,0:T(8,128)(2,1)S(1)}, bf16[64,4096]{1,0:T(8,128)(2,1)S(1)}, u32[]{:S(2)}, u32[]{:S(2)}) %collective-permute-start.7) | collective-permute-done | bytes 524320 | tf_op jit(solution)/shard_map/ppermute | solution.py:409
  54.5 2.0 %collective-permute-start.13 = (bf16[5,16,3584]{2,1,0:T(8,128)(2,1)S(1)}, bf16[5,16,3584]{2,1,0:T(8,128)(2,1)S(1)}, u32[]{:S(2)}, u32[]{:S(2)}) collective-permute-start(bf16[5,16,3584]{2,1,0:T(8,128)(2,1)S(1)} %stack.2.refs_5_), channel_id=1, source_target_pairs={{0,16},{16,0},{1,17},{17,1},{2,18},{18,2},{3,19},{19,3},{4,20},{20... | collective-permute-start | bytes 1720328 | tf_op jit(solution)/shard_map/ppermute | solution.py:390
  56.6 3.0 %collective-permute-start.11 = (bf16[16,3584]{1,0:T(8,128)(2,1)S(1)}, bf16[16,3584]{1,0:T(8,128)(2,1)S(1)}, u32[]{:S(2)}, u32[]{:S(2)}) collective-permute-start(bf16[16,3584]{1,0:T(8,128)(2,1)S(1)} %get-tuple-element.139), channel_id=1, source_target_pairs={{0,8},{2,10},{4,12},{6,14},{8,0},{10,2},{12,4},{14,6},{1,9},{3,11}... | collective-permute-start | bytes 344072 | tf_op jit(solution)/shard_map/ppermute | solution.py:409
  59.5 6.1 %base_chunk.7 = (f32[128,3584]{1,0:T(8,128)S(1)}, bf16[128,3584]{1,0:T(8,128)(2,1)S(1)}, f32[128,64]{1,0:T(8,128)S(1)}) custom-call(f32[128,3584]{1,0:T(8,128)S(1)} %get-tuple-element.106.refs_0_, bf16[128,3584]{1,0:T(8,128)(2,1)S(1)} %get-tuple-element.107.refs_1_, ...), custom_call_target="tpu_custom_call", output_to_operand_aliasing={{0}: (0, {}), {1}: (1, {})} | custom-call | tf_op jit(solution)/shard_map/base_chunk/pallas_call | solution.py:240
  66.8 2.3 %collective-permute-start.16 = (bf16[16,3584]{1,0:T(8,128)(2,1)S(1)}, bf16[16,3584]{1,0:T(8,128)(2,1)S(1)}, u32[]{:S(2)}, u32[]{:S(2)}) collective-permute-start(bf16[16,3584]{1,0:T(8,128)(2,1)S(1)} %get-tuple-element.158), channel_id=1, source_target_pairs={{0,10},{2,8},{4,14},{6,12},{8,2},{10,0},{12,6},{14,4},{1,11},{3,9}... | collective-permute-start | bytes 344072 | tf_op jit(solution)/shard_map/ppermute | solution.py:409
  71.3 3.8 %base_chunk.8 = (f32[128,3584]{1,0:T(8,128)S(1)}, bf16[128,3584]{1,0:T(8,128)(2,1)S(1)}) custom-call(f32[128,3584]{1,0:T(8,128)S(1)} %get-tuple-element.152.refs_0_, bf16[128,3584]{1,0:T(8,128)(2,1)S(1)} %get-tuple-element.153.refs_1_, bf16[4096,2560]{1,0:T(8,128)(2,1)S(1)} %get-tuple-element.93.refs_0_.refs_2_, ...), custom_call_target="tpu_custom_call", output_to_operand_aliasing={{0}: (0, {}), {1}: (1, {})} | custom-call | tf_op jit(solution)/shard_map/base_chunk/pallas_call | solution.py:240
  77.6 2.2 %collective-permute-start.21 = (bf16[256,64]{1,0:T(8,128)(2,1)S(1)}, bf16[256,64]{1,0:T(8,128)(2,1)S(1)}, u32[]{:S(2)}, u32[]{:S(2)}) collective-permute-start(bf16[256,64]{1,0:T(8,128)(2,1)S(1)} %add.1.refs_13_), channel_id=1, source_target_pairs={{0,12},{2,14},{4,0},{6,2},{8,4},{10,6},{12,8},{14,10},{1,13},{3,15... | collective-permute-start | bytes 98312 | tf_op jit(solution)/shard_map/ppermute | solution.py:409
  80.8 4.0 %base_chunk.9 = (f32[128,3584]{1,0:T(8,128)S(1)}, bf16[128,3584]{1,0:T(8,128)(2,1)S(1)}) custom-call(f32[128,3584]{1,0:T(8,128)S(1)} %get-tuple-element.162.refs_0_, bf16[128,3584]{1,0:T(8,128)(2,1)S(1)} %get-tuple-element.163.refs_1_, bf16[4096,2560]{1,0:T(8,128)(2,1)S(1)} %get-tuple-element.93.refs_0_.refs_2_, ...), custom_call_target="tpu_custom_call", output_to_operand_aliasing={{0}: (0, {}), {1}: (1, {})} | custom-call | tf_op jit(solution)/shard_map/base_chunk/pallas_call | solution.py:240
  85.0 1.8 %collective-permute-done.20.refs_15_ = bf16[256,64]{1,0:T(8,128)(2,1)S(1)} collective-permute-done((bf16[256,64]{1,0:T(8,128)(2,1)S(1)}, bf16[256,64]{1,0:T(8,128)(2,1)S(1)}, u32[]{:S(2)}, u32[]{:S(2)}) %collective-permute-start.20) | collective-permute-done | bytes 32800 | tf_op jit(solution)/shard_map/ppermute | solution.py:409
  87.7 2.5 %collective-permute-done.26.refs_12_ = bf16[3,16,3584]{2,1,0:T(8,128)(2,1)S(1)} collective-permute-done((bf16[3,16,3584]{2,1,0:T(8,128)(2,1)S(1)}, bf16[3,16,3584]{2,1,0:T(8,128)(2,1)S(1)}, u32[]{:S(2)}, u32[]{:S(2)}) %collective-permute-start.26) | collective-permute-done | bytes 344096 | tf_op jit(solution)/shard_map/ppermute | solution.py:390
  90.2 3.0 %finish.1 = bf16[256,3584]{1,0:T(8,128)(2,1)} custom-call(f32[128,3584]{1,0:T(8,128)S(1)} %get-tuple-element.132.refs_0_, f32[128,3584]{1,0:T(8,128)S(1)} %get-tuple-element.169.refs_1_, bf16[128,3584]{1,0:T(8,128)(2,1)S(1)} %collective-permute-done.24.refs_2_, bf16[128,3584]{1,0:T(8,128)(2,1)S(1)} %collective-permute-done.25.refs_3_, ...), custom_call_target="tpu_custom_call" | custom-call | tf_op jit(solution)/shard_map/finish/pallas_call | solution.py:372
  (52 shorter events, 12.8 us)
Async XLA Ops:
  0.0 19.6 %collective-permute-start = (bf16[64,4096]{1,0:T(8,128)(2,1)}, bf16[64,4096]{1,0:T(8,128)(2,1)S(1)}, u32[]{:S(2)}, u32[]{:S(2)}) collective-permute-start(bf16[64,4096]{1,0:T(8,128)(2,1)} %refs_2_), channel_id=1, source_target_pairs={{0,4},{2,6},{4,8},{6,10},{8,12},{10,14},{12,0},{14,2},{1,5},{3,7},... | collective-permute-start | bytes 1572872 | tf_op jit(solution)/shard_map/ppermute | solution.py:409
  3.0 16.6 %collective-permute-start.1 = (bf16[64,4096]{1,0:T(8,128)(2,1)}, bf16[64,4096]{1,0:T(8,128)(2,1)S(1)}, u32[]{:S(2)}, u32[]{:S(2)}) collective-permute-start(bf16[64,4096]{1,0:T(8,128)(2,1)} %refs_2_), channel_id=1, source_target_pairs={{0,2},{2,0},{4,6},{6,4},{8,10},{10,8},{12,14},{14,12},{1,3},{3,1},... | collective-permute-start | bytes 1572872 | tf_op jit(solution)/shard_map/ppermute | solution.py:390
  5.9 13.8 %collective-permute-start.2 = (bf16[16,3584]{1,0:T(8,128)(2,1)S(1)}, bf16[16,3584]{1,0:T(8,128)(2,1)S(1)}, u32[]{:S(2)}, u32[]{:S(2)}) collective-permute-start(bf16[16,3584]{1,0:T(8,128)(2,1)S(1)} %get-tuple-element.95), channel_id=1, source_target_pairs={{0,4},{2,6},{4,8},{6,10},{8,12},{10,14},{12,0},{14,2},{1,5},{3,7},... | collective-permute-start | bytes 344072 | tf_op jit(solution)/shard_map/ppermute | solution.py:409
  7.5 12.1 %collective-permute-start.3 = (bf16[16,3584]{1,0:T(8,128)(2,1)S(1)}, bf16[16,3584]{1,0:T(8,128)(2,1)S(1)}, u32[]{:S(2)}, u32[]{:S(2)}) collective-permute-start(bf16[16,3584]{1,0:T(8,128)(2,1)S(1)} %get-tuple-element.96), channel_id=1, source_target_pairs={{0,2},{2,0},{4,6},{6,4},{8,10},{10,8},{12,14},{14,12},{1,3},{3,1},... | collective-permute-start | bytes 344072 | tf_op jit(solution)/shard_map/ppermute | solution.py:409
  19.7 18.6 %collective-permute-start.5 = (bf16[64,4096]{1,0:T(8,128)(2,1)S(1)}, bf16[64,4096]{1,0:T(8,128)(2,1)S(1)}, u32[]{:S(2)}, u32[]{:S(2)}) collective-permute-start(bf16[64,4096]{1,0:T(8,128)(2,1)S(1)} %collective-permute-done.refs_2_), channel_id=1, source_target_pairs={{0,2},{2,0},{4,6},{6,4},{8,10},{10,8},{12,14},{14,12},{1,3},{3,1},... | collective-permute-start | bytes 1572872 | tf_op jit(solution)/shard_map/ppermute | solution.py:390
  21.2 17.0 %collective-permute-start.4 = (bf16[64,4096]{1,0:T(8,128)(2,1)S(1)}, bf16[64,4096]{1,0:T(8,128)(2,1)S(1)}, u32[]{:S(2)}, u32[]{:S(2)}) collective-permute-start(bf16[64,4096]{1,0:T(8,128)(2,1)S(1)} %collective-permute-done.refs_2_), channel_id=1, source_target_pairs={{0,4},{2,6},{4,8},{6,10},{8,12},{10,14},{12,0},{14,2},{1,5},{3,7},... | collective-permute-start | bytes 1572872 | tf_op jit(solution)/shard_map/ppermute | solution.py:409
  22.2 16.1 %collective-permute-start.6 = (bf16[16,3584]{1,0:T(8,128)(2,1)S(1)}, bf16[16,3584]{1,0:T(8,128)(2,1)S(1)}, u32[]{:S(2)}, u32[]{:S(2)}) collective-permute-start(bf16[16,3584]{1,0:T(8,128)(2,1)S(1)} %get-tuple-element.112), channel_id=1, source_target_pairs={{0,6},{2,4},{4,10},{6,8},{8,14},{10,12},{12,2},{14,0},{1,7},{3,5},... | collective-permute-start | bytes 344072 | tf_op jit(solution)/shard_map/ppermute | solution.py:409
  38.3 14.1 %collective-permute-start.8 = (bf16[64,4096]{1,0:T(8,128)(2,1)S(1)}, bf16[64,4096]{1,0:T(8,128)(2,1)S(1)}, u32[]{:S(2)}, u32[]{:S(2)}) collective-permute-start(bf16[64,4096]{1,0:T(8,128)(2,1)S(1)} %collective-permute-done.4.refs_4_), channel_id=1, source_target_pairs={{0,2},{2,0},{4,6},{6,4},{8,10},{10,8},{12,14},{14,12},{1,3},{3,1},... | collective-permute-start | bytes 1572872 | tf_op jit(solution)/shard_map/ppermute | solution.py:390
  39.5 14.2 %collective-permute-start.7 = (bf16[64,4096]{1,0:T(8,128)(2,1)S(1)}, bf16[64,4096]{1,0:T(8,128)(2,1)S(1)}, u32[]{:S(2)}, u32[]{:S(2)}) collective-permute-start(bf16[64,4096]{1,0:T(8,128)(2,1)S(1)} %collective-permute-done.4.refs_4_), channel_id=1, source_target_pairs={{0,4},{2,6},{4,8},{6,10},{8,12},{10,14},{12,0},{14,2},{1,5},{3,7},... | collective-permute-start | bytes 1572872 | tf_op jit(solution)/shard_map/ppermute | solution.py:409
  39.6 12.2 %collective-permute-start.9 = (bf16[16,3584]{1,0:T(8,128)(2,1)S(1)}, bf16[16,3584]{1,0:T(8,128)(2,1)S(1)}, u32[]{:S(2)}, u32[]{:S(2)}) collective-permute-start(bf16[16,3584]{1,0:T(8,128)(2,1)S(1)} %get-tuple-element.123), channel_id=1, source_target_pairs={{0,14},{2,12},{4,2},{6,0},{8,6},{10,4},{12,10},{14,8},{1,15},{3,13... | collective-permute-start | bytes 344072 | tf_op jit(solution)/shard_map/ppermute | solution.py:409
  54.5 11.8 %collective-permute-start.13 = (bf16[5,16,3584]{2,1,0:T(8,128)(2,1)S(1)}, bf16[5,16,3584]{2,1,0:T(8,128)(2,1)S(1)}, u32[]{:S(2)}, u32[]{:S(2)}) collective-permute-start(bf16[5,16,3584]{2,1,0:T(8,128)(2,1)S(1)} %stack.2.refs_5_), channel_id=1, source_target_pairs={{0,16},{16,0},{1,17},{17,1},{2,18},{18,2},{3,19},{19,3},{4,20},{20... | collective-permute-start | bytes 1720328 | tf_op jit(solution)/shard_map/ppermute | solution.py:390
  56.5 9.3 %collective-permute-start.10 = (bf16[64,4096]{1,0:T(8,128)(2,1)S(1)}, bf16[64,4096]{1,0:T(8,128)(2,1)S(1)}, u32[]{:S(2)}, u32[]{:S(2)}) collective-permute-start(bf16[64,4096]{1,0:T(8,128)(2,1)S(1)} %collective-permute-done.7.refs_0_.refs_4_), channel_id=1, source_target_pairs={{0,2},{2,0},{4,6},{6,4},{8,10},{10,8},{12,14},{14,12},{1,3},{3,1},... | collective-permute-start | bytes 1572872 | tf_op jit(solution)/shard_map/ppermute | solution.py:390
  56.6 9.1 %collective-permute-start.11 = (bf16[16,3584]{1,0:T(8,128)(2,1)S(1)}, bf16[16,3584]{1,0:T(8,128)(2,1)S(1)}, u32[]{:S(2)}, u32[]{:S(2)}) collective-permute-start(bf16[16,3584]{1,0:T(8,128)(2,1)S(1)} %get-tuple-element.139), channel_id=1, source_target_pairs={{0,8},{2,10},{4,12},{6,14},{8,0},{10,2},{12,4},{14,6},{1,9},{3,11}... | collective-permute-start | bytes 344072 | tf_op jit(solution)/shard_map/ppermute | solution.py:409
  59.5 6.2 %collective-permute-start.12 = (bf16[16,3584]{1,0:T(8,128)(2,1)S(1)}, bf16[16,3584]{1,0:T(8,128)(2,1)S(1)}, u32[]{:S(2)}, u32[]{:S(2)}) collective-permute-start(bf16[16,3584]{1,0:T(8,128)(2,1)S(1)} %get-tuple-element.140), channel_id=1, source_target_pairs={{0,12},{2,14},{4,0},{6,2},{8,4},{10,6},{12,8},{14,10},{1,13},{3,15... | collective-permute-start | bytes 344072 | tf_op jit(solution)/shard_map/ppermute | solution.py:409
  59.5 15.6 %collective-permute-start.18 = (bf16[5,16,3584]{2,1,0:T(8,128)(2,1)S(1)}, bf16[5,16,3584]{2,1,0:T(8,128)(2,1)S(1)}, u32[]{:S(2)}, u32[]{:S(2)}) collective-permute-start(bf16[5,16,3584]{2,1,0:T(8,128)(2,1)S(1)} %stack.2.refs_5_), channel_id=1, source_target_pairs={{0,1},{1,0},{2,3},{3,2},{4,5},{5,4},{6,7},{7,6},{8,9},{9,8},{10,11... | collective-permute-start | bytes 1720328 | tf_op jit(solution)/shard_map/ppermute | solution.py:390
  66.3 9.9 %collective-permute-start.17 = (bf16[5,16,3584]{2,1,0:T(8,128)(2,1)S(1)}, bf16[5,16,3584]{2,1,0:T(8,128)(2,1)S(1)}, u32[]{:S(2)}, u32[]{:S(2)}) collective-permute-start(bf16[5,16,3584]{2,1,0:T(8,128)(2,1)S(1)} %collective-permute-done.13.refs_7_), channel_id=1, source_target_pairs={{0,1},{1,0},{2,3},{3,2},{4,5},{5,4},{6,7},{7,6},{8,9},{9,8},{10,11... | collective-permute-start | bytes 1720328 | tf_op jit(solution)/shard_map/ppermute | solution.py:390
  66.8 9.4 %collective-permute-start.16 = (bf16[16,3584]{1,0:T(8,128)(2,1)S(1)}, bf16[16,3584]{1,0:T(8,128)(2,1)S(1)}, u32[]{:S(2)}, u32[]{:S(2)}) collective-permute-start(bf16[16,3584]{1,0:T(8,128)(2,1)S(1)} %get-tuple-element.158), channel_id=1, source_target_pairs={{0,10},{2,8},{4,14},{6,12},{8,2},{10,0},{12,6},{14,4},{1,11},{3,9}... | collective-permute-start | bytes 344072 | tf_op jit(solution)/shard_map/ppermute | solution.py:409
  70.5 5.7 %collective-permute-start.15 = (bf16[256,64]{1,0:T(8,128)(2,1)S(1)}, bf16[256,64]{1,0:T(8,128)(2,1)S(1)}, u32[]{:S(2)}, u32[]{:S(2)}) collective-permute-start(bf16[256,64]{1,0:T(8,128)(2,1)S(1)} %low_own.1.one_ref), channel_id=1, source_target_pairs={{0,2},{2,0},{4,6},{6,4},{8,10},{10,8},{12,14},{14,12},{1,3},{3,1},... | collective-permute-start | bytes 98312 | tf_op jit(solution)/shard_map/ppermute | solution.py:390
  76.6 10.1 %collective-permute-start.23 = (bf16[3,16,3584]{2,1,0:T(8,128)(2,1)S(1)}, bf16[3,16,3584]{2,1,0:T(8,128)(2,1)S(1)}, u32[]{:S(2)}, u32[]{:S(2)}) collective-permute-start(bf16[3,16,3584]{2,1,0:T(8,128)(2,1)S(1)} %stack.3.refs_6_), channel_id=1, source_target_pairs={{0,1},{1,0},{2,3},{3,2},{4,5},{5,4},{6,7},{7,6},{8,9},{9,8},{10,11... | collective-permute-start | bytes 1032200 | tf_op jit(solution)/shard_map/ppermute | solution.py:390
  76.7 10.5 %collective-permute-start.22 = (bf16[3,16,3584]{2,1,0:T(8,128)(2,1)S(1)}, bf16[3,16,3584]{2,1,0:T(8,128)(2,1)S(1)}, u32[]{:S(2)}, u32[]{:S(2)}) collective-permute-start(bf16[3,16,3584]{2,1,0:T(8,128)(2,1)S(1)} %stack.3.refs_6_), channel_id=1, source_target_pairs={{0,16},{16,0},{1,17},{17,1},{2,18},{18,2},{3,19},{19,3},{4,20},{20... | collective-permute-start | bytes 1032200 | tf_op jit(solution)/shard_map/ppermute | solution.py:390
  77.6 7.3 %collective-permute-start.21 = (bf16[256,64]{1,0:T(8,128)(2,1)S(1)}, bf16[256,64]{1,0:T(8,128)(2,1)S(1)}, u32[]{:S(2)}, u32[]{:S(2)}) collective-permute-start(bf16[256,64]{1,0:T(8,128)(2,1)S(1)} %add.1.refs_13_), channel_id=1, source_target_pairs={{0,12},{2,14},{4,0},{6,2},{8,4},{10,6},{12,8},{14,10},{1,13},{3,15... | collective-permute-start | bytes 98312 | tf_op jit(solution)/shard_map/ppermute | solution.py:409
  79.8 6.9 %collective-permute-start.20 = (bf16[256,64]{1,0:T(8,128)(2,1)S(1)}, bf16[256,64]{1,0:T(8,128)(2,1)S(1)}, u32[]{:S(2)}, u32[]{:S(2)}) collective-permute-start(bf16[256,64]{1,0:T(8,128)(2,1)S(1)} %add.1.refs_13_), channel_id=1, source_target_pairs={{0,8},{2,10},{4,12},{6,14},{8,0},{10,2},{12,4},{14,6},{1,9},{3,11}... | collective-permute-start | bytes 98312 | tf_op jit(solution)/shard_map/ppermute | solution.py:409
  79.8 6.9 %collective-permute-start.19 = (bf16[256,64]{1,0:T(8,128)(2,1)S(1)}, bf16[256,64]{1,0:T(8,128)(2,1)S(1)}, u32[]{:S(2)}, u32[]{:S(2)}) collective-permute-start(bf16[256,64]{1,0:T(8,128)(2,1)S(1)} %add.1.refs_13_), channel_id=1, source_target_pairs={{0,4},{2,6},{4,8},{6,10},{8,12},{10,14},{12,0},{14,2},{1,5},{3,7},... | collective-permute-start | bytes 98312 | tf_op jit(solution)/shard_map/ppermute | solution.py:409
  87.2 3.0 %collective-permute-start.25 = (bf16[128,3584]{1,0:T(8,128)(2,1)S(1)}, bf16[128,3584]{1,0:T(8,128)(2,1)S(1)}, u32[]{:S(2)}, u32[]{:S(2)}) collective-permute-start(bf16[128,3584]{1,0:T(8,128)(2,1)S(1)} %get-tuple-element.171), channel_id=1, source_target_pairs={{0,1},{1,0},{2,3},{3,2},{4,5},{5,4},{6,7},{7,6},{8,9},{9,8},{10,11... | collective-permute-start | bytes 2752520 | tf_op jit(solution)/shard_map/ppermute | solution.py:390
  (7 other events, 55.0 us)

commit v6 on v5

--- a/solution.py
+++ b/solution.py
@@ -436,8 +436,8 @@
 
     near = tokens
     for stage in range(levels):
+        after = along_mp(near, 1) if stage < levels - 1 else near
         far = along_y(near)
-        after = along_mp(near, 1) if stage < levels - 1 else near
         if stage == 0:
             move_blocks(early)
             bound = [store_row, mark]

time: 93.3 us -> 93.3 us (level)
  no operation moved by 1% of the time
where the time goes in v6:
time: 93.3 us; the launch traced here: 93.2 us
  Pallas kernels  40.3 us (43%)
  starting transfers between devices  29.6 us (32%)
  waiting for transfers between devices  23.1 us (25%)
    pallas_call x5, Pallas kernels, base_chunk(): pl.pallas_call(kernel, grid=(pieces if tiles == 'streamed' else HELD,), i...  26.3 us
    ppermute x13, starting transfers between devices, along_mp(): return lax.ppermute(value, 'mp', pairs_of)  20.2 us
    ppermute x13, waiting for transfers between devices, along_mp(): return lax.ppermute(value, 'mp', pairs_of)  18.3 us
    ppermute x14, starting transfers between devices, move(): return lax.ppermute(value, axis, [(i, i ^ 1) for i in range(size)])  9.4 us
    pallas_call x1, Pallas kernels, hold_gate(): pl.pallas_call(kernel, in_specs=[ANY], out_specs=[VMEM, VMEM], out_shape=...  7.11 us
    ppermute x14, waiting for transfers between devices, move(): return lax.ppermute(value, axis, [(i, i ^ 1) for i in range(size)])  4.73 us
    pallas_call x1, Pallas kernels, finish(): pl.pallas_call(kernel, grid=(width // tile,), in_specs=[VMEM] * pairs + [...  2.99 us
  transfers between devices with their start and end apart: 27, of which 11 were waited for; matrix products, arithmetic and copies ran while one was open for 0% of the time, Pallas kernels for 39%

profile of v6, /device:TPU:0, one launch (start us, length us, event | category | flops | bytes accessed | tf_op | source)
XLA Modules:
  0.0 93.2 jit_solution(4590739895721929275)
XLA Ops:
  0.0 3.0 %collective-permute-start = (bf16[64,4096]{1,0:T(8,128)(2,1)}, bf16[64,4096]{1,0:T(8,128)(2,1)S(1)}, u32[]{:S(2)}, u32[]{:S(2)}) collective-permute-start(bf16[64,4096]{1,0:T(8,128)(2,1)} %refs_2_), channel_id=1, source_target_pairs={{0,4},{2,6},{4,8},{6,10},{8,12},{10,14},{12,0},{14,2},{1,5},{3,7},... | collective-permute-start | bytes 1572872 | tf_op jit(solution)/shard_map/ppermute | solution.py:409
  3.0 1.5 %collective-permute-start.1 = (bf16[64,4096]{1,0:T(8,128)(2,1)}, bf16[64,4096]{1,0:T(8,128)(2,1)S(1)}, u32[]{:S(2)}, u32[]{:S(2)}) collective-permute-start(bf16[64,4096]{1,0:T(8,128)(2,1)} %refs_2_), channel_id=1, source_target_pairs={{0,2},{2,0},{4,6},{6,4},{8,10},{10,8},{12,14},{14,12},{1,3},{3,1},... | collective-permute-start | bytes 1572872 | tf_op jit(solution)/shard_map/ppermute | solution.py:390
  4.5 1.3 %split_panels.1 = (bf16[16,3584]{1,0:T(8,128)(2,1)S(1)}, bf16[16,3584]{1,0:T(8,128)(2,1)S(1)}, bf16[16,3584]{1,0:T(8,128)(2,1)S(1)}, bf16[16,3584]{1,0:T(8,128)(...) custom-call(bf16[1,64,28672]{2,1,0:T(8,128)(2,1)} %up_ref.1), custom_call_target="tpu_custom_call" | custom-call | tf_op jit(solution)/shard_map/split_panels/pallas_call | solution.py:82
  5.9 1.6 %collective-permute-start.2 = (bf16[16,3584]{1,0:T(8,128)(2,1)S(1)}, bf16[16,3584]{1,0:T(8,128)(2,1)S(1)}, u32[]{:S(2)}, u32[]{:S(2)}) collective-permute-start(bf16[16,3584]{1,0:T(8,128)(2,1)S(1)} %get-tuple-element.95), channel_id=1, source_target_pairs={{0,4},{2,6},{4,8},{6,10},{8,12},{10,14},{12,0},{14,2},{1,5},{3,7},... | collective-permute-start | bytes 344072 | tf_op jit(solution)/shard_map/ppermute | solution.py:409
  8.1 7.1 %hold_gate.1 = (bf16[4096,2560]{1,0:T(8,128)(2,1)S(1)}, f32[8,128]{1,0:T(8,128)S(1)}) custom-call(bf16[4096,3584]{1,0:T(8,128)(2,1)} %refs_3_.5), custom_call_target="tpu_custom_call" | custom-call | tf_op jit(solution)/shard_map/hold_gate/pallas_call | solution.py:134
  16.0 3.7 %collective-permute-done.2.refs_1_ = bf16[16,3584]{1,0:T(8,128)(2,1)S(1)} collective-permute-done((bf16[16,3584]{1,0:T(8,128)(2,1)S(1)}, bf16[16,3584]{1,0:T(8,128)(2,1)S(1)}, u32[]{:S(2)}, u32[]{:S(2)}) %collective-permute-start.2) | collective-permute-done | bytes 114720 | tf_op jit(solution)/shard_map/ppermute | solution.py:409
  19.7 1.6 %collective-permute-start.5 = (bf16[64,4096]{1,0:T(8,128)(2,1)S(1)}, bf16[64,4096]{1,0:T(8,128)(2,1)S(1)}, u32[]{:S(2)}, u32[]{:S(2)}) collective-permute-start(bf16[64,4096]{1,0:T(8,128)(2,1)S(1)} %collective-permute-done.refs_2_), channel_id=1, source_target_pairs={{0,2},{2,0},{4,6},{6,4},{8,10},{10,8},{12,14},{14,12},{1,3},{3,1},... | collective-permute-start | bytes 1572872 | tf_op jit(solution)/shard_map/ppermute | solution.py:390
  22.2 1.5 %collective-permute-start.6 = (bf16[16,3584]{1,0:T(8,128)(2,1)S(1)}, bf16[16,3584]{1,0:T(8,128)(2,1)S(1)}, u32[]{:S(2)}, u32[]{:S(2)}) collective-permute-start(bf16[16,3584]{1,0:T(8,128)(2,1)S(1)} %get-tuple-element.112), channel_id=1, source_target_pairs={{0,6},{2,4},{4,10},{6,8},{8,14},{10,12},{12,2},{14,0},{1,7},{3,5},... | collective-permute-start | bytes 344072 | tf_op jit(solution)/shard_map/ppermute | solution.py:409
  23.7 6.1 %base_chunk.5 = (f32[128,3584]{1,0:T(8,128)S(1)}, bf16[128,3584]{1,0:T(8,128)(2,1)S(1)}, f32[128,64]{1,0:T(8,128)S(1)}) custom-call(bf16[4096,2560]{1,0:T(8,128)(2,1)S(1)} %get-tuple-element.93.refs_0_.refs_2_, bf16[4096,3584]{1,0:T(8,128)(2,1)} %refs_3_.5, bf16[64,4096]{1,0:T(8,128)(2,1)S(1)} %copy-done.1, ...), custom_call_target="tpu_custom_call" | custom-call | tf_op jit(solution)/shard_map/base_chunk/pallas_call | solution.py:240
  29.8 8.4 %collective-permute-done.6.refs_3_ = bf16[16,3584]{1,0:T(8,128)(2,1)S(1)} collective-permute-done((bf16[16,3584]{1,0:T(8,128)(2,1)S(1)}, bf16[16,3584]{1,0:T(8,128)(2,1)S(1)}, u32[]{:S(2)}, u32[]{:S(2)}) %collective-permute-start.6) | collective-permute-done | bytes 114720 | tf_op jit(solution)/shard_map/ppermute | solution.py:409
  39.6 4.0 %collective-permute-start.9 = (bf16[16,3584]{1,0:T(8,128)(2,1)S(1)}, bf16[16,3584]{1,0:T(8,128)(2,1)S(1)}, u32[]{:S(2)}, u32[]{:S(2)}) collective-permute-start(bf16[16,3584]{1,0:T(8,128)(2,1)S(1)} %get-tuple-element.123), channel_id=1, source_target_pairs={{0,14},{2,12},{4,2},{6,0},{8,6},{10,4},{12,10},{14,8},{1,15},{3,13... | collective-permute-start | bytes 344072 | tf_op jit(solution)/shard_map/ppermute | solution.py:409
  43.6 6.1 %base_chunk.6 = (f32[128,3584]{1,0:T(8,128)S(1)}, bf16[128,3584]{1,0:T(8,128)(2,1)S(1)}, f32[128,64]{1,0:T(8,128)S(1)}) custom-call(bf16[4096,2560]{1,0:T(8,128)(2,1)S(1)} %get-tuple-element.93.refs_0_.refs_2_, bf16[4096,3584]{1,0:T(8,128)(2,1)} %refs_3_.5, bf16[64,4096]{1,0:T(8,128)(2,1)S(1)} %collective-permute-done.refs_2_, ...), custom_call_target="tpu_custom_call" | custom-call | tf_op jit(solution)/shard_map/base_chunk/pallas_call | solution.py:240
  49.7 2.1 %collective-permute-done.9.refs_4_ = bf16[16,3584]{1,0:T(8,128)(2,1)S(1)} collective-permute-done((bf16[16,3584]{1,0:T(8,128)(2,1)S(1)}, bf16[16,3584]{1,0:T(8,128)(2,1)S(1)}, u32[]{:S(2)}, u32[]{:S(2)}) %collective-permute-start.9) | collective-permute-done | bytes 114720 | tf_op jit(solution)/shard_map/ppermute | solution.py:409
  52.3 1.4 %collective-permute-done.7.refs_0_.refs_4_ = bf16[64,4096]{1,0:T(8,128)(2,1)S(1)} collective-permute-done((bf16[64,4096]{1,0:T(8,128)(2,1)S(1)}, bf16[64,4096]{1,0:T(8,128)(2,1)S(1)}, u32[]{:S(2)}, u32[]{:S(2)}) %collective-permute-start.7) | collective-permute-done | bytes 524320 | tf_op jit(solution)/shard_map/ppermute | solution.py:409
  54.5 2.0 %collective-permute-start.13 = (bf16[5,16,3584]{2,1,0:T(8,128)(2,1)S(1)}, bf16[5,16,3584]{2,1,0:T(8,128)(2,1)S(1)}, u32[]{:S(2)}, u32[]{:S(2)}) collective-permute-start(bf16[5,16,3584]{2,1,0:T(8,128)(2,1)S(1)} %stack.2.refs_5_), channel_id=1, source_target_pairs={{0,16},{16,0},{1,17},{17,1},{2,18},{18,2},{3,19},{19,3},{4,20},{20... | collective-permute-start | bytes 1720328 | tf_op jit(solution)/shard_map/ppermute | solution.py:390
  56.6 3.0 %collective-permute-start.11 = (bf16[16,3584]{1,0:T(8,128)(2,1)S(1)}, bf16[16,3584]{1,0:T(8,128)(2,1)S(1)}, u32[]{:S(2)}, u32[]{:S(2)}) collective-permute-start(bf16[16,3584]{1,0:T(8,128)(2,1)S(1)} %get-tuple-element.139), channel_id=1, source_target_pairs={{0,8},{2,10},{4,12},{6,14},{8,0},{10,2},{12,4},{14,6},{1,9},{3,11}... | collective-permute-start | bytes 344072 | tf_op jit(solution)/shard_map/ppermute | solution.py:409
  59.5 6.1 %base_chunk.7 = (f32[128,3584]{1,0:T(8,128)S(1)}, bf16[128,3584]{1,0:T(8,128)(2,1)S(1)}, f32[128,64]{1,0:T(8,128)S(1)}) custom-call(f32[128,3584]{1,0:T(8,128)S(1)} %get-tuple-element.106.refs_0_, bf16[128,3584]{1,0:T(8,128)(2,1)S(1)} %get-tuple-element.107.refs_1_, ...), custom_call_target="tpu_custom_call", output_to_operand_aliasing={{0}: (0, {}), {1}: (1, {})} | custom-call | tf_op jit(solution)/shard_map/base_chunk/pallas_call | solution.py:240
  66.8 2.3 %collective-permute-start.16 = (bf16[16,3584]{1,0:T(8,128)(2,1)S(1)}, bf16[16,3584]{1,0:T(8,128)(2,1)S(1)}, u32[]{:S(2)}, u32[]{:S(2)}) collective-permute-start(bf16[16,3584]{1,0:T(8,128)(2,1)S(1)} %get-tuple-element.158), channel_id=1, source_target_pairs={{0,10},{2,8},{4,14},{6,12},{8,2},{10,0},{12,6},{14,4},{1,11},{3,9}... | collective-permute-start | bytes 344072 | tf_op jit(solution)/shard_map/ppermute | solution.py:409
  71.3 3.8 %base_chunk.8 = (f32[128,3584]{1,0:T(8,128)S(1)}, bf16[128,3584]{1,0:T(8,128)(2,1)S(1)}) custom-call(f32[128,3584]{1,0:T(8,128)S(1)} %get-tuple-element.152.refs_0_, bf16[128,3584]{1,0:T(8,128)(2,1)S(1)} %get-tuple-element.153.refs_1_, bf16[4096,2560]{1,0:T(8,128)(2,1)S(1)} %get-tuple-element.93.refs_0_.refs_2_, ...), custom_call_target="tpu_custom_call", output_to_operand_aliasing={{0}: (0, {}), {1}: (1, {})} | custom-call | tf_op jit(solution)/shard_map/base_chunk/pallas_call | solution.py:240
  77.6 2.2 %collective-permute-start.21 = (bf16[256,64]{1,0:T(8,128)(2,1)S(1)}, bf16[256,64]{1,0:T(8,128)(2,1)S(1)}, u32[]{:S(2)}, u32[]{:S(2)}) collective-permute-start(bf16[256,64]{1,0:T(8,128)(2,1)S(1)} %add.1.refs_13_), channel_id=1, source_target_pairs={{0,12},{2,14},{4,0},{6,2},{8,4},{10,6},{12,8},{14,10},{1,13},{3,15... | collective-permute-start | bytes 98312 | tf_op jit(solution)/shard_map/ppermute | solution.py:409
  80.8 4.0 %base_chunk.9 = (f32[128,3584]{1,0:T(8,128)S(1)}, bf16[128,3584]{1,0:T(8,128)(2,1)S(1)}) custom-call(f32[128,3584]{1,0:T(8,128)S(1)} %get-tuple-element.162.refs_0_, bf16[128,3584]{1,0:T(8,128)(2,1)S(1)} %get-tuple-element.163.refs_1_, bf16[4096,2560]{1,0:T(8,128)(2,1)S(1)} %get-tuple-element.93.refs_0_.refs_2_, ...), custom_call_target="tpu_custom_call", output_to_operand_aliasing={{0}: (0, {}), {1}: (1, {})} | custom-call | tf_op jit(solution)/shard_map/base_chunk/pallas_call | solution.py:240
  85.0 1.8 %collective-permute-done.20.refs_15_ = bf16[256,64]{1,0:T(8,128)(2,1)S(1)} collective-permute-done((bf16[256,64]{1,0:T(8,128)(2,1)S(1)}, bf16[256,64]{1,0:T(8,128)(2,1)S(1)}, u32[]{:S(2)}, u32[]{:S(2)}) %collective-permute-start.20) | collective-permute-done | bytes 32800 | tf_op jit(solution)/shard_map/ppermute | solution.py:409
  87.7 2.5 %collective-permute-done.26.refs_12_ = bf16[3,16,3584]{2,1,0:T(8,128)(2,1)S(1)} collective-permute-done((bf16[3,16,3584]{2,1,0:T(8,128)(2,1)S(1)}, bf16[3,16,3584]{2,1,0:T(8,128)(2,1)S(1)}, u32[]{:S(2)}, u32[]{:S(2)}) %collective-permute-start.26) | collective-permute-done | bytes 344096 | tf_op jit(solution)/shard_map/ppermute | solution.py:390
  90.2 3.0 %finish.1 = bf16[256,3584]{1,0:T(8,128)(2,1)} custom-call(f32[128,3584]{1,0:T(8,128)S(1)} %get-tuple-element.132.refs_0_, f32[128,3584]{1,0:T(8,128)S(1)} %get-tuple-element.169.refs_1_, bf16[128,3584]{1,0:T(8,128)(2,1)S(1)} %collective-permute-done.24.refs_2_, bf16[128,3584]{1,0:T(8,128)(2,1)S(1)} %collective-permute-done.25.refs_3_, ...), custom_call_target="tpu_custom_call" | custom-call | tf_op jit(solution)/shard_map/finish/pallas_call | solution.py:372
  (52 shorter events, 12.8 us)
Async XLA Ops:
  0.0 19.6 %collective-permute-start = (bf16[64,4096]{1,0:T(8,128)(2,1)}, bf16[64,4096]{1,0:T(8,128)(2,1)S(1)}, u32[]{:S(2)}, u32[]{:S(2)}) collective-permute-start(bf16[64,4096]{1,0:T(8,128)(2,1)} %refs_2_), channel_id=1, source_target_pairs={{0,4},{2,6},{4,8},{6,10},{8,12},{10,14},{12,0},{14,2},{1,5},{3,7},... | collective-permute-start | bytes 1572872 | tf_op jit(solution)/shard_map/ppermute | solution.py:409
  3.0 16.6 %collective-permute-start.1 = (bf16[64,4096]{1,0:T(8,128)(2,1)}, bf16[64,4096]{1,0:T(8,128)(2,1)S(1)}, u32[]{:S(2)}, u32[]{:S(2)}) collective-permute-start(bf16[64,4096]{1,0:T(8,128)(2,1)} %refs_2_), channel_id=1, source_target_pairs={{0,2},{2,0},{4,6},{6,4},{8,10},{10,8},{12,14},{14,12},{1,3},{3,1},... | collective-permute-start | bytes 1572872 | tf_op jit(solution)/shard_map/ppermute | solution.py:390
  5.9 13.8 %collective-permute-start.2 = (bf16[16,3584]{1,0:T(8,128)(2,1)S(1)}, bf16[16,3584]{1,0:T(8,128)(2,1)S(1)}, u32[]{:S(2)}, u32[]{:S(2)}) collective-permute-start(bf16[16,3584]{1,0:T(8,128)(2,1)S(1)} %get-tuple-element.95), channel_id=1, source_target_pairs={{0,4},{2,6},{4,8},{6,10},{8,12},{10,14},{12,0},{14,2},{1,5},{3,7},... | collective-permute-start | bytes 344072 | tf_op jit(solution)/shard_map/ppermute | solution.py:409
  7.5 12.1 %collective-permute-start.3 = (bf16[16,3584]{1,0:T(8,128)(2,1)S(1)}, bf16[16,3584]{1,0:T(8,128)(2,1)S(1)}, u32[]{:S(2)}, u32[]{:S(2)}) collective-permute-start(bf16[16,3584]{1,0:T(8,128)(2,1)S(1)} %get-tuple-element.96), channel_id=1, source_target_pairs={{0,2},{2,0},{4,6},{6,4},{8,10},{10,8},{12,14},{14,12},{1,3},{3,1},... | collective-permute-start | bytes 344072 | tf_op jit(solution)/shard_map/ppermute | solution.py:409
  19.7 18.6 %collective-permute-start.5 = (bf16[64,4096]{1,0:T(8,128)(2,1)S(1)}, bf16[64,4096]{1,0:T(8,128)(2,1)S(1)}, u32[]{:S(2)}, u32[]{:S(2)}) collective-permute-start(bf16[64,4096]{1,0:T(8,128)(2,1)S(1)} %collective-permute-done.refs_2_), channel_id=1, source_target_pairs={{0,2},{2,0},{4,6},{6,4},{8,10},{10,8},{12,14},{14,12},{1,3},{3,1},... | collective-permute-start | bytes 1572872 | tf_op jit(solution)/shard_map/ppermute | solution.py:390
  21.2 17.0 %collective-permute-start.4 = (bf16[64,4096]{1,0:T(8,128)(2,1)S(1)}, bf16[64,4096]{1,0:T(8,128)(2,1)S(1)}, u32[]{:S(2)}, u32[]{:S(2)}) collective-permute-start(bf16[64,4096]{1,0:T(8,128)(2,1)S(1)} %collective-permute-done.refs_2_), channel_id=1, source_target_pairs={{0,4},{2,6},{4,8},{6,10},{8,12},{10,14},{12,0},{14,2},{1,5},{3,7},... | collective-permute-start | bytes 1572872 | tf_op jit(solution)/shard_map/ppermute | solution.py:409
  22.2 16.1 %collective-permute-start.6 = (bf16[16,3584]{1,0:T(8,128)(2,1)S(1)}, bf16[16,3584]{1,0:T(8,128)(2,1)S(1)}, u32[]{:S(2)}, u32[]{:S(2)}) collective-permute-start(bf16[16,3584]{1,0:T(8,128)(2,1)S(1)} %get-tuple-element.112), channel_id=1, source_target_pairs={{0,6},{2,4},{4,10},{6,8},{8,14},{10,12},{12,2},{14,0},{1,7},{3,5},... | collective-permute-start | bytes 344072 | tf_op jit(solution)/shard_map/ppermute | solution.py:409
  38.3 14.1 %collective-permute-start.8 = (bf16[64,4096]{1,0:T(8,128)(2,1)S(1)}, bf16[64,4096]{1,0:T(8,128)(2,1)S(1)}, u32[]{:S(2)}, u32[]{:S(2)}) collective-permute-start(bf16[64,4096]{1,0:T(8,128)(2,1)S(1)} %collective-permute-done.4.refs_4_), channel_id=1, source_target_pairs={{0,2},{2,0},{4,6},{6,4},{8,10},{10,8},{12,14},{14,12},{1,3},{3,1},... | collective-permute-start | bytes 1572872 | tf_op jit(solution)/shard_map/ppermute | solution.py:390
  39.5 14.2 %collective-permute-start.7 = (bf16[64,4096]{1,0:T(8,128)(2,1)S(1)}, bf16[64,4096]{1,0:T(8,128)(2,1)S(1)}, u32[]{:S(2)}, u32[]{:S(2)}) collective-permute-start(bf16[64,4096]{1,0:T(8,128)(2,1)S(1)} %collective-permute-done.4.refs_4_), channel_id=1, source_target_pairs={{0,4},{2,6},{4,8},{6,10},{8,12},{10,14},{12,0},{14,2},{1,5},{3,7},... | collective-permute-start | bytes 1572872 | tf_op jit(solution)/shard_map/ppermute | solution.py:409
  39.6 12.2 %collective-permute-start.9 = (bf16[16,3584]{1,0:T(8,128)(2,1)S(1)}, bf16[16,3584]{1,0:T(8,128)(2,1)S(1)}, u32[]{:S(2)}, u32[]{:S(2)}) collective-permute-start(bf16[16,3584]{1,0:T(8,128)(2,1)S(1)} %get-tuple-element.123), channel_id=1, source_target_pairs={{0,14},{2,12},{4,2},{6,0},{8,6},{10,4},{12,10},{14,8},{1,15},{3,13... | collective-permute-start | bytes 344072 | tf_op jit(solution)/shard_map/ppermute | solution.py:409
  54.5 11.8 %collective-permute-start.13 = (bf16[5,16,3584]{2,1,0:T(8,128)(2,1)S(1)}, bf16[5,16,3584]{2,1,0:T(8,128)(2,1)S(1)}, u32[]{:S(2)}, u32[]{:S(2)}) collective-permute-start(bf16[5,16,3584]{2,1,0:T(8,128)(2,1)S(1)} %stack.2.refs_5_), channel_id=1, source_target_pairs={{0,16},{16,0},{1,17},{17,1},{2,18},{18,2},{3,19},{19,3},{4,20},{20... | collective-permute-start | bytes 1720328 | tf_op jit(solution)/shard_map/ppermute | solution.py:390
  56.5 9.3 %collective-permute-start.10 = (bf16[64,4096]{1,0:T(8,128)(2,1)S(1)}, bf16[64,4096]{1,0:T(8,128)(2,1)S(1)}, u32[]{:S(2)}, u32[]{:S(2)}) collective-permute-start(bf16[64,4096]{1,0:T(8,128)(2,1)S(1)} %collective-permute-done.7.refs_0_.refs_4_), channel_id=1, source_target_pairs={{0,2},{2,0},{4,6},{6,4},{8,10},{10,8},{12,14},{14,12},{1,3},{3,1},... | collective-permute-start | bytes 1572872 | tf_op jit(solution)/shard_map/ppermute | solution.py:390
  56.6 9.1 %collective-permute-start.11 = (bf16[16,3584]{1,0:T(8,128)(2,1)S(1)}, bf16[16,3584]{1,0:T(8,128)(2,1)S(1)}, u32[]{:S(2)}, u32[]{:S(2)}) collective-permute-start(bf16[16,3584]{1,0:T(8,128)(2,1)S(1)} %get-tuple-element.139), channel_id=1, source_target_pairs={{0,8},{2,10},{4,12},{6,14},{8,0},{10,2},{12,4},{14,6},{1,9},{3,11}... | collective-permute-start | bytes 344072 | tf_op jit(solution)/shard_map/ppermute | solution.py:409
  59.5 6.2 %collective-permute-start.12 = (bf16[16,3584]{1,0:T(8,128)(2,1)S(1)}, bf16[16,3584]{1,0:T(8,128)(2,1)S(1)}, u32[]{:S(2)}, u32[]{:S(2)}) collective-permute-start(bf16[16,3584]{1,0:T(8,128)(2,1)S(1)} %get-tuple-element.140), channel_id=1, source_target_pairs={{0,12},{2,14},{4,0},{6,2},{8,4},{10,6},{12,8},{14,10},{1,13},{3,15... | collective-permute-start | bytes 344072 | tf_op jit(solution)/shard_map/ppermute | solution.py:409
  59.5 15.6 %collective-permute-start.18 = (bf16[5,16,3584]{2,1,0:T(8,128)(2,1)S(1)}, bf16[5,16,3584]{2,1,0:T(8,128)(2,1)S(1)}, u32[]{:S(2)}, u32[]{:S(2)}) collective-permute-start(bf16[5,16,3584]{2,1,0:T(8,128)(2,1)S(1)} %stack.2.refs_5_), channel_id=1, source_target_pairs={{0,1},{1,0},{2,3},{3,2},{4,5},{5,4},{6,7},{7,6},{8,9},{9,8},{10,11... | collective-permute-start | bytes 1720328 | tf_op jit(solution)/shard_map/ppermute | solution.py:390
  66.3 9.9 %collective-permute-start.17 = (bf16[5,16,3584]{2,1,0:T(8,128)(2,1)S(1)}, bf16[5,16,3584]{2,1,0:T(8,128)(2,1)S(1)}, u32[]{:S(2)}, u32[]{:S(2)}) collective-permute-start(bf16[5,16,3584]{2,1,0:T(8,128)(2,1)S(1)} %collective-permute-done.13.refs_7_), channel_id=1, source_target_pairs={{0,1},{1,0},{2,3},{3,2},{4,5},{5,4},{6,7},{7,6},{8,9},{9,8},{10,11... | collective-permute-start | bytes 1720328 | tf_op jit(solution)/shard_map/ppermute | solution.py:390
  66.8 9.4 %collective-permute-start.16 = (bf16[16,3584]{1,0:T(8,128)(2,1)S(1)}, bf16[16,3584]{1,0:T(8,128)(2,1)S(1)}, u32[]{:S(2)}, u32[]{:S(2)}) collective-permute-start(bf16[16,3584]{1,0:T(8,128)(2,1)S(1)} %get-tuple-element.158), channel_id=1, source_target_pairs={{0,10},{2,8},{4,14},{6,12},{8,2},{10,0},{12,6},{14,4},{1,11},{3,9}... | collective-permute-start | bytes 344072 | tf_op jit(solution)/shard_map/ppermute | solution.py:409
  70.5 5.7 %collective-permute-start.15 = (bf16[256,64]{1,0:T(8,128)(2,1)S(1)}, bf16[256,64]{1,0:T(8,128)(2,1)S(1)}, u32[]{:S(2)}, u32[]{:S(2)}) collective-permute-start(bf16[256,64]{1,0:T(8,128)(2,1)S(1)} %low_own.1.one_ref), channel_id=1, source_target_pairs={{0,2},{2,0},{4,6},{6,4},{8,10},{10,8},{12,14},{14,12},{1,3},{3,1},... | collective-permute-start | bytes 98312 | tf_op jit(solution)/shard_map/ppermute | solution.py:390
  76.6 10.1 %collective-permute-start.23 = (bf16[3,16,3584]{2,1,0:T(8,128)(2,1)S(1)}, bf16[3,16,3584]{2,1,0:T(8,128)(2,1)S(1)}, u32[]{:S(2)}, u32[]{:S(2)}) collective-permute-start(bf16[3,16,3584]{2,1,0:T(8,128)(2,1)S(1)} %stack.3.refs_6_), channel_id=1, source_target_pairs={{0,1},{1,0},{2,3},{3,2},{4,5},{5,4},{6,7},{7,6},{8,9},{9,8},{10,11... | collective-permute-start | bytes 1032200 | tf_op jit(solution)/shard_map/ppermute | solution.py:390
  76.7 10.5 %collective-permute-start.22 = (bf16[3,16,3584]{2,1,0:T(8,128)(2,1)S(1)}, bf16[3,16,3584]{2,1,0:T(8,128)(2,1)S(1)}, u32[]{:S(2)}, u32[]{:S(2)}) collective-permute-start(bf16[3,16,3584]{2,1,0:T(8,128)(2,1)S(1)} %stack.3.refs_6_), channel_id=1, source_target_pairs={{0,16},{16,0},{1,17},{17,1},{2,18},{18,2},{3,19},{19,3},{4,20},{20... | collective-permute-start | bytes 1032200 | tf_op jit(solution)/shard_map/ppermute | solution.py:390
  77.6 7.3 %collective-permute-start.21 = (bf16[256,64]{1,0:T(8,128)(2,1)S(1)}, bf16[256,64]{1,0:T(8,128)(2,1)S(1)}, u32[]{:S(2)}, u32[]{:S(2)}) collective-permute-start(bf16[256,64]{1,0:T(8,128)(2,1)S(1)} %add.1.refs_13_), channel_id=1, source_target_pairs={{0,12},{2,14},{4,0},{6,2},{8,4},{10,6},{12,8},{14,10},{1,13},{3,15... | collective-permute-start | bytes 98312 | tf_op jit(solution)/shard_map/ppermute | solution.py:409
  79.8 6.9 %collective-permute-start.20 = (bf16[256,64]{1,0:T(8,128)(2,1)S(1)}, bf16[256,64]{1,0:T(8,128)(2,1)S(1)}, u32[]{:S(2)}, u32[]{:S(2)}) collective-permute-start(bf16[256,64]{1,0:T(8,128)(2,1)S(1)} %add.1.refs_13_), channel_id=1, source_target_pairs={{0,8},{2,10},{4,12},{6,14},{8,0},{10,2},{12,4},{14,6},{1,9},{3,11}... | collective-permute-start | bytes 98312 | tf_op jit(solution)/shard_map/ppermute | solution.py:409
  79.8 6.9 %collective-permute-start.19 = (bf16[256,64]{1,0:T(8,128)(2,1)S(1)}, bf16[256,64]{1,0:T(8,128)(2,1)S(1)}, u32[]{:S(2)}, u32[]{:S(2)}) collective-permute-start(bf16[256,64]{1,0:T(8,128)(2,1)S(1)} %add.1.refs_13_), channel_id=1, source_target_pairs={{0,4},{2,6},{4,8},{6,10},{8,12},{10,14},{12,0},{14,2},{1,5},{3,7},... | collective-permute-start | bytes 98312 | tf_op jit(solution)/shard_map/ppermute | solution.py:409
  87.2 3.0 %collective-permute-start.25 = (bf16[128,3584]{1,0:T(8,128)(2,1)S(1)}, bf16[128,3584]{1,0:T(8,128)(2,1)S(1)}, u32[]{:S(2)}, u32[]{:S(2)}) collective-permute-start(bf16[128,3584]{1,0:T(8,128)(2,1)S(1)} %get-tuple-element.171), channel_id=1, source_target_pairs={{0,1},{1,0},{2,3},{3,2},{4,5},{5,4},{6,7},{7,6},{8,9},{9,8},{10,11... | collective-permute-start | bytes 2752520 | tf_op jit(solution)/shard_map/ppermute | solution.py:390
  (7 other events, 55.0 us)
